TPU v7x, 128 devices: a whole 4x4x4 slice. The times are simulated.
128 devices in a mesh: dp: 16 (over y, z_hi, core), fsdp: 8 (over z_lo, x).
Axes of the slice: x: 4, y: 4, z: 4 (z_hi: 2, z_lo: 2; z = z_hi * 2 + z_lo), core: 2. Of those that a mesh axis runs over, the one named last changes fastest.
Arguments:
- tokens: bfloat16 [65536, 8192], P(('dp', 'fsdp')), may hold values from -24 to 24
- cotangent: bfloat16 [65536, 1024], P(('dp', 'fsdp')), may hold values from -0.0625 to 0.0625
- weight: bfloat16 [8192, 1024], P('fsdp'), may hold values from -0.0625 to 0.0625
- basis: bfloat16 [1024, 512], replicated, may hold values from -0.1875 to 0.1875
- exp_avg: float32 [8192, 512], P(('fsdp', 'dp')), may hold values from -4 to 4
- exp_avg_sq: float32 [8192, 512], P(('fsdp', 'dp')), may hold values from 0.01 to 1
Outputs:
- keys: bfloat16 [65536, 1024], P(('dp', 'fsdp'))
- new_weight: bfloat16 [8192, 1024], P('fsdp')
- new_avg: float32 [8192, 512], P(('fsdp', 'dp'))
- new_sq: float32 [8192, 512], P(('fsdp', 'dp'))
All inputs are finite; a program needn't handle non-finite values.
Results may differ from a plain program's by a relative error of at most 0.0065.
Values may be sent and summed in bfloat16 or wider, within the bound.
No kernel may reach another device: no remote copies, remote signals or barrier semaphores. Data moves between devices by JAX's collectives and lax.ppermute only.
A program may use at most 128 MiB of HBM per device.

v0:
```python
import jax
import jax.numpy as jnp
from jax import lax
from jax.sharding import PartitionSpec as P

STEP = 100


learn_rate = 0.01
galore_scale = 0.25


def local(tokens, cotangent, weight, basis, exp_avg, exp_avg_sq):
    width = tokens.shape[1]
    rank_cols = basis.shape[1]
    fsdp_size = lax.axis_size("fsdp")
    dp_size = lax.axis_size("dp")
    block = width // (fsdp_size * dp_size)
    columns = tokens
    keys = jnp.dot(
        columns,
        lax.all_gather(weight, "fsdp", axis=0, tiled=True),
        preferred_element_type=jnp.float32,
    ).astype(jnp.bfloat16)
    low = jnp.dot(cotangent, basis, preferred_element_type=jnp.float32).astype(jnp.bfloat16)
    columns = tokens
    whole = lax.dot_general(
        columns, low, (((0,), (0,)), ((), ())), preferred_element_type=jnp.float32
    )
    ordered = (
        whole.reshape(fsdp_size, dp_size, block, rank_cols)
        .transpose(1, 0, 2, 3)
        .reshape(width, rank_cols)
    )
    projected = lax.psum_scatter(ordered, ("dp", "fsdp"), scatter_dimension=0, tiled=True)
    new_avg = 0.9 * exp_avg + 0.1 * projected
    new_sq = 0.999 * exp_avg_sq + 0.001 * projected * projected
    first_fix = 1.0 - 0.9**STEP
    second_fix = 1.0 - 0.999**STEP
    direction = new_avg / first_fix / (jnp.sqrt(new_sq / second_fix) + 1e-08)
    update = lax.dot_general(
        direction,
        basis.astype(jnp.float32),
        (((1,), (1,)), ((), ())),
        precision=lax.Precision.HIGHEST,
    )
    own_rows = lax.dynamic_slice_in_dim(weight, lax.axis_index("dp") * block, block, 0)
    fresh = (own_rows.astype(jnp.float32) - learn_rate * galore_scale * update).astype(jnp.bfloat16)
    new_weight = lax.all_gather(fresh, "dp", axis=0, tiled=True)
    return (keys, new_weight, new_avg, new_sq)


def solution(mesh):
    in_specs = (
        P(("dp", "fsdp"), None),
        P(("dp", "fsdp"), None),
        P("fsdp", None),
        P(),
        P(("fsdp", "dp"), None),
        P(("fsdp", "dp"), None),
    )
    out_specs = (
        P(("dp", "fsdp"), None),
        P("fsdp", None),
        P(("fsdp", "dp"), None),
        P(("fsdp", "dp"), None),
    )
    return jax.shard_map(local, mesh=mesh, in_specs=in_specs, out_specs=out_specs, check_vma=False)
```

profile of v0, /device:TPU:1, one launch (start us, length us, event | category | flops | bytes accessed | tf_op | source)
XLA Modules:
  0.0 915.6 jit_solution(5072764953694697547)
XLA Ops:
  8.0 0.0 copy-start
  8.0 0.0 reduce-scatter.2.cloned.1.call-start
  8.1 1.2 copy-done
  9.2 11.8 %convolution_bitcast_fusion = f32[8192,512]{0,1:T(8,128)} fusion(bf16[512,8192]{1,0:T(8,128)(2,1)} %param.6, bf16[512,1024]{1,0:T(8,128)(2,1)} %param.7, bf16[1024,512]{1,0:T(8,128)(2,1)S(1)} %copy-done), kind=kOutput, calls=%fused_computation | convolution fusion | flops 4832100352 | bytes 27262976 | tf_op jit(solution)/shard_map/dot_general | solution.py:27
  21.1 17.4 %copy.12 = f32[8192,512]{1,0:T(8,128)} copy(f32[8192,512]{0,1:T(8,128)} %convolution_bitcast_fusion) | data formatting | bytes 33554432 | tf_op jit(solution)/shard_map/dot_general | solution.py:27
  38.5 12.0 %copy.13 = f32[16,8,64,512]{3,2,1,0:T(8,128)} copy(f32[16,8,64,512]{3,2,0,1:T(8,128)} %bitcast.13) | data formatting | bytes 33554432 | tf_op jit(solution)/shard_map/transpose | solution.py:32
  50.5 0.0 copy-start.3
  50.5 0.0 copy-start.4
  50.5 0.0 reduce-scatter.2.cloned.1.call-update
  50.6 0.0 all-gather.3.cloned.1.call-start
  50.6 0.5 all-gather.3.cloned.1.call-update
  51.1 0.0 all-gather.5.cloned.1.call-start
  51.2 788.3 %reduce-scatter.2.cloned.1.call-done = f32[64,512]{1,0:T(8,128)} async-done(((f32[8192,512]{1,0:T(8,128)}), f32[64,512]{1,0:T(8,128)}) %reduce-scatter.2.cloned.1.call-update) | async-done | bytes 131088 | tf_op jit(solution)/shard_map/reduce_scatter | solution.py:35
  839.5 0.0 copy-done.3
  839.5 0.0 copy-done.4
  839.5 0.9 multiply_add_fusion
  840.5 0.0 copy-start.1
  840.5 0.0 copy-start.2
  840.5 2.7 fusion.1
  843.2 0.0 all-gather.5.cloned.1.call-update
  843.2 0.0 all-gather.3.cloned.1.call-done
  843.2 15.6 %convolution_convert_fusion = bf16[512,1024]{1,0:T(8,128)(2,1)} fusion(bf16[512,8192]{1,0:T(8,128)(2,1)} %param.6, bf16[8192,1024]{1,0:T(8,128)(2,1)} %all-gather.3.cloned.1.call-done), kind=kOutput, calls=%fused_computation.1 | convolution fusion | flops 8590458880 | bytes 26214400 | tf_op jit(solution)/shard_map/dot_general | solution.py:20
  858.8 0.0 copy-done.1
  858.8 0.0 copy-done.2
  858.8 46.3 %all-gather.5.cloned.1.call-done = bf16[1024,1024]{1,0:T(8,128)(2,1)} async-done(((bf16[64,1024]{1,0:T(8,128)(2,1)}), bf16[1024,1024]{1,0:T(8,128)(2,1)}) %all-gather.5.cloned.1.call-update) | async-done | bytes 2097168 | tf_op jit(solution)/shard_map/all_gather | solution.py:49
  905.1 3.1 copy.15
Async XLA Ops:
  8.0 1.2 copy-start
  8.0 831.5 %reduce-scatter.2.cloned.1.call-start = ((), (), s32[]{:S(2)}) async-start(), calls=%async_computation.2 | async-start | bytes 16908288 | tf_op jit(solution)/shard_map/reduce_scatter | solution.py:35
  50.5 789.0 %copy-start.3 = (f32[64,512]{1,0:T(8,128)S(1)}, f32[64,512]{1,0:T(8,128)}, u32[]{:S(2)}) copy-start(f32[64,512]{1,0:T(8,128)} %param.10) | copy-start | bytes 393220
  50.5 789.0 %copy-start.4 = (f32[64,512]{1,0:T(8,128)S(1)}, f32[64,512]{1,0:T(8,128)}, u32[]{:S(2)}) copy-start(f32[64,512]{1,0:T(8,128)} %param.11) | copy-start | bytes 393220
  50.6 792.7 %all-gather.3.cloned.1.call-start = ((), (), s32[]{:S(2)}) async-start(), calls=%async_computation.1 | async-start | bytes 18874368 | tf_op jit(solution)/shard_map/all_gather | solution.py:22
  51.1 854.0 %all-gather.5.cloned.1.call-start = ((), (), s32[]{:S(2)}) async-start(), calls=%async_computation.3 | async-start | bytes 2228224 | tf_op jit(solution)/shard_map/all_gather | solution.py:49
  840.5 18.4 %copy-start.1 = (f32[64,512]{1,0:T(8,128)}, f32[64,512]{1,0:T(8,128)S(1)}, u32[]{:S(2)}) copy-start(f32[64,512]{1,0:T(8,128)S(1)} %get-tuple-element.12) | copy-start | bytes 393220
  840.5 18.3 %copy-start.2 = (f32[64,512]{1,0:T(8,128)}, f32[64,512]{1,0:T(8,128)S(1)}, u32[]{:S(2)}) copy-start(f32[64,512]{1,0:T(8,128)S(1)} %get-tuple-element.13) | copy-start | bytes 393220
Sparse Core Ops, SparseCore 0:
  50.7 788.7 reduce-scatter.1
Sparse Core Ops, SparseCore 1:
  52.7 182.0 all-gather.2
  843.3 61.8 all-gather.4
where the time goes:
time: 916 us
  waiting for transfers between devices  835 us (91%)
  local copies, waits for them, and re-layouts  33.8 us (4%)
  matrix products  30.1 us (3%)
  between operations  15.5 us (2%)
    reduce_scatter x1, waiting for transfers between devices, local(): lax.psum_scatter(ordered, ('dp', 'fsdp'), scatter_dimension=0, tiled=True)  788 us
    all_gather x1, waiting for transfers between devices, local(): new_weight = lax.all_gather(fresh, 'dp', axis=0, tiled=True)  46.3 us
  transfers between devices with their start and end apart: 3, of which 2 were waited for; matrix products, arithmetic and copies ran while one was open for 2% of the time, Pallas kernels for 0%

commit v1 on v0

v1 whole, which is shorter than its diff:
```python
import jax
import jax.numpy as jnp
from jax import lax
from jax.experimental import pallas as pl
from jax.experimental.pallas import tpu as pltpu
from jax.sharding import PartitionSpec as P

STEP = 100
AXES = ("dp", "fsdp")

learn_rate = 0.01
galore_scale = 0.25

ROWS = 64
VMEM = 48 * 1024 * 1024


def pack_columns(parity, tokens):
    count, width = tokens.shape
    blocks = 8
    wide = width // blocks

    def body(parity_ref, x_ref, o_ref):
        row = lax.broadcasted_iota(jnp.int32, (256, 128), 0)
        col = lax.broadcasted_iota(jnp.int32, (256, 128), 1)
        chosen = col + jnp.where(col >= 64, 64, 0) + parity_ref[0] * 64
        select = jnp.where(row == chosen, 1.0, 0.0).astype(jnp.bfloat16)
        for j in range(wide // 256):
            o_ref[0, :, j * 128 : (j + 1) * 128] = jnp.dot(
                x_ref[:, j * 256 : (j + 1) * 256], select, preferred_element_type=jnp.float32
            ).astype(jnp.bfloat16)

    return pl.pallas_call(
        body,
        grid_spec=pltpu.PrefetchScalarGridSpec(
            num_scalar_prefetch=1,
            grid=(blocks,),
            in_specs=[pl.BlockSpec((count, wide), lambda f, p: (0, f))],
            out_specs=pl.BlockSpec((1, count, wide // 2), lambda f, p: (f, 0, 0)),
        ),
        out_shape=jax.ShapeDtypeStruct((blocks, count, wide // 2), jnp.bfloat16),
        compiler_params=pltpu.CompilerParams(vmem_limit_bytes=VMEM),
        cost_estimate=pl.CostEstimate(flops=2 * count * width * 128, bytes_accessed=3 * count * width, transcendentals=0),
        name="pack_columns",
    )(parity, tokens)


def partial_gradient(own, other, low, low_other):
    blocks, count, wide = own.shape
    rank = low.shape[1]
    parts = wide // ROWS
    contract = (((0,), (0,)), ((), ()))

    def body(a_ref, b_ref, la_ref, lb_ref, o_ref):
        total = lax.dot_general(a_ref[0], la_ref[...], contract, preferred_element_type=jnp.float32)
        total = total + lax.dot_general(b_ref[0], lb_ref[...], contract, preferred_element_type=jnp.float32)
        o_ref[...] = total.reshape(parts, 1, ROWS, rank).astype(jnp.bfloat16)

    piece = pl.BlockSpec((1, count, wide), lambda f: (f, 0, 0))
    whole = pl.BlockSpec((count, rank), lambda f: (0, 0))
    return pl.pallas_call(
        body,
        grid=(blocks,),
        in_specs=[piece, piece, whole, whole],
        out_specs=pl.BlockSpec((parts, 1, ROWS, rank), lambda f: (0, f, 0, 0)),
        out_shape=jax.ShapeDtypeStruct((parts, blocks, ROWS, rank), jnp.bfloat16),
        compiler_params=pltpu.CompilerParams(vmem_limit_bytes=VMEM),
        cost_estimate=pl.CostEstimate(
            flops=4 * blocks * count * wide * rank, bytes_accessed=6 * blocks * count * wide, transcendentals=0
        ),
        name="partial_gradient",
    )(own, other, low, low_other)


def keys_partial(packed, weight, addend=None):
    blocks, count, wide = packed.shape
    features = weight.shape[1]

    def body(x_ref, w_ref, *refs):
        f = pl.program_id(0)
        acc_ref = refs[-1]
        product = jnp.dot(x_ref[0], w_ref[...], preferred_element_type=jnp.float32)

        @pl.when(f == 0)
        def _():
            acc_ref[...] = product if addend is None else product + refs[0][...]

        @pl.when(f > 0)
        def _():
            acc_ref[...] += product

        if addend is not None:

            @pl.when(f == blocks - 1)
            def _():
                refs[1][...] = acc_ref[...].astype(jnp.bfloat16)

    whole = pl.BlockSpec((count, features), lambda f: (0, 0))
    specs = [
        pl.BlockSpec((1, count, wide), lambda f: (f, 0, 0)),
        pl.BlockSpec((wide, features), lambda f: (f, 0)),
    ]
    kind = jnp.float32 if addend is None else jnp.bfloat16
    return pl.pallas_call(
        body,
        grid=(blocks,),
        in_specs=specs + ([] if addend is None else [whole]),
        out_specs=whole,
        out_shape=jax.ShapeDtypeStruct((count, features), kind),
        scratch_shapes=[] if addend is None else [pltpu.VMEM((count, features), jnp.float32)],
        compiler_params=pltpu.CompilerParams(vmem_limit_bytes=VMEM),
        cost_estimate=pl.CostEstimate(
            flops=2 * blocks * count * wide * features,
            bytes_accessed=2 * blocks * wide * (count + features),
            transcendentals=0,
        ),
        name="keys_partial",
    )(*([packed, weight] + ([] if addend is None else [addend])))


def local(tokens, cotangent, weight, basis, exp_avg, exp_avg_sq):
    fsdp_size = lax.axis_size("fsdp")
    dp_size = lax.axis_size("dp")
    core = lax.axis_index("dp") % 2
    chips = dp_size // 2
    features = weight.shape[1]
    swap = [
        (d * fsdp_size + f, (d + 1 - 2 * (d % 2)) * fsdp_size + f) for d in range(dp_size) for f in range(fsdp_size)
    ]
    same_core = [
        [(2 * q + c) * fsdp_size + f for q in range(chips) for f in range(fsdp_size)] for c in range(2)
    ]
    shard_chips = [[(2 * q + c) * fsdp_size + f for q in range(chips)] for c in range(2) for f in range(fsdp_size)]

    send = pack_columns((1 - core).reshape(1), tokens)
    other = lax.ppermute(send, AXES, swap)
    low = jnp.dot(cotangent, basis, preferred_element_type=jnp.float32).astype(jnp.bfloat16)
    low_other = lax.ppermute(low, AXES, swap)
    own = pack_columns(core.reshape(1), tokens)

    rows = weight.reshape(chips, 2, ROWS, features)
    half = lax.dynamic_index_in_dim(rows, core, 1, keepdims=False)
    gathered = lax.all_gather(half.reshape(chips * ROWS, features), "fsdp", axis=0, tiled=True)

    partial = partial_gradient(own, other, low, low_other)
    spread = lax.all_to_all(
        partial.reshape(chips * fsdp_size, ROWS, partial.shape[-1]),
        AXES,
        split_axis=0,
        concat_axis=0,
        axis_index_groups=same_core,
        tiled=True,
    )
    projected = jnp.sum(spread.astype(jnp.float32), axis=0)
    new_avg = 0.9 * exp_avg + 0.1 * projected
    new_sq = 0.999 * exp_avg_sq + 0.001 * projected * projected
    first_fix = 1.0 - 0.9**STEP
    second_fix = 1.0 - 0.999**STEP
    direction = new_avg / first_fix / (jnp.sqrt(new_sq / second_fix) + 1e-08)
    update = lax.dot_general(
        direction,
        basis.astype(jnp.float32),
        (((1,), (1,)), ((), ())),
        precision=lax.Precision.HIGHEST,
    )
    place = lax.axis_index("dp") * ROWS
    own_rows = lax.dynamic_slice_in_dim(weight, place, ROWS, 0)
    fresh = (own_rows.astype(jnp.float32) - learn_rate * galore_scale * update).astype(jnp.bfloat16)
    mine = lax.all_to_all(
        jnp.broadcast_to(fresh[None], (chips, ROWS, features)),
        AXES,
        split_axis=0,
        concat_axis=0,
        axis_index_groups=shard_chips,
        tiled=True,
    )
    theirs = lax.ppermute(mine, AXES, swap)
    first = jnp.where(core == 0, mine, theirs)
    second = jnp.where(core == 0, theirs, mine)
    new_weight = jnp.stack([first, second], axis=1).reshape(weight.shape)

    for_other = keys_partial(other, gathered)
    from_other = lax.ppermute(for_other, AXES, swap)
    keys = keys_partial(own, gathered, from_other)
    return (keys, new_weight, new_avg, new_sq)


def solution(mesh):
    in_specs = (
        P(("dp", "fsdp"), None),
        P(("dp", "fsdp"), None),
        P("fsdp", None),
        P(),
        P(("fsdp", "dp"), None),
        P(("fsdp", "dp"), None),
    )
    out_specs = (
        P(("dp", "fsdp"), None),
        P("fsdp", None),
        P(("fsdp", "dp"), None),
        P(("fsdp", "dp"), None),
    )
    return jax.shard_map(local, mesh=mesh, in_specs=in_specs, out_specs=out_specs, check_vma=False)
```

time: 916 us -> 204 us (0.22)
  waiting for transfers between devices: 835 us -> 103 us
  Pallas kernels: 0 us -> 47 us
  matrix products: 30.1 us -> 2.76 us
  local copies, waits for them, and re-layouts: 33.8 us -> 9.36 us
  starting transfers between devices: 0.12 us -> 20.3 us
    reduce_scatter x1 -> x0, waiting for transfers between devices: 788 us -> none  [local(): lax.psum_scatter(ordered, ('dp', 'fsdp'), scatter_dimension=0, tiled=True)]
    all_to_all x0 -> x2, waiting for transfers between devices: none -> 101 us  [the longest x1 98.6 us: local(): lax.all_to_all(partial.reshape(chips * fsdp_size, ROWS, partial.shape[-1]...]
    pallas_call x0 -> x5, Pallas kernels: none -> 47 us  [the longest x2 23.1 us: keys_partial(): pl.pallas_call(body, grid=(blocks,), in_specs=specs + ([] if addend is No...]
    all_gather x2 -> x1, waiting for transfers between devices: 46.3 us -> 0.02 us  [local(): lax.all_gather(half.reshape(chips * ROWS, features), 'fsdp', axis=0, tile...]
    dot_general x2 -> x1, matrix products: 27.4 us -> 0.71 us  [local(): jnp.dot(cotangent, basis, preferred_element_type=jnp.float32)]
    dot_general x1 -> x0, local copies, waits for them, and re-layouts: 17.4 us -> none  [local(): lax.dot_general(columns, low, (((0,), (0,)), ((), ())), preferred_element...]
    all_to_all x0 -> x2, starting transfers between devices: none -> 15.7 us  [the longest x1 11.5 us: local(): lax.all_to_all(partial.reshape(chips * fsdp_size, ROWS, partial.shape[-1]...]
    transpose x1 -> x0, local copies, waits for them, and re-layouts: 12 us -> none  [local(): ordered = whole.reshape(fsdp_size, dp_size, block, rank_cols).transpose(1...]
  transfers between devices with their start and end apart: 3 -> 7, of which waited for: 2 -> 3; matrix products, arithmetic and copies ran while one was open for 2% -> 5% of each run, Pallas kernels for 0% -> 17%
where the time goes in v1:
time: 204 us; the launch traced here: 203 us
  waiting for transfers between devices  103 us (50%)
  Pallas kernels  47 us (23%)
  starting transfers between devices  20.3 us (10%)
  between operations  14.2 us (7%)
  local copies, waits for them, and re-layouts  9.36 us (5%)
  other arithmetic  6.06 us (3%)
  matrix products  2.76 us (1%)
    all_to_all x1, waiting for transfers between devices, local(): lax.all_to_all(partial.reshape(chips * fsdp_size, ROWS, partial.shape[-1]...  98.6 us
    pallas_call x2, Pallas kernels, keys_partial(): pl.pallas_call(body, grid=(blocks,), in_specs=specs + ([] if addend is No...  23.1 us
    pallas_call x2, Pallas kernels, pack_columns(): pl.pallas_call(body, grid_spec=pltpu.PrefetchScalarGridSpec(num_scalar_pr...  14.9 us
    all_to_all x1, starting transfers between devices, local(): lax.all_to_all(partial.reshape(chips * fsdp_size, ROWS, partial.shape[-1]...  11.5 us
    pallas_call x1, Pallas kernels, partial_gradient(): pl.pallas_call(body, grid=(blocks,), in_specs=[piece, piece, whole, whole...  8.93 us
    unnamed x18, local copies, waits for them, and re-layouts  5.91 us
    all_to_all x1, starting transfers between devices, local(): lax.all_to_all(jnp.broadcast_to(fresh[None], (chips, ROWS, features)), AX...  4.24 us
  transfers between devices with their start and end apart: 7, of which 3 were waited for; matrix products, arithmetic and copies ran while one was open for 5% of the time, Pallas kernels for 17%

profile of v1, /device:TPU:1, one launch (start us, length us, event | category | flops | bytes accessed | tf_op | source)
XLA Modules:
  0.0 203.1 jit_solution(807048428914303144)
XLA Ops:
  7.2 0.0 copy-start
  7.2 0.0 all-gather.2.cloned.1.call-start
  7.2 2.3 %constant_dynamic-slice_fusion = bf16[8,1,64,1024]{3,2,1,0:T(8,128)(2,1)} fusion(bf16[8,2,64,1024]{3,2,1,0:T(8,128)(2,1)} %bitcast.20, s32[]{:T(128)S(6)} %select_n.27), kind=kLoop, calls=%fused_computation.19 | loop fusion | bytes 2097156 | tf_op jit(solution)/shard_map/jit(dynamic_index_in_dim)/dynamic_slice | solution.py:142
  9.6 0.0 all-gather.2.cloned.1.call-update
  9.6 0.0 copy-start.8
  9.6 7.5 %pack_columns.3 = bf16[8,512,512]{2,1,0:T(8,128)(2,1)S(1)} custom-call(s32[1]{0:T(128)} %bitcast.3.parity_ref, bf16[512,8192]{1,0:T(8,128)(2,1)} %x_ref.3), custom_call_target="tpu_custom_call" | custom-call | flops 1073741824 | bytes 12582912 | tf_op jit(solution)/shard_map/pack_columns/pallas_call | solution.py:33
  17.1 1.5 collective-permute-start
  18.6 0.7 convolution_convert_fusion.la_ref
  19.3 0.1 collective-permute-start.2
  19.4 7.5 %pack_columns.2.x_ref.a_ref = bf16[8,512,512]{2,1,0:T(8,128)(2,1)S(1)} custom-call(s32[1]{0:T(128)} %bitcast.parity_ref, bf16[512,8192]{1,0:T(8,128)(2,1)} %x_ref.3), custom_call_target="tpu_custom_call" | custom-call | flops 1073741824 | bytes 12582912 | tf_op jit(solution)/shard_map/pack_columns/pallas_call | solution.py:33
  26.9 2.0 copy-done.1
  28.9 1.9 copy-done.7
  30.8 8.9 %partial_gradient.1 = bf16[8,8,64,512]{3,2,1,0:T(8,128)(2,1)S(1)} custom-call(bf16[8,512,512]{2,1,0:T(8,128)(2,1)} %copy-done.1, bf16[8,512,512]{2,1,0:T(8,128)(2,1)} %copy-done.7, bf16[512,512]{1,0:T(8,128)(2,1)S(1)} %convolution_convert_fusion.la_ref, bf16[512,512]{1,0:T(8,128)(2,1)S(1)} %collective-permute-done.2.lb_ref), custom_call_target="tpu_custom_call" | custom-call | flops 4294967296 | bytes 12582912 | tf_op jit(solution)/shard_map/partial_gradient/pallas_call | solution.py:61
  39.8 2.0 copy-done.2
  41.7 11.5 %all-to-all-start = ((bf16[64,64,512]{2,1,0:T(8,128)(2,1)}), bf16[64,64,512]{2,1,0:T(8,128)(2,1)}, u32[]{:S(2)}, u32[]{:S(2)}) async-start(bf16[64,64,512]{2,1,0:T(8,128)(2,1)} %bitcast.17), calls=%async_computation | async-start | bytes 8388608 | tf_op jit(solution)/shard_map/all_to_all | solution.py:146
  53.2 0.0 copy-start.5
  53.2 98.6 %all-to-all-done = bf16[64,64,512]{2,1,0:T(8,128)(2,1)} async-done(((bf16[64,64,512]{2,1,0:T(8,128)(2,1)}), bf16[64,64,512]{2,1,0:T(8,128)(2,1)}, u32[]{:S(2)}, u32[]{:S(2)}) %all-to-all-start) | async-done | bytes 4194336 | tf_op jit(solution)/shard_map/all_to_all | solution.py:146
  151.8 2.8 %convert_reduce_fusion = f32[64,512]{1,0:T(8,128)S(1)} fusion(bf16[64,64,512]{2,1,0:T(8,128)(2,1)} %all-to-all-done), kind=kLoop, calls=%fused_computation | loop fusion | flops 4161536 | bytes 4325376 | tf_op jit(solution)/shard_map/reduce_sum | solution.py:154
  154.7 0.0 copy-start.3
  154.7 0.0 copy-start.4
  154.8 2.1 %fusion.1 = bf16[64,1024]{1,0:T(8,128)(2,1)S(1)} fusion(bf16[1024,512]{1,0:T(8,128)(2,1)S(1)} %copy-done, f32[64,512]{1,0:T(8,128)S(1)} %get-tuple-element.7, f32[64,512]{1,0:T(8,128)S(1)} %get-tuple-element.6, bf16[1024,1024]{1,0:T(8,128)(2,1)} %param.8, s32[]{:T(128)S(6)} %select_n.29), kind=kOutput, calls=%fused_computation.5 | convolution fusion | flops 403046400 | bytes 1572868 | tf_op jit(solution)/shard_map/dot_general | solution.py:160
  156.8 1.1 broadcast_in_dim.2
  157.9 4.2 %all-to-all-start.1 = ((bf16[8,64,1024]{2,1,0:T(8,128)(2,1)}), bf16[8,64,1024]{2,1,0:T(8,128)(2,1)}, u32[]{:S(2)}, u32[]{:S(2)}) async-start(bf16[8,64,1024]{2,1,0:T(8,128)(2,1)} %broadcast_in_dim.2), calls=%async_computation.1 | async-start | bytes 2097152 | tf_op jit(solution)/shard_map/all_to_all | solution.py:169
  162.2 0.0 all-gather.2.cloned.1.call-done.w_ref
  162.2 11.6 %keys_partial.2 = f32[512,1024]{1,0:T(8,128)} custom-call(bf16[8,512,512]{2,1,0:T(8,128)(2,1)} %copy-done.7, bf16[4096,1024]{1,0:T(8,128)(2,1)} %all-gather.2.cloned.1.call-done.w_ref), custom_call_target="tpu_custom_call" | custom-call | flops 4294967296 | bytes 12582912 | tf_op jit(solution)/shard_map/keys_partial/pallas_call | solution.py:104
  173.8 1.6 collective-permute-start.1
  175.4 2.2 %all-to-all-done.1 = bf16[8,64,1024]{2,1,0:T(8,128)(2,1)} async-done(((bf16[8,64,1024]{2,1,0:T(8,128)(2,1)}), bf16[8,64,1024]{2,1,0:T(8,128)(2,1)}, u32[]{:S(2)}, u32[]{:S(2)}) %all-to-all-start.1) | async-done | bytes 1048608 | tf_op jit(solution)/shard_map/all_to_all | solution.py:169
  177.6 1.4 collective-permute-start.3
  178.9 2.6 %collective-permute-done.3 = bf16[8,64,1024]{2,1,0:T(8,128)(2,1)} collective-permute-done((bf16[8,64,1024]{2,1,0:T(8,128)(2,1)}, bf16[8,64,1024]{2,1,0:T(8,128)(2,1)}, u32[]{:S(2)}, u32[]{:S(2)}) %collective-permute-start.3) | collective-permute-done | bytes 1048608 | tf_op jit(solution)/shard_map/ppermute | solution.py:177
  181.6 1.7 select_bitcast_fusion.1
  183.2 1.5 pad_maximum_fusion
  184.8 11.5 %keys_partial.3 = bf16[512,1024]{1,0:T(8,128)(2,1)} custom-call(bf16[8,512,512]{2,1,0:T(8,128)(2,1)} %copy-done.1, bf16[4096,1024]{1,0:T(8,128)(2,1)} %all-gather.2.cloned.1.call-done.w_ref, f32[512,1024]{1,0:T(8,128)S(1)} %collective-permute-done.1.refs_0_), custom_call_target="tpu_custom_call" | custom-call | flops 4294967296 | bytes 12582912 | tf_op jit(solution)/shard_map/keys_partial/pallas_call | solution.py:104
  (14 shorter events, 0.1 us)
Async XLA Ops:
  7.2 11.4 %copy-start = (bf16[1024,512]{1,0:T(8,128)(2,1)S(1)}, bf16[1024,512]{1,0:T(8,128)(2,1)}, u32[]{:S(2)}) copy-start(bf16[1024,512]{1,0:T(8,128)(2,1)} %param.9) | copy-start | bytes 3145732
  7.2 155.0 %all-gather.2.cloned.1.call-start = ((), (), s32[]{:S(2)}) async-start(), calls=%async_computation.2 | async-start | bytes 9437184 | tf_op jit(solution)/shard_map/all_gather | solution.py:143
  9.6 9.0 %copy-start.8 = (bf16[512,1024]{1,0:T(8,128)(2,1)S(1)}, bf16[512,1024]{1,0:T(8,128)(2,1)}, u32[]{:S(2)}) copy-start(bf16[512,1024]{1,0:T(8,128)(2,1)} %param.7) | copy-start | bytes 3145732
  17.1 11.8 %collective-permute-start = (bf16[8,512,512]{2,1,0:T(8,128)(2,1)S(1)}, bf16[8,512,512]{2,1,0:T(8,128)(2,1)S(1)}, u32[]{:S(2)}, u32[]{:S(2)}) collective-permute-start(bf16[8,512,512]{2,1,0:T(8,128)(2,1)S(1)} %pack_columns.3), channel_id=1, source_target_pairs={{0,8},{1,9},{2,10},{3,11},{4,12},{5,13},{6,14},{7,15},{8,0},{9,1},... | collective-permute-start | bytes 12582920 | tf_op jit(solution)/shard_map/ppermute | solution.py:136
  19.3 9.6 %collective-permute-start.2 = (bf16[512,512]{1,0:T(8,128)(2,1)S(1)}, bf16[512,512]{1,0:T(8,128)(2,1)S(1)}, u32[]{:S(2)}, u32[]{:S(2)}) collective-permute-start(bf16[512,512]{1,0:T(8,128)(2,1)S(1)} %convolution_convert_fusion.la_ref), channel_id=1, source_target_pairs={{0,8},{1,9},{2,10},{3,11},{4,12},{5,13},{6,14},{7,15},{8,0},{9,1},... | collective-permute-start | bytes 1572872 | tf_op jit(solution)/shard_map/ppermute | solution.py:138
  26.9 2.0 copy-start.1
  28.9 1.9 copy-start.7
  39.8 2.0 copy-start.2
  41.7 110.1 %all-to-all-start = ((bf16[64,64,512]{2,1,0:T(8,128)(2,1)}), bf16[64,64,512]{2,1,0:T(8,128)(2,1)}, u32[]{:S(2)}, u32[]{:S(2)}) async-start(bf16[64,64,512]{2,1,0:T(8,128)(2,1)} %bitcast.17), calls=%async_computation | async-start | bytes 8388608 | tf_op jit(solution)/shard_map/all_to_all | solution.py:146
  53.2 101.5 %copy-start.5 = (f32[64,512]{1,0:T(8,128)S(1)}, f32[64,512]{1,0:T(8,128)}, u32[]{:S(2)}) copy-start(f32[64,512]{1,0:T(8,128)} %param.10) | copy-start | bytes 393220
  53.2 101.5 %copy-start.6 = (f32[64,512]{1,0:T(8,128)S(1)}, f32[64,512]{1,0:T(8,128)}, u32[]{:S(2)}) copy-start(f32[64,512]{1,0:T(8,128)} %param.11) | copy-start | bytes 393220
  154.7 19.1 %copy-start.3 = (f32[64,512]{1,0:T(8,128)}, f32[64,512]{1,0:T(8,128)S(1)}, u32[]{:S(2)}) copy-start(f32[64,512]{1,0:T(8,128)S(1)} %get-tuple-element.6) | copy-start | bytes 393220
  154.7 19.1 %copy-start.4 = (f32[64,512]{1,0:T(8,128)}, f32[64,512]{1,0:T(8,128)S(1)}, u32[]{:S(2)}) copy-start(f32[64,512]{1,0:T(8,128)S(1)} %get-tuple-element.7) | copy-start | bytes 393220
  157.9 19.6 %all-to-all-start.1 = ((bf16[8,64,1024]{2,1,0:T(8,128)(2,1)}), bf16[8,64,1024]{2,1,0:T(8,128)(2,1)}, u32[]{:S(2)}, u32[]{:S(2)}) async-start(bf16[8,64,1024]{2,1,0:T(8,128)(2,1)} %broadcast_in_dim.2), calls=%async_computation.1 | async-start | bytes 2097152 | tf_op jit(solution)/shard_map/all_to_all | solution.py:169
  173.8 10.9 %collective-permute-start.1 = (f32[512,1024]{1,0:T(8,128)}, f32[512,1024]{1,0:T(8,128)S(1)}, u32[]{:S(2)}, u32[]{:S(2)}) collective-permute-start(f32[512,1024]{1,0:T(8,128)} %keys_partial.2), channel_id=1, source_target_pairs={{0,8},{1,9},{2,10},{3,11},{4,12},{5,13},{6,14},{7,15},{8,0},{9,1},... | collective-permute-start | bytes 6291464 | tf_op jit(solution)/shard_map/ppermute | solution.py:183
  177.6 4.0 %collective-permute-start.3 = (bf16[8,64,1024]{2,1,0:T(8,128)(2,1)}, bf16[8,64,1024]{2,1,0:T(8,128)(2,1)}, u32[]{:S(2)}, u32[]{:S(2)}) collective-permute-start(bf16[8,64,1024]{2,1,0:T(8,128)(2,1)} %all-to-all-done.1), channel_id=1, source_target_pairs={{0,8},{1,9},{2,10},{3,11},{4,12},{5,13},{6,14},{7,15},{8,0},{9,1},... | collective-permute-start | bytes 3145736 | tf_op jit(solution)/shard_map/ppermute | solution.py:177
Sparse Core Ops, SparseCore 0:
  10.2 141.7 all-gather.1

commit v2 on v0

v2 whole, which is shorter than its diff:
```python
import jax
import jax.numpy as jnp
from jax import lax
from jax.experimental import pallas as pl
from jax.experimental.pallas import tpu as pltpu
from jax.sharding import PartitionSpec as P

STEP = 100
AXES = ("dp", "fsdp")

learn_rate = 0.01
galore_scale = 0.25

ROWS = 64
VMEM = 48 * 1024 * 1024


CORE, LO, X = 2, 2, 4
PAIR = 2 * ROWS


def pack_columns(place, tokens):
    count, width = tokens.shape
    steps = 4
    tall = count // steps

    def body(place_ref, x_ref, own_ref, send_ref):
        for now in range(2):

            @pl.when(place_ref[0] == now)
            def _():
                for j, (y, shard) in enumerate((y, shard) for y in range(4) for shard in range(LO * X)):
                    for out_ref, side in ((own_ref, now), (send_ref, 1 - now)):
                        a = shard * (width // (LO * X)) + y * 2 * PAIR + side * ROWS
                        out_ref[:, j * PAIR : (j + 1) * PAIR] = jnp.concatenate(
                            [x_ref[:, a : a + ROWS], x_ref[:, a + PAIR : a + PAIR + ROWS]], axis=1
                        )

    out = jax.ShapeDtypeStruct((count, width // 2), jnp.bfloat16)
    spec = pl.BlockSpec((tall, width // 2), lambda i, c: (i, 0))
    return pl.pallas_call(
        body,
        grid_spec=pltpu.PrefetchScalarGridSpec(
            num_scalar_prefetch=1,
            grid=(steps,),
            in_specs=[pl.BlockSpec((tall, width), lambda i, c: (i, 0))],
            out_specs=[spec, spec],
        ),
        out_shape=[out, out],
        compiler_params=pltpu.CompilerParams(vmem_limit_bytes=VMEM),
        cost_estimate=pl.CostEstimate(flops=1, bytes_accessed=1, transcendentals=0),
        name="pack_columns",
    )(place, tokens)


def pack_rows(place, weight):
    chips, _, rows, features = weight.shape
    steps = 2
    block = chips // steps

    def body(place_ref, w_ref, o_ref):
        o_ref[...] = w_ref[:, place_ref[0]]

    return pl.pallas_call(
        body,
        grid_spec=pltpu.PrefetchScalarGridSpec(
            num_scalar_prefetch=1,
            grid=(steps,),
            in_specs=[pl.BlockSpec((block, 2, rows, features), lambda i, c: (i, 0, 0, 0))],
            out_specs=pl.BlockSpec((block, rows, features), lambda i, c: (i, 0, 0)),
        ),
        out_shape=jax.ShapeDtypeStruct((chips, rows, features), weight.dtype),
        compiler_params=pltpu.CompilerParams(vmem_limit_bytes=VMEM),
        cost_estimate=pl.CostEstimate(flops=1, bytes_accessed=1, transcendentals=0),
        name="pack_rows",
    )(place, weight)


def keys_of(packed, place, near, far):
    _, _, part, features = near.shape
    count = LO * X
    tokens = packed.shape[0]
    depth = count * 4 * part
    wide = features // 4

    def body(place_ref, x_ref, near_ref, far_ref, o_ref, rows_ref, x_now, sems):
        copies = [pltpu.make_async_copy(x_ref, x_now, sems.at[count])]
        for lo, ref in enumerate((near_ref, far_ref)):
            for x in range(X):
                at = lax.rem(place_ref[1] + lo, LO) * X + x
                copies.append(pltpu.make_async_copy(ref.at[x], rows_ref.at[:, at], sems.at[lo * X + x]))
        for copy in copies:
            copy.start()
        for copy in copies:
            copy.wait()
        for n in range(4):
            columns = slice(n * wide, (n + 1) * wide)
            block = rows_ref[:, :, :, columns].reshape(depth, wide)
            o_ref[:, columns] = jnp.dot(x_now[...], block, preferred_element_type=jnp.float32)

    out, joined = pl.pallas_call(
        body,
        grid_spec=pltpu.PrefetchScalarGridSpec(
            num_scalar_prefetch=1,
            grid=(),
            in_specs=[pl.BlockSpec(memory_space=pl.ANY)] * 3,
            out_specs=[pl.BlockSpec(memory_space=pltpu.VMEM)] * 2,
            scratch_shapes=[pltpu.VMEM(packed.shape, packed.dtype), pltpu.SemaphoreType.DMA((count + 1,))],
        ),
        out_shape=[
            jax.ShapeDtypeStruct((tokens, features), jnp.float32),
            jax.ShapeDtypeStruct((4, count, part, features), jnp.bfloat16),
        ],
        compiler_params=pltpu.CompilerParams(vmem_limit_bytes=VMEM),
        cost_estimate=pl.CostEstimate(flops=1, bytes_accessed=1, transcendentals=0),
        name="keys_of",
    )(place, packed, near, far)
    return out, joined.reshape(depth, features)


def together(*arrays, after=()):
    def body(*refs):
        pass

    return pl.pallas_call(
        body,
        in_specs=[pl.BlockSpec(memory_space=pl.ANY)] * (len(arrays) + len(after)),
        out_specs=[pl.BlockSpec(memory_space=pl.ANY)] * len(arrays),
        out_shape=[jax.ShapeDtypeStruct(a.shape, a.dtype) for a in arrays],
        input_output_aliases={i: i for i in range(len(arrays))},
        name="together",
    )(*arrays, *after)


def device(x, y, z, core):
    return ((y % 4) * 4 + (z % 4 >> 1) * 2 + core % 2) * 8 + (z % 2) * 4 + x % 4


def every():
    return [(x, y, z, c) for y in range(4) for z in range(4) for c in range(2) for x in range(4)]


def move(array, x=0, y=0, z=0, core=0):
    return lax.ppermute(
        array, AXES, [(device(*at), device(at[0] + x, at[1] + y, at[2] + z, at[3] + core)) for at in every()]
    )


def move_apart(array, x=0, z=0):
    pairs = []
    for at in every():
        sign = 1 - 2 * at[3]
        pairs.append((device(*at), device(at[0] + sign * x, at[1], at[2] + sign * z, at[3])))
    return lax.ppermute(array, AXES, pairs)


def exchange(array, groups):
    return lax.all_to_all(array, AXES, split_axis=0, concat_axis=0, axis_index_groups=groups, tiled=True)


def local(tokens, cotangent, weight, basis, exp_avg, exp_avg_sq):
    core = lax.axis_index("dp") % 2
    shard = lax.axis_index("fsdp")
    my_lo = shard // X
    my_z = lax.axis_index("dp") // 2 % 2 * 2 + my_lo
    features = weight.shape[1]
    chips = lax.axis_size("dp") // CORE
    rank = basis.shape[1]
    along_y = [[device(x, y, z, c) for y in range(4)] for x in range(4) for z in range(4) for c in range(2)]
    along_x = [[device(x, y, z, c) for x in range(4)] for y in range(4) for z in range(4) for c in range(2)]
    same_shard = [
        [device(x, y, z + 2 * hi, c) for y in range(4) for hi in range(2)]
        for x in range(4)
        for z in range(2)
        for c in range(2)
    ]
    place = jnp.stack([core, my_lo])

    def wide(array):
        return array.astype(jnp.float32)

    own, send = pack_columns(place, tokens)
    other = move(send, core=1)
    low = jnp.dot(cotangent, basis, preferred_element_type=jnp.float32).astype(jnp.bfloat16)
    low_other = move(low, core=1)

    half = pack_rows(place, weight.reshape(chips, CORE, ROWS, features)).reshape(-1, features)
    near = lax.all_gather(half, AXES, axis=0, tiled=True, axis_index_groups=along_x)
    far = move_apart(half, z=-1)

    contract = (((0,), (0,)), ((), ()))
    partial = lax.dot_general(own, low, contract, preferred_element_type=jnp.float32)
    partial = partial + lax.dot_general(other, low_other, contract, preferred_element_type=jnp.float32)
    partial = partial.astype(jnp.bfloat16)

    def sum_all(spread):
        total = wide(spread[0])
        for i in range(1, spread.shape[0]):
            total = total + wide(spread[i])
        return total

    (far,) = together(far, after=(partial,))
    far = lax.all_gather(far, AXES, axis=0, tiled=True, axis_index_groups=along_x)

    def sum_z(parts):
        def take(step):
            z = (my_z + step) % 4
            some = lax.dynamic_slice_in_dim(parts, z % 2, 1, axis=-5)
            some = lax.dynamic_slice_in_dim(some, z // 2, 1, axis=-3)
            return some.reshape(-1, ROWS, parts.shape[-1])

        total = wide(take(0))
        for step in (1, 3, 2):
            total = total + wide(move(take(step), z=step))
        return total.astype(jnp.bfloat16)

    first = partial[:, : rank // 2].reshape(4, -1, rank // 2)
    first = sum_all(exchange(first, along_y)).astype(jnp.bfloat16)
    second = sum_z(partial[:, rank // 2 :].reshape(4, LO, X, 2, ROWS, rank // 2))
    first, second = together(first, second)
    second = sum_all(exchange(second.reshape(4, X * ROWS, rank // 2), along_y)).astype(jnp.bfloat16)
    first = sum_z(first.reshape(LO, X, 2, ROWS, rank // 2))
    both = jnp.concatenate([first.reshape(X, ROWS, -1), second.reshape(X, ROWS, -1)], axis=2)
    projected = sum_all(exchange(both, along_x))
    new_avg = 0.9 * exp_avg + 0.1 * projected
    new_sq = 0.999 * exp_avg_sq + 0.001 * projected * projected
    first_fix = 1.0 - 0.9**STEP
    second_fix = 1.0 - 0.999**STEP
    direction = new_avg / first_fix / (jnp.sqrt(new_sq / second_fix) + 1e-08)
    direction = direction.astype(jnp.bfloat16)
    near, far = (rows.reshape(X, 4, 2 * ROWS, features) for rows in (near, far))
    for_other, rows = keys_of(other, place, near, far)
    own_keys = jnp.dot(own, rows, preferred_element_type=jnp.float32)

    mine = exchange(jnp.broadcast_to(direction[None], (chips, ROWS, rank)), same_shard)
    mine, own_keys = together(mine, own_keys)
    theirs = move(mine, core=1)
    from_other = move(for_other, core=1)
    even = jnp.where(core == 0, mine, theirs)
    odd = jnp.where(core == 0, theirs, mine)
    update = lax.dot_general(
        jnp.stack([even, odd], axis=1).reshape(-1, rank),
        basis,
        (((1,), (1,)), ((), ())),
        preferred_element_type=jnp.float32,
    )
    new_weight = (wide(weight) - learn_rate * galore_scale * update).astype(jnp.bfloat16)
    keys = (own_keys + from_other).astype(jnp.bfloat16)
    return (keys, new_weight, new_avg, new_sq)


def solution(mesh):
    in_specs = (
        P(("dp", "fsdp"), None),
        P(("dp", "fsdp"), None),
        P("fsdp", None),
        P(),
        P(("fsdp", "dp"), None),
        P(("fsdp", "dp"), None),
    )
    out_specs = (
        P(("dp", "fsdp"), None),
        P("fsdp", None),
        P(("fsdp", "dp"), None),
        P(("fsdp", "dp"), None),
    )
    return jax.shard_map(local, mesh=mesh, in_specs=in_specs, out_specs=out_specs, check_vma=False)
```

time: 916 us -> 152 us (0.17)
  waiting for transfers between devices: 835 us -> 40.1 us
  starting transfers between devices: 0.12 us -> 26 us
  local copies, waits for them, and re-layouts: 33.8 us -> 11 us
  Pallas kernels: 0 us -> 20.4 us
  blocking collectives: 0 us -> 12.8 us
  matrix products: 30.1 us -> 18.7 us
    reduce_scatter x1 -> x0, waiting for transfers between devices: 788 us -> none  [local(): lax.psum_scatter(ordered, ('dp', 'fsdp'), scatter_dimension=0, tiled=True)]
    all_gather x2, waiting for transfers between devices: 46.3 us -> 3.22 us  [the longest x1 3.21 us: local(): lax.all_gather(far, AXES, axis=0, tiled=True, axis_index_groups=along_x)]
    ppermute x0 -> x11, waiting for transfers between devices: none -> 36.9 us  [the longest x10 32.4 us: move(): lax.ppermute(array, AXES, [(device(*at), device(at[0] + x, at[1] + y, at[...]
    pallas_call x0 -> x6, Pallas kernels: none -> 20.4 us  [the longest x1 11.3 us: keys_of(): pl.pallas_call(body, grid_spec=pltpu.PrefetchScalarGridSpec(num_scalar_pr...]
    dot_general x1 -> x0, local copies, waits for them, and re-layouts: 17.4 us -> none  [local(): lax.dot_general(columns, low, (((0,), (0,)), ((), ())), preferred_element...]
    all_to_all x0 -> x3, starting transfers between devices: none -> 14 us  [exchange(): lax.all_to_all(array, AXES, split_axis=0, concat_axis=0, axis_index_group...]
    all_to_all x0 -> x1, blocking collectives: none -> 12.8 us  [exchange(): lax.all_to_all(array, AXES, split_axis=0, concat_axis=0, axis_index_group...]
    transpose x1 -> x0, local copies, waits for them, and re-layouts: 12 us -> none  [local(): ordered = whole.reshape(fsdp_size, dp_size, block, rank_cols).transpose(1...]
  transfers between devices with their start and end apart: 3 -> 16, of which waited for: 2 -> 10; matrix products, arithmetic and copies ran while one was open for 2% -> 21% of each run, Pallas kernels for 0% -> 12%
where the time goes in v2:
time: 152 us
  waiting for transfers between devices  40.1 us (26%)
  starting transfers between devices  26 us (17%)
  Pallas kernels  20.4 us (13%)
  matrix products  18.7 us (12%)
  between operations  14.2 us (9%)
  blocking collectives  12.8 us (8%)
  local copies, waits for them, and re-layouts  11 us (7%)
  other arithmetic  8.5 us (6%)
    ppermute x10, waiting for transfers between devices, move(): lax.ppermute(array, AXES, [(device(*at), device(at[0] + x, at[1] + y, at[...  32.4 us
    all_to_all x3, starting transfers between devices, exchange(): lax.all_to_all(array, AXES, split_axis=0, concat_axis=0, axis_index_group...  14 us
    all_to_all x1, blocking collectives, exchange(): lax.all_to_all(array, AXES, split_axis=0, concat_axis=0, axis_index_group...  12.8 us
    pallas_call x1, Pallas kernels, keys_of(): pl.pallas_call(body, grid_spec=pltpu.PrefetchScalarGridSpec(num_scalar_pr...  11.3 us
    ppermute x10, starting transfers between devices, move(): lax.ppermute(array, AXES, [(device(*at), device(at[0] + x, at[1] + y, at[...  10.2 us
    dot_general x1, matrix products, local(): own_keys = jnp.dot(own, rows, preferred_element_type=jnp.float32)  8.3 us
    pallas_call x1, Pallas kernels, pack_columns(): pl.pallas_call(body, grid_spec=pltpu.PrefetchScalarGridSpec(num_scalar_pr...  7.53 us
    dot_general x1, matrix products, local(): lax.dot_general(other, low_other, contract, preferred_element_type=jnp.fl...  4.63 us
  transfers between devices with their start and end apart: 16, of which 10 were waited for; matrix products, arithmetic and copies ran while one was open for 21% of the time, Pallas kernels for 12%

profile of v2, /device:TPU:1, one launch (start us, length us, event | category | flops | bytes accessed | tf_op | source)
XLA Modules:
  0.0 151.7 jit_solution(14129781143736765494)
XLA Ops:
  7.3 1.7 %copy-done.3 = bf16[1024,1024]{1,0:T(8,128)(2,1)S(1)} copy-done((bf16[1024,1024]{1,0:T(8,128)(2,1)S(1)}, bf16[1024,1024]{1,0:T(8,128)(2,1)}, u32[]{:S(2)}) %copy-start.3) | copy-done | bytes 2097176
  9.0 1.6 %pack_rows.1 = bf16[8,64,1024]{2,1,0:T(8,128)(2,1)} custom-call(s32[2]{0:T(128)S(1)} %pad_add_fusion.place_ref, bf16[8,2,64,1024]{3,2,1,0:T(8,128)(2,1)S(1)} %bitcast.53), custom_call_target="tpu_custom_call" | custom-call | flops 1 | bytes 1 | tf_op jit(solution)/shard_map/pack_rows/pallas_call | solution.py:64
  10.7 7.5 %pack_columns.1 = (bf16[512,4096]{1,0:T(8,128)(2,1)S(1)}, bf16[512,4096]{1,0:T(8,128)(2,1)}) custom-call(s32[2]{0:T(128)S(1)} %pad_add_fusion.place_ref, bf16[512,8192]{1,0:T(8,128)(2,1)} %x_ref.1), custom_call_target="tpu_custom_call" | custom-call | flops 1 | bytes 1 | tf_op jit(solution)/shard_map/pack_columns/pallas_call | solution.py:41
  18.2 1.4 collective-permute-start
  19.6 1.7 %collective-permute-start.8 = (bf16[512,1024]{1,0:T(8,128)(2,1)}, bf16[512,1024]{1,0:T(8,128)(2,1)S(1)}, u32[]{:S(2)}, u32[]{:S(2)}) collective-permute-start(bf16[512,1024]{1,0:T(8,128)(2,1)} %bitcast.18), channel_id=1, source_target_pairs={{0,20},{1,21},{2,22},{3,23},{8,12},{9,13},{10,14},{11,15},{4,0},{5... | collective-permute-start | bytes 3145736 | tf_op jit(solution)/shard_map/ppermute | solution.py:154
  22.0 2.5 %collective-permute-start.1 = (bf16[512,512]{1,0:T(8,128)(2,1)S(1)}, bf16[512,512]{1,0:T(8,128)(2,1)S(1)}, u32[]{:S(2)}, u32[]{:S(2)}) collective-permute-start(bf16[512,512]{1,0:T(8,128)(2,1)S(1)} %convolution_convert_fusion), channel_id=1, source_target_pairs={{0,8},{1,9},{2,10},{3,11},{8,0},{9,1},{10,2},{11,3},{4,12},{5,13},... | collective-permute-start | bytes 1572872 | tf_op jit(solution)/shard_map/ppermute | solution.py:144
  24.5 2.4 %fusion.12 = f32[4096,512]{1,0:T(8,128)S(1)} fusion(bf16[512,4096]{1,0:T(8,128)(2,1)S(1)} %get-tuple-element.12, bf16[512,512]{1,0:T(8,128)(2,1)S(1)} %convolution_convert_fusion), kind=kOutput, calls=%fused_computation.34 | convolution fusion | flops 2147483648 | bytes 13107200 | tf_op jit(solution)/shard_map/dot_general | solution.py:192
  27.1 4.6 %add_convert_fusion.refs_1_ = bf16[4096,512]{1,0:T(8,128)(2,1)} fusion(f32[4096,512]{1,0:T(8,128)S(1)} %fusion.12, bf16[512,4096]{1,0:T(8,128)(2,1)S(1)} %collective-permute-done.x_ref, bf16[512,512]{1,0:T(8,128)(2,1)S(1)} %collective-permute-done.1), kind=kOutput, calls=%fused_computation | convolution fusion | flops 2151677952 | bytes 17301504 | tf_op jit(solution)/shard_map/dot_general | solution.py:193
  31.8 4.5 %collective-permute-done.8.refs_0_ = bf16[512,1024]{1,0:T(8,128)(2,1)S(1)} collective-permute-done((bf16[512,1024]{1,0:T(8,128)(2,1)}, bf16[512,1024]{1,0:T(8,128)(2,1)S(1)}, u32[]{:S(2)}, u32[]{:S(2)}) %collective-permute-start.8) | collective-permute-done | bytes 1048608 | tf_op jit(solution)/shard_map/ppermute | solution.py:154
  37.2 4.6 %fusion.11 = (bf16[4096,256]{1,0:T(8,128)(2,1)}, bf16[4096,256]{1,0:T(8,128)(2,1)}) fusion(bf16[4096,512]{1,0:T(8,128)(2,1)} %add_convert_fusion.refs_1_), kind=kLoop, calls=%fused_computation.33 | loop fusion | bytes 8388608 | tf_op jit(solution)/shard_map/slice | solution.py:219
  41.9 4.2 %all-to-all-start = ((bf16[4,1024,256]{2,1,0:T(8,128)(2,1)}), bf16[4,1024,256]{2,1,0:T(8,128)(2,1)S(1)}, u32[]{:S(2)}, u32[]{:S(2)}) async-start(bf16[4,1024,256]{2,1,0:T(8,128)(2,1)} %bitcast.55), calls=%async_computation | async-start | bytes 4194304 | tf_op jit(solution)/shard_map/all_to_all | solution.py:158
  46.0 1.7 %constant_dynamic-slice_fusion.3 = (bf16[4,1,4,1,64,256]{5,4,3,2,1,0:T(8,128)(2,1)S(1)}, bf16[4,1,4,1,64,256]{5,4,3,2,1,0:T(8,128)(2,1)S(1)}, bf16[4,1,4,1,64,25...) fusion(bf16[4,2,4,2,64,256]{5,4,3,2,1,0:T(8,128)(2,1)} %bitcast.54, s32[]{:T(128)S(6)} %select_n.149, ...), kind=kLoop, calls=%fused_computation.31 | loop fusion | bytes 4194336 | tf_op jit(solution)/shard_map/dynamic_slice | solution.py:209
  47.7 1.3 collective-permute-start.4
  50.5 11.9 %collective-permute-done.4 = bf16[16,64,256]{2,1,0:T(8,128)(2,1)S(1)} collective-permute-done((bf16[16,64,256]{2,1,0:T(8,128)(2,1)S(1)}, bf16[16,64,256]{2,1,0:T(8,128)(2,1)S(1)}, u32[]{:S(2)}, u32[]{:S(2)}) %collective-permute-start.4) | collective-permute-done | bytes 524320 | tf_op jit(solution)/shard_map/ppermute | solution.py:144
  62.4 9.8 %collective-permute-done.3 = bf16[16,64,256]{2,1,0:T(8,128)(2,1)S(1)} collective-permute-done((bf16[16,64,256]{2,1,0:T(8,128)(2,1)S(1)}, bf16[16,64,256]{2,1,0:T(8,128)(2,1)S(1)}, u32[]{:S(2)}, u32[]{:S(2)}) %collective-permute-start.3) | collective-permute-done | bytes 524320 | tf_op jit(solution)/shard_map/ppermute | solution.py:144
  72.3 2.1 %collective-permute-done.2 = bf16[16,64,256]{2,1,0:T(8,128)(2,1)S(1)} collective-permute-done((bf16[16,64,256]{2,1,0:T(8,128)(2,1)S(1)}, bf16[16,64,256]{2,1,0:T(8,128)(2,1)S(1)}, u32[]{:S(2)}, u32[]{:S(2)}) %collective-permute-start.2) | collective-permute-done | bytes 524320 | tf_op jit(solution)/shard_map/ppermute | solution.py:144
  74.4 1.2 fusion.2.refs_1_
  75.6 1.1 fusion.3.refs_0_
  76.7 4.2 %all-to-all-start.1 = ((bf16[4,256,256]{2,1,0:T(8,128)(2,1)}), bf16[4,256,256]{2,1,0:T(8,128)(2,1)S(1)}, u32[]{:S(2)}, u32[]{:S(2)}) async-start(bf16[4,256,256]{2,1,0:T(8,128)(2,1)} %bitcast.56), calls=%async_computation.1 | async-start | bytes 1048576 | tf_op jit(solution)/shard_map/all_to_all | solution.py:158
  82.0 1.3 collective-permute-start.7
  84.8 3.1 %collective-permute-done.7 = bf16[4,64,256]{2,1,0:T(8,128)(2,1)S(1)} collective-permute-done((bf16[4,64,256]{2,1,0:T(8,128)(2,1)S(1)}, bf16[4,64,256]{2,1,0:T(8,128)(2,1)S(1)}, u32[]{:S(2)}, u32[]{:S(2)}) %collective-permute-start.7) | collective-permute-done | bytes 131104 | tf_op jit(solution)/shard_map/ppermute | solution.py:144
  87.8 1.7 %collective-permute-done.6 = bf16[4,64,256]{2,1,0:T(8,128)(2,1)S(1)} collective-permute-done((bf16[4,64,256]{2,1,0:T(8,128)(2,1)S(1)}, bf16[4,64,256]{2,1,0:T(8,128)(2,1)S(1)}, u32[]{:S(2)}, u32[]{:S(2)}) %collective-permute-start.6) | collective-permute-done | bytes 131104 | tf_op jit(solution)/shard_map/ppermute | solution.py:144
  89.5 1.3 collective-permute-done.5
  92.0 12.8 %all_to_all.20 = bf16[4,64,512]{2,1,0:T(8,128)(2,1)S(1)} all-to-all(bf16[4,64,512]{2,1,0:T(8,128)(2,1)S(1)} %pad_maximum_fusion.1), channel_id=1, replica_groups={{0,1,2,3},{8,9,10,11},{4,5,6,7},{12,13,14,15},{16,17,18,19},{24,25,26,2..., dimensions={0} | all-to-all | bytes 524288 | tf_op jit(solution)/shard_map/all_to_all | solution.py:158
  106.4 5.6 %all-to-all-start.3 = ((bf16[8,64,512]{2,1,0:T(8,128)(2,1)}), bf16[8,64,512]{2,1,0:T(8,128)(2,1)}, u32[]{:S(2)}, u32[]{:S(2)}) async-start(bf16[8,64,512]{2,1,0:T(8,128)(2,1)} %broadcast_in_dim.2), calls=%async_computation.3 | async-start | bytes 1048576 | tf_op jit(solution)/shard_map/all_to_all | solution.py:158
  112.0 3.2 %all-gather.5.cloned.1.call-done = bf16[2048,1024]{1,0:T(8,128)(2,1)} async-done(((bf16[512,1024]{1,0:T(8,128)(2,1)}), bf16[2048,1024]{1,0:T(8,128)(2,1)}) %all-gather.5.cloned.1.call-update) | async-done | bytes 4194320 | tf_op jit(solution)/shard_map/all_gather | solution.py:203
  115.2 11.3 %keys_of.1 = (f32[512,1024]{1,0:T(8,128)}, bf16[4,8,128,1024]{3,2,1,0:T(8,128)(2,1)}) custom-call(s32[2]{0:T(128)S(1)} %pad_add_fusion.place_ref, bf16[512,4096]{1,0:T(8,128)(2,1)} %copy-done.5, bf16[4,4,128,1024]{3,2,1,0:T(8,128)(2,1)} %bitcast.59, bf16[4,4,128,1024]{3,2,1,0:T(8,128)(2,1)} %bitcast.60), custom_call_target="tpu_custom_call" | custom-call | flops 1 | bytes 1 | tf_op jit(solution)/shard_map/keys_of/pallas_call | solution.py:101
  127.4 8.3 %fusion.13.refs_1_ = f32[512,1024]{1,0:T(8,128)} fusion(bf16[512,4096]{1,0:T(8,128)(2,1)S(1)} %copy-done.2, bf16[4096,1024]{1,0:T(8,128)(2,1)} %bitcast.66), kind=kOutput, calls=%fused_computation.35 | convolution fusion | flops 4294967296 | bytes 14680064 | tf_op jit(solution)/shard_map/dot_general | solution.py:233
  135.7 2.2 %collective-permute-done.10 = bf16[8,64,512]{2,1,0:T(8,128)(2,1)} collective-permute-done((bf16[8,64,512]{2,1,0:T(8,128)(2,1)}, bf16[8,64,512]{2,1,0:T(8,128)(2,1)}, u32[]{:S(2)}, u32[]{:S(2)}) %collective-permute-start.10) | collective-permute-done | bytes 524320 | tf_op jit(solution)/shard_map/ppermute | solution.py:144
  137.9 1.3 select_bitcast_fusion.1
  139.4 2.6 %subtract_convert_fusion = bf16[1024,1024]{1,0:T(8,128)(2,1)} fusion(bf16[1024,1024]{1,0:T(8,128)(2,1)S(1)} %copy-done.4, bf16[1024,512]{1,0:T(8,128)(2,1)S(1)} %bitcast.61, bf16[1024,512]{1,0:T(8,128)(2,1)S(1)} %copy-done), kind=kOutput, calls=%fused_computation.1 | convolution fusion | flops 1077936128 | bytes 6291456 | tf_op jit(solution)/shard_map/dot_general | solution.py:241
  142.0 2.9 %add_convert_fusion.1 = bf16[512,1024]{1,0:T(8,128)(2,1)} fusion(f32[512,1024]{1,0:T(8,128)S(1)} %copy-done.6, f32[512,1024]{1,0:T(8,128)} %collective-permute-done.9), kind=kLoop, calls=%fused_computation.2 | loop fusion | flops 1048576 | bytes 5242880 | tf_op jit(solution)/shard_map/convert_element_type | solution.py:248
  (51 shorter events, 9.8 us)
Async XLA Ops:
  7.2 14.1 %copy-start = (bf16[1024,512]{1,0:T(8,128)(2,1)S(1)}, bf16[1024,512]{1,0:T(8,128)(2,1)}, u32[]{:S(2)}) copy-start(bf16[1024,512]{1,0:T(8,128)(2,1)} %param.9) | copy-start | bytes 3145732
  7.2 104.8 %all-gather.3.cloned.1.call-start = ((), (), s32[]{:S(2)}) async-start(), calls=%async_computation.4 | async-start | bytes 5242880 | tf_op jit(solution)/shard_map/all_gather | solution.py:188
  7.3 1.7 %copy-start.3 = (bf16[1024,1024]{1,0:T(8,128)(2,1)S(1)}, bf16[1024,1024]{1,0:T(8,128)(2,1)}, u32[]{:S(2)}) copy-start(bf16[1024,1024]{1,0:T(8,128)(2,1)} %param.8) | copy-start | bytes 6291460
  10.6 104.6 %all-gather.5.cloned.1.call-start = ((), (), s32[]{:S(2)}) async-start(), calls=%async_computation.5 | async-start | bytes 5242880 | tf_op jit(solution)/shard_map/all_gather | solution.py:203
  10.6 10.7 %copy-start.10 = (bf16[512,1024]{1,0:T(8,128)(2,1)S(1)}, bf16[512,1024]{1,0:T(8,128)(2,1)}, u32[]{:S(2)}) copy-start(bf16[512,1024]{1,0:T(8,128)(2,1)} %param.7) | copy-start | bytes 3145732
  18.2 8.8 %copy-start.1 = (bf16[512,4096]{1,0:T(8,128)(2,1)}, bf16[512,4096]{1,0:T(8,128)(2,1)S(1)}, u32[]{:S(2)}) copy-start(bf16[512,4096]{1,0:T(8,128)(2,1)S(1)} %get-tuple-element.12) | copy-start | bytes 12582916
  18.2 8.9 %collective-permute-start = (bf16[512,4096]{1,0:T(8,128)(2,1)}, bf16[512,4096]{1,0:T(8,128)(2,1)S(1)}, u32[]{:S(2)}, u32[]{:S(2)}) collective-permute-start(bf16[512,4096]{1,0:T(8,128)(2,1)} %get-tuple-element.13), channel_id=1, source_target_pairs={{0,8},{1,9},{2,10},{3,11},{8,0},{9,1},{10,2},{11,3},{4,12},{5,13},... | collective-permute-start | bytes 12582920 | tf_op jit(solution)/shard_map/ppermute | solution.py:144
  19.6 16.6 %collective-permute-start.8 = (bf16[512,1024]{1,0:T(8,128)(2,1)}, bf16[512,1024]{1,0:T(8,128)(2,1)S(1)}, u32[]{:S(2)}, u32[]{:S(2)}) collective-permute-start(bf16[512,1024]{1,0:T(8,128)(2,1)} %bitcast.18), channel_id=1, source_target_pairs={{0,20},{1,21},{2,22},{3,23},{8,12},{9,13},{10,14},{11,15},{4,0},{5... | collective-permute-start | bytes 3145736 | tf_op jit(solution)/shard_map/ppermute | solution.py:154
  22.0 5.1 %collective-permute-start.1 = (bf16[512,512]{1,0:T(8,128)(2,1)S(1)}, bf16[512,512]{1,0:T(8,128)(2,1)S(1)}, u32[]{:S(2)}, u32[]{:S(2)}) collective-permute-start(bf16[512,512]{1,0:T(8,128)(2,1)S(1)} %convolution_convert_fusion), channel_id=1, source_target_pairs={{0,8},{1,9},{2,10},{3,11},{8,0},{9,1},{10,2},{11,3},{4,12},{5,13},... | collective-permute-start | bytes 1572872 | tf_op jit(solution)/shard_map/ppermute | solution.py:144
  27.1 4.6 %copy-start.5 = (bf16[512,4096]{1,0:T(8,128)(2,1)}, bf16[512,4096]{1,0:T(8,128)(2,1)S(1)}, u32[]{:S(2)}) copy-start(bf16[512,4096]{1,0:T(8,128)(2,1)S(1)} %collective-permute-done.x_ref) | copy-start | bytes 12582916
  36.2 1.0 copy-start.7
  41.9 33.8 %all-to-all-start = ((bf16[4,1024,256]{2,1,0:T(8,128)(2,1)}), bf16[4,1024,256]{2,1,0:T(8,128)(2,1)S(1)}, u32[]{:S(2)}, u32[]{:S(2)}) async-start(bf16[4,1024,256]{2,1,0:T(8,128)(2,1)} %bitcast.55), calls=%async_computation | async-start | bytes 4194304 | tf_op jit(solution)/shard_map/all_to_all | solution.py:158
  47.7 14.7 %collective-permute-start.4 = (bf16[16,64,256]{2,1,0:T(8,128)(2,1)S(1)}, bf16[16,64,256]{2,1,0:T(8,128)(2,1)S(1)}, u32[]{:S(2)}, u32[]{:S(2)}) collective-permute-start(bf16[16,64,256]{2,1,0:T(8,128)(2,1)S(1)} %bitcast.64), channel_id=1, source_target_pairs={{0,16},{1,17},{2,18},{3,19},{8,24},{9,25},{10,26},{11,27},{4,20},{... | collective-permute-start | bytes 1572872 | tf_op jit(solution)/shard_map/ppermute | solution.py:144
  49.0 23.2 %collective-permute-start.3 = (bf16[16,64,256]{2,1,0:T(8,128)(2,1)S(1)}, bf16[16,64,256]{2,1,0:T(8,128)(2,1)S(1)}, u32[]{:S(2)}, u32[]{:S(2)}) collective-permute-start(bf16[16,64,256]{2,1,0:T(8,128)(2,1)S(1)} %bitcast.63), channel_id=1, source_target_pairs={{0,20},{1,21},{2,22},{3,23},{8,28},{9,29},{10,30},{11,31},{4,0},{5... | collective-permute-start | bytes 1572872 | tf_op jit(solution)/shard_map/ppermute | solution.py:144
  49.5 24.9 %collective-permute-start.2 = (bf16[16,64,256]{2,1,0:T(8,128)(2,1)S(1)}, bf16[16,64,256]{2,1,0:T(8,128)(2,1)S(1)}, u32[]{:S(2)}, u32[]{:S(2)}) collective-permute-start(bf16[16,64,256]{2,1,0:T(8,128)(2,1)S(1)} %bitcast.62), channel_id=1, source_target_pairs={{0,4},{1,5},{2,6},{3,7},{8,12},{9,13},{10,14},{11,15},{4,16},{5,17... | collective-permute-start | bytes 1572872 | tf_op jit(solution)/shard_map/ppermute | solution.py:144
  75.6 29.2 %copy-start.8 = (f32[64,512]{1,0:T(8,128)S(1)}, f32[64,512]{1,0:T(8,128)}, u32[]{:S(2)}) copy-start(f32[64,512]{1,0:T(8,128)} %param.10) | copy-start | bytes 393220
  75.6 29.2 %copy-start.9 = (f32[64,512]{1,0:T(8,128)S(1)}, f32[64,512]{1,0:T(8,128)}, u32[]{:S(2)}) copy-start(f32[64,512]{1,0:T(8,128)} %param.11) | copy-start | bytes 393220
  76.7 15.2 %all-to-all-start.1 = ((bf16[4,256,256]{2,1,0:T(8,128)(2,1)}), bf16[4,256,256]{2,1,0:T(8,128)(2,1)S(1)}, u32[]{:S(2)}, u32[]{:S(2)}) async-start(bf16[4,256,256]{2,1,0:T(8,128)(2,1)} %bitcast.56), calls=%async_computation.1 | async-start | bytes 1048576 | tf_op jit(solution)/shard_map/all_to_all | solution.py:158
  82.0 5.8 %collective-permute-start.7 = (bf16[4,64,256]{2,1,0:T(8,128)(2,1)S(1)}, bf16[4,64,256]{2,1,0:T(8,128)(2,1)S(1)}, u32[]{:S(2)}, u32[]{:S(2)}) collective-permute-start(bf16[4,64,256]{2,1,0:T(8,128)(2,1)S(1)} %get-tuple-element.32), channel_id=1, source_target_pairs={{0,16},{1,17},{2,18},{3,19},{8,24},{9,25},{10,26},{11,27},{4,20},{... | collective-permute-start | bytes 393224 | tf_op jit(solution)/shard_map/ppermute | solution.py:144
  83.3 6.2 %collective-permute-start.6 = (bf16[4,64,256]{2,1,0:T(8,128)(2,1)S(1)}, bf16[4,64,256]{2,1,0:T(8,128)(2,1)S(1)}, u32[]{:S(2)}, u32[]{:S(2)}) collective-permute-start(bf16[4,64,256]{2,1,0:T(8,128)(2,1)S(1)} %get-tuple-element.33), channel_id=1, source_target_pairs={{0,20},{1,21},{2,22},{3,23},{8,28},{9,29},{10,30},{11,31},{4,0},{5... | collective-permute-start | bytes 393224 | tf_op jit(solution)/shard_map/ppermute | solution.py:144
  83.7 7.2 %collective-permute-start.5 = (bf16[4,64,256]{2,1,0:T(8,128)(2,1)S(1)}, bf16[4,64,256]{2,1,0:T(8,128)(2,1)S(1)}, u32[]{:S(2)}, u32[]{:S(2)}) collective-permute-start(bf16[4,64,256]{2,1,0:T(8,128)(2,1)S(1)} %get-tuple-element.31), channel_id=1, source_target_pairs={{0,4},{1,5},{2,6},{3,7},{8,12},{9,13},{10,14},{11,15},{4,16},{5,17... | collective-permute-start | bytes 393224 | tf_op jit(solution)/shard_map/ppermute | solution.py:144
  106.4 29.2 %all-to-all-start.3 = ((bf16[8,64,512]{2,1,0:T(8,128)(2,1)}), bf16[8,64,512]{2,1,0:T(8,128)(2,1)}, u32[]{:S(2)}, u32[]{:S(2)}) async-start(bf16[8,64,512]{2,1,0:T(8,128)(2,1)} %broadcast_in_dim.2), calls=%async_computation.3 | async-start | bytes 1048576 | tf_op jit(solution)/shard_map/all_to_all | solution.py:158
  115.2 12.1 %copy-start.2 = (bf16[512,4096]{1,0:T(8,128)(2,1)S(1)}, bf16[512,4096]{1,0:T(8,128)(2,1)}, u32[]{:S(2)}) copy-start(bf16[512,4096]{1,0:T(8,128)(2,1)} %copy-done.1) | copy-start | bytes 12582916
  126.6 15.4 %collective-permute-start.9 = (f32[512,1024]{1,0:T(8,128)}, f32[512,1024]{1,0:T(8,128)}, u32[]{:S(2)}, u32[]{:S(2)}) collective-permute-start(f32[512,1024]{1,0:T(8,128)} %get-tuple-element.18), channel_id=1, source_target_pairs={{0,8},{1,9},{2,10},{3,11},{8,0},{9,1},{10,2},{11,3},{4,12},{5,13},... | collective-permute-start | bytes 6291464 | tf_op jit(solution)/shard_map/ppermute | solution.py:144
  135.7 3.7 %copy-start.4 = (bf16[1024,1024]{1,0:T(8,128)(2,1)S(1)}, bf16[1024,1024]{1,0:T(8,128)(2,1)}, u32[]{:S(2)}) copy-start(bf16[1024,1024]{1,0:T(8,128)(2,1)} %param.8) | copy-start | bytes 6291460
  135.7 2.3 %collective-permute-start.10 = (bf16[8,64,512]{2,1,0:T(8,128)(2,1)}, bf16[8,64,512]{2,1,0:T(8,128)(2,1)}, u32[]{:S(2)}, u32[]{:S(2)}) collective-permute-start(bf16[8,64,512]{2,1,0:T(8,128)(2,1)} %get-tuple-element.19), channel_id=1, source_target_pairs={{0,8},{1,9},{2,10},{3,11},{8,0},{9,1},{10,2},{11,3},{4,12},{5,13},... | collective-permute-start | bytes 1572872 | tf_op jit(solution)/shard_map/ppermute | solution.py:144
  139.4 2.6 %copy-start.6 = (f32[512,1024]{1,0:T(8,128)S(1)}, f32[512,1024]{1,0:T(8,128)}, u32[]{:S(2)}) copy-start(f32[512,1024]{1,0:T(8,128)} %get-tuple-element.17) | copy-start | bytes 6291460
Sparse Core Ops, SparseCore 0:
  10.7 51.4 all-gather.2
  63.8 51.3 all-gather.4

commit v3 on v2

--- a/solution.py
+++ b/solution.py
@@ -47,18 +47,18 @@
             out_specs=[spec, spec],
         ),
         out_shape=[out, out],
-        compiler_params=pltpu.CompilerParams(vmem_limit_bytes=VMEM),
+        compiler_params=pltpu.CompilerParams(vmem_limit_bytes=60 * 1024 * 1024),
         cost_estimate=pl.CostEstimate(flops=1, bytes_accessed=1, transcendentals=0),
         name="pack_columns",
     )(place, tokens)
 
 
-def pack_rows(place, weight):
+def pack_rows(place, weight, after):
     chips, _, rows, features = weight.shape
     steps = 2
     block = chips // steps
 
-    def body(place_ref, w_ref, o_ref):
+    def body(place_ref, w_ref, after_ref, o_ref):
         o_ref[...] = w_ref[:, place_ref[0]]
 
     return pl.pallas_call(
@@ -66,56 +66,61 @@
         grid_spec=pltpu.PrefetchScalarGridSpec(
             num_scalar_prefetch=1,
             grid=(steps,),
-            in_specs=[pl.BlockSpec((block, 2, rows, features), lambda i, c: (i, 0, 0, 0))],
+            in_specs=[
+                pl.BlockSpec((block, 2, rows, features), lambda i, c: (i, 0, 0, 0)),
+                pl.BlockSpec(memory_space=pl.ANY),
+            ],
             out_specs=pl.BlockSpec((block, rows, features), lambda i, c: (i, 0, 0)),
         ),
         out_shape=jax.ShapeDtypeStruct((chips, rows, features), weight.dtype),
         compiler_params=pltpu.CompilerParams(vmem_limit_bytes=VMEM),
         cost_estimate=pl.CostEstimate(flops=1, bytes_accessed=1, transcendentals=0),
         name="pack_rows",
-    )(place, weight)
-
-
-def keys_of(packed, place, near, far):
-    _, _, part, features = near.shape
-    count = LO * X
-    tokens = packed.shape[0]
-    depth = count * 4 * part
+    )(place, weight, after)
+
+
+def keys_of(packed, shards, pieces):
+    rows, features = pieces[0].shape
+    count, many = len(pieces), len(packed)
+    part = rows // 4
+    tokens, depth = packed[0].shape
     wide = features // 4
 
-    def body(place_ref, x_ref, near_ref, far_ref, o_ref, rows_ref, x_now, sems):
-        copies = [pltpu.make_async_copy(x_ref, x_now, sems.at[count])]
-        for lo, ref in enumerate((near_ref, far_ref)):
-            for x in range(X):
-                at = lax.rem(place_ref[1] + lo, LO) * X + x
-                copies.append(pltpu.make_async_copy(ref.at[x], rows_ref.at[:, at], sems.at[lo * X + x]))
+    def body(shard_ref, *refs):
+        ins, outs = refs[: many + count], refs[many + count : 2 * many + count]
+        rows_ref, packed_ref, sems = refs[-3:]
+        copies = [
+            pltpu.make_async_copy(ins[many + k], rows_ref.at[:, shard_ref[k]], sems.at[many + k]) for k in range(count)
+        ]
+        copies = [pltpu.make_async_copy(ins[i], packed_ref.at[i], sems.at[i]) for i in range(many)] + copies
         for copy in copies:
             copy.start()
         for copy in copies:
             copy.wait()
-        for n in range(4):
-            columns = slice(n * wide, (n + 1) * wide)
-            block = rows_ref[:, :, :, columns].reshape(depth, wide)
-            o_ref[:, columns] = jnp.dot(x_now[...], block, preferred_element_type=jnp.float32)
-
-    out, joined = pl.pallas_call(
+        for i in range(many):
+            for n in range(4):
+                columns = slice(n * wide, (n + 1) * wide)
+                block = rows_ref[:, :, :, columns].reshape(depth, wide)
+                outs[i][:, columns] = jnp.dot(packed_ref[i], block, preferred_element_type=jnp.float32)
+
+    return pl.pallas_call(
         body,
         grid_spec=pltpu.PrefetchScalarGridSpec(
             num_scalar_prefetch=1,
             grid=(),
-            in_specs=[pl.BlockSpec(memory_space=pl.ANY)] * 3,
-            out_specs=[pl.BlockSpec(memory_space=pltpu.VMEM)] * 2,
-            scratch_shapes=[pltpu.VMEM(packed.shape, packed.dtype), pltpu.SemaphoreType.DMA((count + 1,))],
+            in_specs=[pl.BlockSpec(memory_space=pl.ANY)] * (many + count),
+            out_specs=[pl.BlockSpec(memory_space=pltpu.VMEM)] * many,
+            scratch_shapes=[
+                pltpu.VMEM((4, count, part, features), jnp.bfloat16),
+                pltpu.VMEM((many, tokens, depth), jnp.bfloat16),
+                pltpu.SemaphoreType.DMA((many + count,)),
+            ],
         ),
-        out_shape=[
-            jax.ShapeDtypeStruct((tokens, features), jnp.float32),
-            jax.ShapeDtypeStruct((4, count, part, features), jnp.bfloat16),
-        ],
+        out_shape=[jax.ShapeDtypeStruct((tokens, features), jnp.float32)] * many,
         compiler_params=pltpu.CompilerParams(vmem_limit_bytes=VMEM),
         cost_estimate=pl.CostEstimate(flops=1, bytes_accessed=1, transcendentals=0),
         name="keys_of",
-    )(place, packed, near, far)
-    return out, joined.reshape(depth, features)
+    )(shards, *packed, *[piece.reshape(4, part, features) for piece in pieces])
 
 
 def together(*arrays, after=()):
@@ -161,7 +166,7 @@
 def local(tokens, cotangent, weight, basis, exp_avg, exp_avg_sq):
     core = lax.axis_index("dp") % 2
     shard = lax.axis_index("fsdp")
-    my_lo = shard // X
+    my_x, my_lo = shard % X, shard // X
     my_z = lax.axis_index("dp") // 2 % 2 * 2 + my_lo
     features = weight.shape[1]
     chips = lax.axis_size("dp") // CORE
@@ -174,7 +179,7 @@
         for z in range(2)
         for c in range(2)
     ]
-    place = jnp.stack([core, my_lo])
+    place = core.reshape(1)
 
     def wide(array):
         return array.astype(jnp.float32)
@@ -184,9 +189,10 @@
     low = jnp.dot(cotangent, basis, preferred_element_type=jnp.float32).astype(jnp.bfloat16)
     low_other = move(low, core=1)
 
-    half = pack_rows(place, weight.reshape(chips, CORE, ROWS, features)).reshape(-1, features)
-    near = lax.all_gather(half, AXES, axis=0, tiled=True, axis_index_groups=along_x)
-    far = move_apart(half, z=-1)
+    half = pack_rows(place, weight.reshape(chips, CORE, ROWS, features), own).reshape(-1, features)
+    w_up = move(half, x=-1)
+    w_down = move(half, x=1)
+    w_z = move_apart(half, z=-1)
 
     contract = (((0,), (0,)), ((), ()))
     partial = lax.dot_general(own, low, contract, preferred_element_type=jnp.float32)
@@ -199,27 +205,33 @@
             total = total + wide(spread[i])
         return total
 
-    (far,) = together(far, after=(partial,))
-    far = lax.all_gather(far, AXES, axis=0, tiled=True, axis_index_groups=along_x)
-
-    def sum_z(parts):
-        def take(step):
-            z = (my_z + step) % 4
-            some = lax.dynamic_slice_in_dim(parts, z % 2, 1, axis=-5)
-            some = lax.dynamic_slice_in_dim(some, z // 2, 1, axis=-3)
-            return some.reshape(-1, ROWS, parts.shape[-1])
-
-        total = wide(take(0))
-        for step in (1, 3, 2):
-            total = total + wide(move(take(step), z=step))
+    def take(parts, step):
+        z = (my_z + step) % 4
+        some = lax.dynamic_slice_in_dim(parts, z % 2, 1, axis=-5)
+        some = lax.dynamic_slice_in_dim(some, z // 2, 1, axis=-3)
+        return some.reshape(-1, ROWS, parts.shape[-1])
+
+    def sum_z(own_part, others):
+        total = wide(own_part)
+        for step, part in others:
+            total = total + wide(move(part, z=step))
         return total.astype(jnp.bfloat16)
 
     first = partial[:, : rank // 2].reshape(4, -1, rank // 2)
     first = sum_all(exchange(first, along_y)).astype(jnp.bfloat16)
-    second = sum_z(partial[:, rank // 2 :].reshape(4, LO, X, 2, ROWS, rank // 2))
-    first, second = together(first, second)
+    second = partial[:, rank // 2 :].reshape(4, LO, X, 2, ROWS, rank // 2)
+    others = [(step, take(second, step)) for step in (1, 3, 2)]
+    second = sum_z(take(second, 0), others)
+    w_up, w_down, w_z = together(w_up, w_down, w_z, after=[part for _, part in others])
+    zx_up = move(w_z, x=-1)
+    zx_down = move(w_z, x=1)
+    w_far = move_apart(jnp.where(core == 0, w_up, w_down), x=-1)
     second = sum_all(exchange(second.reshape(4, X * ROWS, rank // 2), along_y)).astype(jnp.bfloat16)
-    first = sum_z(first.reshape(LO, X, 2, ROWS, rank // 2))
+    first = first.reshape(LO, X, 2, ROWS, rank // 2)
+    others = [(step, take(first, step)) for step in (1, 3, 2)]
+    first = sum_z(take(first, 0), others)
+    w_far, zx_up, zx_down = together(w_far, zx_up, zx_down, after=[part for _, part in others])
+    zx_far = move_apart(w_far, z=-1)
     both = jnp.concatenate([first.reshape(X, ROWS, -1), second.reshape(X, ROWS, -1)], axis=2)
     projected = sum_all(exchange(both, along_x))
     new_avg = 0.9 * exp_avg + 0.1 * projected
@@ -228,14 +240,14 @@
     second_fix = 1.0 - 0.999**STEP
     direction = new_avg / first_fix / (jnp.sqrt(new_sq / second_fix) + 1e-08)
     direction = direction.astype(jnp.bfloat16)
-    near, far = (rows.reshape(X, 4, 2 * ROWS, features) for rows in (near, far))
-    for_other, rows = keys_of(other, place, near, far)
-    own_keys = jnp.dot(own, rows, preferred_element_type=jnp.float32)
-
+    (zx_far,) = together(zx_far, after=(direction,))
+    steps = [(0, 0), (0, 1), (0, 3), (1, 0), (1, 1), (1, 3), (0, 2), (1, 2)]
+    shards = jnp.stack([(my_lo + lo) % LO * X + (my_x + x) % X for lo, x in steps])
+    for_other, own_keys = keys_of([other, own], shards, [half, w_up, w_down, w_z, zx_up, zx_down, w_far, zx_far])
     mine = exchange(jnp.broadcast_to(direction[None], (chips, ROWS, rank)), same_shard)
-    mine, own_keys = together(mine, own_keys)
     theirs = move(mine, core=1)
-    from_other = move(for_other, core=1)
+    (for_other,) = together(for_other, after=(mine,))
+    keys = (own_keys + move(for_other, core=1)).astype(jnp.bfloat16)
     even = jnp.where(core == 0, mine, theirs)
     odd = jnp.where(core == 0, theirs, mine)
     update = lax.dot_general(
@@ -245,7 +257,6 @@
         preferred_element_type=jnp.float32,
     )
     new_weight = (wide(weight) - learn_rate * galore_scale * update).astype(jnp.bfloat16)
-    keys = (own_keys + from_other).astype(jnp.bfloat16)
     return (keys, new_weight, new_avg, new_sq)
 
 

time: 152 us -> 136 us (0.89)
  between operations: 14.2 us -> 1.21 us
  starting transfers between devices: 26 us -> 36 us
  matrix products: 18.7 us -> 9.7 us
  waiting for transfers between devices: 40.1 us -> 32.8 us
  other arithmetic: 8.5 us -> 13.8 us
  Pallas kernels: 20.4 us -> 25.3 us
  blocking collectives: 12.8 us -> 7.92 us
  local copies, waits for them, and re-layouts: 11 us -> 8.99 us
    ppermute x10 -> x14, starting transfers between devices: 10.2 us -> 19.6 us  [move(): lax.ppermute(array, AXES, [(device(*at), device(at[0] + x, at[1] + y, at[...]
    dot_general x1 -> x0, matrix products: 8.3 us -> none  [local(): own_keys = jnp.dot(own, rows, preferred_element_type=jnp.float32)]
    all_to_all x1, blocking collectives: 12.8 us -> 7.92 us  [exchange(): lax.all_to_all(array, AXES, split_axis=0, concat_axis=0, axis_index_group...]
    pallas_call x1, Pallas kernels: 11.3 us -> 16 us  [keys_of(): pl.pallas_call(body, grid_spec=pltpu.PrefetchScalarGridSpec(num_scalar_pr...]
    ppermute x1 -> x3, waiting for transfers between devices: 4.46 us -> 0.01 us  [move_apart(): return lax.ppermute(array, AXES, pairs)]
    all_to_all x3, waiting for transfers between devices: 0.01 us -> 3.32 us  [exchange(): lax.all_to_all(array, AXES, split_axis=0, concat_axis=0, axis_index_group...]
    all_gather x2 -> x0, waiting for transfers between devices: 3.22 us -> none  [the longest x1 3.21 us: local(): lax.all_gather(far, AXES, axis=0, tiled=True, axis_index_groups=along_x)]
    ppermute x10 -> x14, waiting for transfers between devices: 32.4 us -> 29.5 us  [move(): lax.ppermute(array, AXES, [(device(*at), device(at[0] + x, at[1] + y, at[...]
  transfers between devices with their start and end apart: 16 -> 20, of which waited for: 10 -> 4; matrix products, arithmetic and copies ran while one was open for 21% -> 21% of each run, Pallas kernels for 12% -> 13%
where the time goes in v3:
time: 136 us
  starting transfers between devices  36 us (26%)
  waiting for transfers between devices  32.8 us (24%)
  Pallas kernels  25.3 us (19%)
  other arithmetic  13.8 us (10%)
  matrix products  9.7 us (7%)
  local copies, waits for them, and re-layouts  8.99 us (7%)
  blocking collectives  7.92 us (6%)
    ppermute x14, waiting for transfers between devices, move(): lax.ppermute(array, AXES, [(device(*at), device(at[0] + x, at[1] + y, at[...  29.5 us
    ppermute x14, starting transfers between devices, move(): lax.ppermute(array, AXES, [(device(*at), device(at[0] + x, at[1] + y, at[...  19.6 us
    pallas_call x1, Pallas kernels, keys_of(): pl.pallas_call(body, grid_spec=pltpu.PrefetchScalarGridSpec(num_scalar_pr...  16 us
    all_to_all x3, starting transfers between devices, exchange(): lax.all_to_all(array, AXES, split_axis=0, concat_axis=0, axis_index_group...  13.8 us
    pallas_call x1, Pallas kernels, pack_columns(): pl.pallas_call(body, grid_spec=pltpu.PrefetchScalarGridSpec(num_scalar_pr...  8.29 us
    all_to_all x1, blocking collectives, exchange(): lax.all_to_all(array, AXES, split_axis=0, concat_axis=0, axis_index_group...  7.92 us
    convert_element_type x2, other arithmetic, sum_z(): return total.astype(jnp.bfloat16)  3.85 us
    all_to_all x3, waiting for transfers between devices, exchange(): lax.all_to_all(array, AXES, split_axis=0, concat_axis=0, axis_index_group...  3.32 us
  transfers between devices with their start and end apart: 20, of which 4 were waited for; matrix products, arithmetic and copies ran while one was open for 21% of the time, Pallas kernels for 13%

profile of v3, /device:TPU:1, one launch (start us, length us, event | category | flops | bytes accessed | tf_op | source)
XLA Modules:
  0.0 135.7 jit_solution(4299634876475650600)
XLA Ops:
  0.7 8.3 %pack_columns.1 = (bf16[512,4096]{1,0:T(8,128)(2,1)}, bf16[512,4096]{1,0:T(8,128)(2,1)}) custom-call(s32[1]{0:T(128)} %bitcast.8.place_ref, bf16[512,8192]{1,0:T(8,128)(2,1)} %x_ref.1), custom_call_target="tpu_custom_call" | custom-call | flops 1 | bytes 1 | tf_op jit(solution)/shard_map/pack_columns/pallas_call | solution.py:41
  9.0 1.4 %collective-permute-start = (bf16[512,4096]{1,0:T(8,128)(2,1)}, bf16[512,4096]{1,0:T(8,128)(2,1)S(1)}, u32[]{:S(2)}, u32[]{:S(2)}) collective-permute-start(bf16[512,4096]{1,0:T(8,128)(2,1)} %get-tuple-element.14), channel_id=1, source_target_pairs={{0,8},{1,9},{2,10},{3,11},{8,0},{9,1},{10,2},{11,3},{4,12},{5,13},... | collective-permute-start | bytes 12582920 | tf_op jit(solution)/shard_map/ppermute | solution.py:149
  10.3 1.6 %copy-done.5 = bf16[1024,1024]{1,0:T(8,128)(2,1)S(1)} copy-done((bf16[1024,1024]{1,0:T(8,128)(2,1)S(1)}, bf16[1024,1024]{1,0:T(8,128)(2,1)}, u32[]{:S(2)}) %copy-start.5) | copy-done | bytes 2097176
  12.9 2.6 %collective-permute-start.1 = (bf16[512,1024]{1,0:T(8,128)(2,1)}, bf16[512,1024]{1,0:T(8,128)(2,1)S(1)}, u32[]{:S(2)}, u32[]{:S(2)}) collective-permute-start(bf16[512,1024]{1,0:T(8,128)(2,1)} %bitcast.11), channel_id=1, source_target_pairs={{0,3},{1,0},{2,1},{3,2},{8,11},{9,8},{10,9},{11,10},{4,7},{5,4},{6... | collective-permute-start | bytes 3145736 | tf_op jit(solution)/shard_map/ppermute | solution.py:149
  15.5 1.6 %collective-permute-start.3 = (bf16[512,1024]{1,0:T(8,128)(2,1)}, bf16[512,1024]{1,0:T(8,128)(2,1)}, u32[]{:S(2)}, u32[]{:S(2)}) collective-permute-start(bf16[512,1024]{1,0:T(8,128)(2,1)} %bitcast.11), channel_id=1, source_target_pairs={{0,20},{1,21},{2,22},{3,23},{8,12},{9,13},{10,14},{11,15},{4,0},{5... | collective-permute-start | bytes 3145736 | tf_op jit(solution)/shard_map/ppermute | solution.py:159
  17.1 1.9 %convolution_convert_fusion = bf16[512,512]{1,0:T(8,128)(2,1)S(1)} fusion(bf16[512,1024]{1,0:T(8,128)(2,1)} %param.7, bf16[1024,512]{1,0:T(8,128)(2,1)S(1)} %copy-done), kind=kOutput, calls=%fused_computation.3 | convolution fusion | flops 537133056 | bytes 2621440 | tf_op jit(solution)/shard_map/dot_general | solution.py:189
  19.1 2.8 %collective-permute-start.4 = (bf16[512,512]{1,0:T(8,128)(2,1)S(1)}, bf16[512,512]{1,0:T(8,128)(2,1)S(1)}, u32[]{:S(2)}, u32[]{:S(2)}) collective-permute-start(bf16[512,512]{1,0:T(8,128)(2,1)S(1)} %convolution_convert_fusion), channel_id=1, source_target_pairs={{0,8},{1,9},{2,10},{3,11},{8,0},{9,1},{10,2},{11,3},{4,12},{5,13},... | collective-permute-start | bytes 1572872 | tf_op jit(solution)/shard_map/ppermute | solution.py:149
  21.8 2.5 %fusion.11 = f32[4096,512]{1,0:T(8,128)S(1)} fusion(bf16[512,4096]{1,0:T(8,128)(2,1)S(1)} %copy-done.7, bf16[512,512]{1,0:T(8,128)(2,1)S(1)} %convolution_convert_fusion), kind=kOutput, calls=%fused_computation.33 | convolution fusion | flops 2147483648 | bytes 13107200 | tf_op jit(solution)/shard_map/dot_general | solution.py:198
  24.3 2.7 %add_convert_fusion = bf16[4096,512]{1,0:T(8,128)(2,1)S(1)} fusion(f32[4096,512]{1,0:T(8,128)S(1)} %fusion.11, bf16[512,4096]{1,0:T(8,128)(2,1)S(1)} %collective-permute-done.refs_0_, bf16[512,512]{1,0:T(8,128)(2,1)S(1)} %collective-permute-done.4), kind=kOutput, calls=%fused_computation | convolution fusion | flops 2151677952 | bytes 17301504 | tf_op jit(solution)/shard_map/dot_general | solution.py:199
  27.0 2.4 %fusion.10 = (bf16[4096,256]{1,0:T(8,128)(2,1)}, bf16[4096,256]{1,0:T(8,128)(2,1)}) fusion(bf16[4096,512]{1,0:T(8,128)(2,1)S(1)} %add_convert_fusion), kind=kLoop, calls=%fused_computation.32 | loop fusion | bytes 8388608 | tf_op jit(solution)/shard_map/slice | solution.py:220
  29.4 4.5 %all-to-all-start = ((bf16[4,1024,256]{2,1,0:T(8,128)(2,1)}), bf16[4,1024,256]{2,1,0:T(8,128)(2,1)}, u32[]{:S(2)}, u32[]{:S(2)}) async-start(bf16[4,1024,256]{2,1,0:T(8,128)(2,1)} %bitcast.73), calls=%async_computation | async-start | bytes 4194304 | tf_op jit(solution)/shard_map/all_to_all | solution.py:163
  34.1 2.9 %constant_dynamic-slice_fusion = (bf16[4,1,4,1,64,256]{5,4,3,2,1,0:T(8,128)(2,1)}, bf16[4,1,4,1,64,256]{5,4,3,2,1,0:T(8,128)(2,1)}, bf16[4,1,4,1,64,256]{5,4,3,2,1,0:T(8,128)(2,1)}, bf16[4,1,4,1,64,256]{5,4,3,2,1,0:T(8,128)(2,1)}) fusion(bf16[4,2,4,2,64,256]{5,4,3,2,1,0:T(8,128)(2,1)} %bitcast.72, s32[]{:T(128)S(6)} %select_n.235, s32[]{:T(128)S(6)} %select_n.238, ...), kind=kLoop, calls=%fused_computation.28 | loop fusion | bytes 4194336 | tf_op jit(solution)/shard_map/dynamic_slice | solution.py:211
  37.1 2.7 %collective-permute-start.13 = (bf16[16,64,256]{2,1,0:T(8,128)(2,1)}, bf16[16,64,256]{2,1,0:T(8,128)(2,1)}, u32[]{:S(2)}, u32[]{:S(2)}) collective-permute-start(bf16[16,64,256]{2,1,0:T(8,128)(2,1)} %bitcast.14.refs_4_), channel_id=1, source_target_pairs={{0,20},{1,21},{2,22},{3,23},{8,28},{9,29},{10,30},{11,31},{4,0},{5... | collective-permute-start | bytes 1572872 | tf_op jit(solution)/shard_map/ppermute | solution.py:149
  39.7 2.3 %collective-permute-start.14 = (bf16[16,64,256]{2,1,0:T(8,128)(2,1)}, bf16[16,64,256]{2,1,0:T(8,128)(2,1)}, u32[]{:S(2)}, u32[]{:S(2)}) collective-permute-start(bf16[16,64,256]{2,1,0:T(8,128)(2,1)} %bitcast.15.refs_5_), channel_id=1, source_target_pairs={{0,16},{1,17},{2,18},{3,19},{8,24},{9,25},{10,26},{11,27},{4,20},{... | collective-permute-start | bytes 1572872 | tf_op jit(solution)/shard_map/ppermute | solution.py:149
  43.0 2.3 %broadcast_select_fusion = bf16[512,1024]{1,0:T(8,128)(2,1)} fusion(bf16[512,1024]{1,0:T(8,128)(2,1)} %get-tuple-element.16, bf16[512,1024]{1,0:T(8,128)(2,1)} %get-tuple-element.17, pred[]{:T(512)S(6)} %eq.41), kind=kLoop, calls=%fused_computation.10 | loop fusion | flops 524288 | bytes 3145729 | tf_op jit(solution)/shard_map/jit(_where)/select_n | solution.py:228
  46.2 2.5 %collective-permute-start.6 = (bf16[512,1024]{1,0:T(8,128)(2,1)}, bf16[512,1024]{1,0:T(8,128)(2,1)}, u32[]{:S(2)}, u32[]{:S(2)}) collective-permute-start(bf16[512,1024]{1,0:T(8,128)(2,1)} %get-tuple-element.18), channel_id=1, source_target_pairs={{0,3},{1,0},{2,1},{3,2},{8,11},{9,8},{10,9},{11,10},{4,7},{5,4},{6... | collective-permute-start | bytes 3145736 | tf_op jit(solution)/shard_map/ppermute | solution.py:149
  48.7 14.6 %collective-permute-done.12 = bf16[16,64,256]{2,1,0:T(8,128)(2,1)} collective-permute-done((bf16[16,64,256]{2,1,0:T(8,128)(2,1)}, bf16[16,64,256]{2,1,0:T(8,128)(2,1)}, u32[]{:S(2)}, u32[]{:S(2)}) %collective-permute-start.12) | collective-permute-done | bytes 524320 | tf_op jit(solution)/shard_map/ppermute | solution.py:149
  63.8 2.7 %fusion.2 = bf16[16,64,256]{2,1,0:T(8,128)(2,1)} fusion(bf16[16,64,256]{2,1,0:T(8,128)(2,1)} %collective-permute-done.14, bf16[16,64,256]{2,1,0:T(8,128)(2,1)} %collective-permute-done.13, bf16[16,64,256]{2,1,0:T(8,128)(2,1)} %collective-permute-done.12, bf16[4,1,4,1,64,256]{5,4,3,2,1,0:T(8,128)(2,1)} %get-tuple-element.29), kind=kLoop, calls=%fused_computation.8 | loop fusion | flops 2097152 | bytes 2621440 | tf_op jit(solution)/shard_map/convert_element_type | solution.py:218
  66.5 4.1 %all-to-all-start.1 = ((bf16[4,256,256]{2,1,0:T(8,128)(2,1)}), bf16[4,256,256]{2,1,0:T(8,128)(2,1)S(1)}, u32[]{:S(2)}, u32[]{:S(2)}) async-start(bf16[4,256,256]{2,1,0:T(8,128)(2,1)} %bitcast.29), calls=%async_computation.1 | async-start | bytes 1048576 | tf_op jit(solution)/shard_map/all_to_all | solution.py:163
  70.7 1.8 %add_convert_fusion.2 = bf16[1,1024,256]{2,1,0:T(8,128)(2,1)S(1)} fusion(bf16[4,1024,256]{2,1,0:T(8,128)(2,1)} %all-to-all-done), kind=kLoop, calls=%fused_computation.9 | loop fusion | flops 2097152 | bytes 2621440 | tf_op jit(solution)/shard_map/convert.3
  72.5 1.9 %collective-permute-start.10 = (bf16[4,64,256]{2,1,0:T(8,128)(2,1)S(1)}, bf16[4,64,256]{2,1,0:T(8,128)(2,1)}, u32[]{:S(2)}, u32[]{:S(2)}) collective-permute-start(bf16[4,64,256]{2,1,0:T(8,128)(2,1)S(1)} %get-tuple-element.36.refs_4_), channel_id=1, source_target_pairs={{0,20},{1,21},{2,22},{3,23},{8,28},{9,29},{10,30},{11,31},{4,0},{5... | collective-permute-start | bytes 393224 | tf_op jit(solution)/shard_map/ppermute | solution.py:149
  75.1 3.3 %all-to-all-done.1 = bf16[4,256,256]{2,1,0:T(8,128)(2,1)S(1)} async-done(((bf16[4,256,256]{2,1,0:T(8,128)(2,1)}), bf16[4,256,256]{2,1,0:T(8,128)(2,1)S(1)}, u32[]{:S(2)}, u32[]{:S(2)}) %all-to-all-start.1) | async-done | bytes 524320 | tf_op jit(solution)/shard_map/all_to_all | solution.py:163
  79.2 10.2 %collective-permute-done.7.refs_2_ = bf16[512,1024]{1,0:T(8,128)(2,1)} collective-permute-done((bf16[512,1024]{1,0:T(8,128)(2,1)}, bf16[512,1024]{1,0:T(8,128)(2,1)}, u32[]{:S(2)}, u32[]{:S(2)}) %collective-permute-start.7) | collective-permute-done | bytes 1048608 | tf_op jit(solution)/shard_map/ppermute | solution.py:149
  89.5 1.2 fusion.5
  91.6 7.9 %all_to_all.20 = bf16[4,64,512]{2,1,0:T(8,128)(2,1)S(1)} all-to-all(bf16[4,64,512]{2,1,0:T(8,128)(2,1)S(1)} %pad_maximum_fusion.1), channel_id=1, replica_groups={{0,1,2,3},{8,9,10,11},{4,5,6,7},{12,13,14,15},{16,17,18,19},{24,25,26,2..., dimensions={0} | all-to-all | bytes 524288 | tf_op jit(solution)/shard_map/all_to_all | solution.py:163
  99.5 1.8 %divide_convert_fusion = (bf16[64,512]{1,0:T(8,128)(2,1)S(1)}, f32[64,512]{1,0:T(8,128)}, f32[64,512]{1,0:T(8,128)}) fusion(bf16[4,64,512]{2,1,0:T(8,128)(2,1)S(1)} %all_to_all.20, f32[64,512]{1,0:T(8,128)} %param.10, f32[64,512]{1,0:T(8,128)} %param.11), kind=kLoop, calls=%fused_computation.23 | loop fusion | flops 622592 | bytes 851968 | tf_op jit(solution)/shard_map/convert_element_type | solution.py:242
  102.1 5.2 %all-to-all-start.3 = ((bf16[8,64,512]{2,1,0:T(8,128)(2,1)}), bf16[8,64,512]{2,1,0:T(8,128)(2,1)}, u32[]{:S(2)}, u32[]{:S(2)}) async-start(bf16[8,64,512]{2,1,0:T(8,128)(2,1)} %broadcast_in_dim.2), calls=%async_computation.3 | async-start | bytes 1048576 | tf_op jit(solution)/shard_map/all_to_all | solution.py:163
  107.5 16.0 %keys_of.1 = (f32[512,1024]{1,0:T(8,128)}, f32[512,1024]{1,0:T(8,128)}) custom-call(s32[8]{0:T(128)S(1)} %stack.44.shard_ref, bf16[512,4096]{1,0:T(8,128)(2,1)} %copy-done.8, bf16[512,4096]{1,0:T(8,128)(2,1)} %get-tuple-element.15.after_ref.refs_1_, bf16[4,128,1024]{2,1,0:T(8,128)(2,1)} %bitcast.10.refs_2_, bf16[4,128,1024]{2,1,0:T(8,128)(2,1)S(1)} %bitcast.69, ...), custom_call_target="tpu_custom_call" | custom-call | flops 1 | bytes 1 | tf_op jit(solution)/shard_map/keys_of/pallas_call | solution.py:106
  123.5 2.3 %collective-permute-start.15 = (f32[512,1024]{1,0:T(8,128)}, f32[512,1024]{1,0:T(8,128)S(1)}, u32[]{:S(2)}, u32[]{:S(2)}) collective-permute-start(f32[512,1024]{1,0:T(8,128)} %together.7), channel_id=1, source_target_pairs={{0,8},{1,9},{2,10},{3,11},{8,0},{9,1},{10,2},{11,3},{4,12},{5,13},... | collective-permute-start | bytes 6291464 | tf_op jit(solution)/shard_map/ppermute | solution.py:149
  125.8 4.7 %collective-permute-done.16 = bf16[8,64,512]{2,1,0:T(8,128)(2,1)S(1)} collective-permute-done((bf16[8,64,512]{2,1,0:T(8,128)(2,1)}, bf16[8,64,512]{2,1,0:T(8,128)(2,1)S(1)}, u32[]{:S(2)}, u32[]{:S(2)}) %collective-permute-start.16) | collective-permute-done | bytes 524320 | tf_op jit(solution)/shard_map/ppermute | solution.py:149
  131.8 2.6 %subtract_convert_fusion = bf16[1024,1024]{1,0:T(8,128)(2,1)} fusion(bf16[1024,1024]{1,0:T(8,128)(2,1)S(1)} %copy-done.6, bf16[1024,512]{1,0:T(8,128)(2,1)S(1)} %bitcast.77, bf16[1024,512]{1,0:T(8,128)(2,1)S(1)} %copy-done), kind=kOutput, calls=%fused_computation.1 | convolution fusion | flops 1077936128 | bytes 6291456 | tf_op jit(solution)/shard_map/dot_general | solution.py:253
  134.5 1.3 add_convert_fusion.1
  (68 shorter events, 8.3 us)
Async XLA Ops:
  0.6 16.5 %copy-start = (bf16[1024,512]{1,0:T(8,128)(2,1)S(1)}, bf16[1024,512]{1,0:T(8,128)(2,1)}, u32[]{:S(2)}) copy-start(bf16[1024,512]{1,0:T(8,128)(2,1)} %param.9) | copy-start | bytes 3145732
  9.0 15.4 %collective-permute-start = (bf16[512,4096]{1,0:T(8,128)(2,1)}, bf16[512,4096]{1,0:T(8,128)(2,1)S(1)}, u32[]{:S(2)}, u32[]{:S(2)}) collective-permute-start(bf16[512,4096]{1,0:T(8,128)(2,1)} %get-tuple-element.14), channel_id=1, source_target_pairs={{0,8},{1,9},{2,10},{3,11},{8,0},{9,1},{10,2},{11,3},{4,12},{5,13},... | collective-permute-start | bytes 12582920 | tf_op jit(solution)/shard_map/ppermute | solution.py:149
  11.9 9.9 %copy-start.7 = (bf16[512,4096]{1,0:T(8,128)(2,1)S(1)}, bf16[512,4096]{1,0:T(8,128)(2,1)}, u32[]{:S(2)}) copy-start(bf16[512,4096]{1,0:T(8,128)(2,1)} %get-tuple-element.15.after_ref.refs_1_) | copy-start | bytes 12582916
  12.9 26.8 %collective-permute-start.1 = (bf16[512,1024]{1,0:T(8,128)(2,1)}, bf16[512,1024]{1,0:T(8,128)(2,1)S(1)}, u32[]{:S(2)}, u32[]{:S(2)}) collective-permute-start(bf16[512,1024]{1,0:T(8,128)(2,1)} %bitcast.11), channel_id=1, source_target_pairs={{0,3},{1,0},{2,1},{3,2},{8,11},{9,8},{10,9},{11,10},{4,7},{5,4},{6... | collective-permute-start | bytes 3145736 | tf_op jit(solution)/shard_map/ppermute | solution.py:149
  15.5 26.5 %collective-permute-start.2 = (bf16[512,1024]{1,0:T(8,128)(2,1)}, bf16[512,1024]{1,0:T(8,128)(2,1)S(1)}, u32[]{:S(2)}, u32[]{:S(2)}) collective-permute-start(bf16[512,1024]{1,0:T(8,128)(2,1)} %bitcast.11), channel_id=1, source_target_pairs={{0,1},{1,2},{2,3},{3,0},{8,9},{9,10},{10,11},{11,8},{4,5},{5,6},{6... | collective-permute-start | bytes 3145736 | tf_op jit(solution)/shard_map/ppermute | solution.py:149
  15.5 26.5 %collective-permute-start.3 = (bf16[512,1024]{1,0:T(8,128)(2,1)}, bf16[512,1024]{1,0:T(8,128)(2,1)}, u32[]{:S(2)}, u32[]{:S(2)}) collective-permute-start(bf16[512,1024]{1,0:T(8,128)(2,1)} %bitcast.11), channel_id=1, source_target_pairs={{0,20},{1,21},{2,22},{3,23},{8,12},{9,13},{10,14},{11,15},{4,0},{5... | collective-permute-start | bytes 3145736 | tf_op jit(solution)/shard_map/ppermute | solution.py:159
  19.1 5.2 %collective-permute-start.4 = (bf16[512,512]{1,0:T(8,128)(2,1)S(1)}, bf16[512,512]{1,0:T(8,128)(2,1)S(1)}, u32[]{:S(2)}, u32[]{:S(2)}) collective-permute-start(bf16[512,512]{1,0:T(8,128)(2,1)S(1)} %convolution_convert_fusion), channel_id=1, source_target_pairs={{0,8},{1,9},{2,10},{3,11},{8,0},{9,1},{10,2},{11,3},{4,12},{5,13},... | collective-permute-start | bytes 1572872 | tf_op jit(solution)/shard_map/ppermute | solution.py:149
  24.3 2.7 %copy-start.8 = (bf16[512,4096]{1,0:T(8,128)(2,1)}, bf16[512,4096]{1,0:T(8,128)(2,1)S(1)}, u32[]{:S(2)}) copy-start(bf16[512,4096]{1,0:T(8,128)(2,1)S(1)} %collective-permute-done.refs_0_) | copy-start | bytes 12582916
  29.4 37.1 %all-to-all-start = ((bf16[4,1024,256]{2,1,0:T(8,128)(2,1)}), bf16[4,1024,256]{2,1,0:T(8,128)(2,1)}, u32[]{:S(2)}, u32[]{:S(2)}) async-start(bf16[4,1024,256]{2,1,0:T(8,128)(2,1)} %bitcast.73), calls=%async_computation | async-start | bytes 4194304 | tf_op jit(solution)/shard_map/all_to_all | solution.py:163
  37.1 26.3 %collective-permute-start.12 = (bf16[16,64,256]{2,1,0:T(8,128)(2,1)}, bf16[16,64,256]{2,1,0:T(8,128)(2,1)}, u32[]{:S(2)}, u32[]{:S(2)}) collective-permute-start(bf16[16,64,256]{2,1,0:T(8,128)(2,1)} %bitcast.13.refs_3_), channel_id=1, source_target_pairs={{0,4},{1,5},{2,6},{3,7},{8,12},{9,13},{10,14},{11,15},{4,16},{5,17... | collective-permute-start | bytes 1572872 | tf_op jit(solution)/shard_map/ppermute | solution.py:149
  37.1 26.8 %collective-permute-start.13 = (bf16[16,64,256]{2,1,0:T(8,128)(2,1)}, bf16[16,64,256]{2,1,0:T(8,128)(2,1)}, u32[]{:S(2)}, u32[]{:S(2)}) collective-permute-start(bf16[16,64,256]{2,1,0:T(8,128)(2,1)} %bitcast.14.refs_4_), channel_id=1, source_target_pairs={{0,20},{1,21},{2,22},{3,23},{8,28},{9,29},{10,30},{11,31},{4,0},{5... | collective-permute-start | bytes 1572872 | tf_op jit(solution)/shard_map/ppermute | solution.py:149
  39.7 24.1 %collective-permute-start.14 = (bf16[16,64,256]{2,1,0:T(8,128)(2,1)}, bf16[16,64,256]{2,1,0:T(8,128)(2,1)}, u32[]{:S(2)}, u32[]{:S(2)}) collective-permute-start(bf16[16,64,256]{2,1,0:T(8,128)(2,1)} %bitcast.15.refs_5_), channel_id=1, source_target_pairs={{0,16},{1,17},{2,18},{3,19},{8,24},{9,25},{10,26},{11,27},{4,20},{... | collective-permute-start | bytes 1572872 | tf_op jit(solution)/shard_map/ppermute | solution.py:149
  45.3 29.2 %collective-permute-start.5 = (bf16[512,1024]{1,0:T(8,128)(2,1)}, bf16[512,1024]{1,0:T(8,128)(2,1)S(1)}, u32[]{:S(2)}, u32[]{:S(2)}) collective-permute-start(bf16[512,1024]{1,0:T(8,128)(2,1)} %broadcast_select_fusion), channel_id=1, source_target_pairs={{0,3},{1,0},{2,1},{3,2},{8,9},{9,10},{10,11},{11,8},{4,7},{5,4},{6... | collective-permute-start | bytes 3145736 | tf_op jit(solution)/shard_map/ppermute | solution.py:159
  46.2 33.0 %collective-permute-start.6 = (bf16[512,1024]{1,0:T(8,128)(2,1)}, bf16[512,1024]{1,0:T(8,128)(2,1)}, u32[]{:S(2)}, u32[]{:S(2)}) collective-permute-start(bf16[512,1024]{1,0:T(8,128)(2,1)} %get-tuple-element.18), channel_id=1, source_target_pairs={{0,3},{1,0},{2,1},{3,2},{8,11},{9,8},{10,9},{11,10},{4,7},{5,4},{6... | collective-permute-start | bytes 3145736 | tf_op jit(solution)/shard_map/ppermute | solution.py:149
  63.4 26.0 %collective-permute-start.7 = (bf16[512,1024]{1,0:T(8,128)(2,1)}, bf16[512,1024]{1,0:T(8,128)(2,1)}, u32[]{:S(2)}, u32[]{:S(2)}) collective-permute-start(bf16[512,1024]{1,0:T(8,128)(2,1)} %get-tuple-element.18), channel_id=1, source_target_pairs={{0,1},{1,2},{2,3},{3,0},{8,9},{9,10},{10,11},{11,8},{4,5},{5,6},{6... | collective-permute-start | bytes 3145736 | tf_op jit(solution)/shard_map/ppermute | solution.py:149
  66.5 11.9 %all-to-all-start.1 = ((bf16[4,256,256]{2,1,0:T(8,128)(2,1)}), bf16[4,256,256]{2,1,0:T(8,128)(2,1)S(1)}, u32[]{:S(2)}, u32[]{:S(2)}) async-start(bf16[4,256,256]{2,1,0:T(8,128)(2,1)} %bitcast.29), calls=%async_computation.1 | async-start | bytes 1048576 | tf_op jit(solution)/shard_map/all_to_all | solution.py:163
  72.4 6.0 %copy-start.10 = (bf16[1,1024,256]{2,1,0:T(8,128)(2,1)}, bf16[1,1024,256]{2,1,0:T(8,128)(2,1)S(1)}, u32[]{:S(2)}) copy-start(bf16[1,1024,256]{2,1,0:T(8,128)(2,1)S(1)} %add_convert_fusion.2) | copy-start | bytes 1572868
  72.5 16.9 %copy-start.13 = (bf16[4,64,256]{2,1,0:T(8,128)(2,1)}, bf16[4,64,256]{2,1,0:T(8,128)(2,1)S(1)}, u32[]{:S(2)}) copy-start(bf16[4,64,256]{2,1,0:T(8,128)(2,1)S(1)} %get-tuple-element.37.refs_3_) | copy-start | bytes 393220
  72.5 16.9 %copy-start.14 = (bf16[4,64,256]{2,1,0:T(8,128)(2,1)}, bf16[4,64,256]{2,1,0:T(8,128)(2,1)S(1)}, u32[]{:S(2)}) copy-start(bf16[4,64,256]{2,1,0:T(8,128)(2,1)S(1)} %get-tuple-element.35.refs_5_) | copy-start | bytes 393220
  72.5 16.9 %copy-start.15 = (bf16[4,64,256]{2,1,0:T(8,128)(2,1)}, bf16[4,64,256]{2,1,0:T(8,128)(2,1)S(1)}, u32[]{:S(2)}) copy-start(bf16[4,64,256]{2,1,0:T(8,128)(2,1)S(1)} %get-tuple-element.36.refs_4_) | copy-start | bytes 393220
  72.5 16.9 %collective-permute-start.10 = (bf16[4,64,256]{2,1,0:T(8,128)(2,1)S(1)}, bf16[4,64,256]{2,1,0:T(8,128)(2,1)}, u32[]{:S(2)}, u32[]{:S(2)}) collective-permute-start(bf16[4,64,256]{2,1,0:T(8,128)(2,1)S(1)} %get-tuple-element.36.refs_4_), channel_id=1, source_target_pairs={{0,20},{1,21},{2,22},{3,23},{8,28},{9,29},{10,30},{11,31},{4,0},{5... | collective-permute-start | bytes 393224 | tf_op jit(solution)/shard_map/ppermute | solution.py:149
  74.5 15.0 %collective-permute-start.11 = (bf16[4,64,256]{2,1,0:T(8,128)(2,1)S(1)}, bf16[4,64,256]{2,1,0:T(8,128)(2,1)}, u32[]{:S(2)}, u32[]{:S(2)}) collective-permute-start(bf16[4,64,256]{2,1,0:T(8,128)(2,1)S(1)} %get-tuple-element.35.refs_5_), channel_id=1, source_target_pairs={{0,16},{1,17},{2,18},{3,19},{8,24},{9,25},{10,26},{11,27},{4,20},{... | collective-permute-start | bytes 393224 | tf_op jit(solution)/shard_map/ppermute | solution.py:149
  74.5 4.0 %copy-start.9 = (bf16[512,1024]{1,0:T(8,128)(2,1)}, bf16[512,1024]{1,0:T(8,128)(2,1)S(1)}, u32[]{:S(2)}) copy-start(bf16[512,1024]{1,0:T(8,128)(2,1)S(1)} %collective-permute-done.5.refs_0_) | copy-start | bytes 3145732
  74.5 15.0 %collective-permute-start.9 = (bf16[4,64,256]{2,1,0:T(8,128)(2,1)S(1)}, bf16[4,64,256]{2,1,0:T(8,128)(2,1)}, u32[]{:S(2)}, u32[]{:S(2)}) collective-permute-start(bf16[4,64,256]{2,1,0:T(8,128)(2,1)S(1)} %get-tuple-element.37.refs_3_), channel_id=1, source_target_pairs={{0,4},{1,5},{2,6},{3,7},{8,12},{9,13},{10,14},{11,15},{4,16},{5,17... | collective-permute-start | bytes 393224 | tf_op jit(solution)/shard_map/ppermute | solution.py:149
  79.2 28.3 %copy-start.2 = (bf16[512,1024]{1,0:T(8,128)(2,1)S(1)}, bf16[512,1024]{1,0:T(8,128)(2,1)}, u32[]{:S(2)}) copy-start(bf16[512,1024]{1,0:T(8,128)(2,1)} %get-tuple-element.16) | copy-start | bytes 3145732
  79.2 28.3 %copy-start.4 = (bf16[512,1024]{1,0:T(8,128)(2,1)S(1)}, bf16[512,1024]{1,0:T(8,128)(2,1)}, u32[]{:S(2)}) copy-start(bf16[512,1024]{1,0:T(8,128)(2,1)} %get-tuple-element.17) | copy-start | bytes 3145732
  89.4 18.1 %collective-permute-start.8 = (bf16[512,1024]{1,0:T(8,128)(2,1)}, bf16[512,1024]{1,0:T(8,128)(2,1)}, u32[]{:S(2)}, u32[]{:S(2)}) collective-permute-start(bf16[512,1024]{1,0:T(8,128)(2,1)} %get-tuple-element.21), channel_id=1, source_target_pairs={{0,20},{1,21},{2,22},{3,23},{8,12},{9,13},{10,14},{11,15},{4,0},{5... | collective-permute-start | bytes 3145736 | tf_op jit(solution)/shard_map/ppermute | solution.py:159
  101.3 6.1 %copy-start.12 = (bf16[64,512]{1,0:T(8,128)(2,1)}, bf16[64,512]{1,0:T(8,128)(2,1)S(1)}, u32[]{:S(2)}) copy-start(bf16[64,512]{1,0:T(8,128)(2,1)S(1)} %get-tuple-element.24.refs_1_) | copy-start | bytes 196612
  102.1 21.3 %all-to-all-start.3 = ((bf16[8,64,512]{2,1,0:T(8,128)(2,1)}), bf16[8,64,512]{2,1,0:T(8,128)(2,1)}, u32[]{:S(2)}, u32[]{:S(2)}) async-start(bf16[8,64,512]{2,1,0:T(8,128)(2,1)} %broadcast_in_dim.2), calls=%async_computation.3 | async-start | bytes 1048576 | tf_op jit(solution)/shard_map/all_to_all | solution.py:163
  123.5 8.3 %copy-start.6 = (bf16[1024,1024]{1,0:T(8,128)(2,1)S(1)}, bf16[1024,1024]{1,0:T(8,128)(2,1)}, u32[]{:S(2)}) copy-start(bf16[1024,1024]{1,0:T(8,128)(2,1)} %param.8) | copy-start | bytes 6291460
  123.5 11.0 %collective-permute-start.15 = (f32[512,1024]{1,0:T(8,128)}, f32[512,1024]{1,0:T(8,128)S(1)}, u32[]{:S(2)}, u32[]{:S(2)}) collective-permute-start(f32[512,1024]{1,0:T(8,128)} %together.7), channel_id=1, source_target_pairs={{0,8},{1,9},{2,10},{3,11},{8,0},{9,1},{10,2},{11,3},{4,12},{5,13},... | collective-permute-start | bytes 6291464 | tf_op jit(solution)/shard_map/ppermute | solution.py:149
  125.7 4.7 %collective-permute-start.16 = (bf16[8,64,512]{2,1,0:T(8,128)(2,1)}, bf16[8,64,512]{2,1,0:T(8,128)(2,1)S(1)}, u32[]{:S(2)}, u32[]{:S(2)}) collective-permute-start(bf16[8,64,512]{2,1,0:T(8,128)(2,1)} %all-to-all-done.3.refs_1_), channel_id=1, source_target_pairs={{0,8},{1,9},{2,10},{3,11},{8,0},{9,1},{10,2},{11,3},{4,12},{5,13},... | collective-permute-start | bytes 1572872 | tf_op jit(solution)/shard_map/ppermute | solution.py:149
  (4 other events, 7.5 us)

commit v4 on v3

--- a/solution.py
+++ b/solution.py
@@ -12,7 +12,7 @@
 galore_scale = 0.25
 
 ROWS = 64
-VMEM = 48 * 1024 * 1024
+VMEM = 60 * 1024 * 1024
 
 
 CORE, LO, X = 2, 2, 4
@@ -47,7 +47,7 @@
             out_specs=[spec, spec],
         ),
         out_shape=[out, out],
-        compiler_params=pltpu.CompilerParams(vmem_limit_bytes=60 * 1024 * 1024),
+        compiler_params=pltpu.CompilerParams(vmem_limit_bytes=VMEM),
         cost_estimate=pl.CostEstimate(flops=1, bytes_accessed=1, transcendentals=0),
         name="pack_columns",
     )(place, tokens)
@@ -79,48 +79,65 @@
     )(place, weight, after)
 
 
-def keys_of(packed, shards, pieces):
+def keys_of(packed, shards, pieces, addends=(), after=()):
     rows, features = pieces[0].shape
     count, many = len(pieces), len(packed)
     part = rows // 4
-    tokens, depth = packed[0].shape
+    tokens, width = packed[0].shape
+    every_shard = width // rows
+    depth = count * rows
     wide = features // 4
+    inputs = many + count + len(addends) + len(after)
 
     def body(shard_ref, *refs):
-        ins, outs = refs[: many + count], refs[many + count : 2 * many + count]
+        ins, plus, outs = refs[: many + count], refs[many + count :], refs[inputs : inputs + many]
         rows_ref, packed_ref, sems = refs[-3:]
-        copies = [
-            pltpu.make_async_copy(ins[many + k], rows_ref.at[:, shard_ref[k]], sems.at[many + k]) for k in range(count)
-        ]
-        copies = [pltpu.make_async_copy(ins[i], packed_ref.at[i], sems.at[i]) for i in range(many)] + copies
-        for copy in copies:
+        copies = [pltpu.make_async_copy(ins[many + k], rows_ref.at[:, k], sems.at[many, k]) for k in range(count)]
+        loads = []
+        for i in range(many):
+            loads.append([])
+            for y in range(4):
+                for k in range(count):
+                    at = pl.multiple_of((y * every_shard + shard_ref[k]) * part, part)
+                    to = packed_ref.at[i, :, pl.ds((y * count + k) * part, part)]
+                    loads[i].append(pltpu.make_async_copy(ins[i].at[:, pl.ds(at, part)], to, sems.at[i, y * count + k]))
+        for copy in copies + sum(loads, []):
             copy.start()
         for copy in copies:
             copy.wait()
         for i in range(many):
+            for copy in loads[i]:
+                copy.wait()
             for n in range(4):
                 columns = slice(n * wide, (n + 1) * wide)
                 block = rows_ref[:, :, :, columns].reshape(depth, wide)
-                outs[i][:, columns] = jnp.dot(packed_ref[i], block, preferred_element_type=jnp.float32)
+                product = jnp.dot(packed_ref[i], block, preferred_element_type=jnp.float32)
+                outs[i][:, columns] = product + plus[i][:, columns] if addends else product
 
     return pl.pallas_call(
         body,
         grid_spec=pltpu.PrefetchScalarGridSpec(
             num_scalar_prefetch=1,
             grid=(),
-            in_specs=[pl.BlockSpec(memory_space=pl.ANY)] * (many + count),
+            in_specs=[pl.BlockSpec(memory_space=pl.ANY)] * (many + count)
+            + [pl.BlockSpec(memory_space=pltpu.VMEM)] * len(addends)
+            + [pl.BlockSpec(memory_space=pl.ANY)] * len(after),
             out_specs=[pl.BlockSpec(memory_space=pltpu.VMEM)] * many,
             scratch_shapes=[
                 pltpu.VMEM((4, count, part, features), jnp.bfloat16),
                 pltpu.VMEM((many, tokens, depth), jnp.bfloat16),
-                pltpu.SemaphoreType.DMA((many + count,)),
+                pltpu.SemaphoreType.DMA((many + 1, 4 * count)),
             ],
         ),
         out_shape=[jax.ShapeDtypeStruct((tokens, features), jnp.float32)] * many,
         compiler_params=pltpu.CompilerParams(vmem_limit_bytes=VMEM),
-        cost_estimate=pl.CostEstimate(flops=1, bytes_accessed=1, transcendentals=0),
+        cost_estimate=pl.CostEstimate(
+            flops=1 if addends else 2 * many * tokens * depth * features,
+            bytes_accessed=1 if addends else 2 * depth * (many * tokens + features),
+            transcendentals=0,
+        ),
         name="keys_of",
-    )(shards, *packed, *[piece.reshape(4, part, features) for piece in pieces])
+    )(shards, *packed, *[piece.reshape(4, part, features) for piece in pieces], *addends, *after)
 
 
 def together(*arrays, after=()):
@@ -225,7 +242,11 @@
     w_up, w_down, w_z = together(w_up, w_down, w_z, after=[part for _, part in others])
     zx_up = move(w_z, x=-1)
     zx_down = move(w_z, x=1)
-    w_far = move_apart(jnp.where(core == 0, w_up, w_down), x=-1)
+    steps = [(0, 0), (0, 1), (0, 3), (1, 0), (1, 1), (1, 3), (0, 2), (1, 2)]
+    shards = jnp.stack([(my_lo + lo) % LO * X + (my_x + x) % X for lo, x in steps])
+    other_near, own_near = keys_of([other, own], shards[:4], [half, w_up, w_down, w_z])
+    second, w_far = together(second, jnp.where(core == 0, w_up, w_down), after=(own_near,))
+    w_far = move_apart(w_far, x=-1)
     second = sum_all(exchange(second.reshape(4, X * ROWS, rank // 2), along_y)).astype(jnp.bfloat16)
     first = first.reshape(LO, X, 2, ROWS, rank // 2)
     others = [(step, take(first, step)) for step in (1, 3, 2)]
@@ -240,10 +261,10 @@
     second_fix = 1.0 - 0.999**STEP
     direction = new_avg / first_fix / (jnp.sqrt(new_sq / second_fix) + 1e-08)
     direction = direction.astype(jnp.bfloat16)
-    (zx_far,) = together(zx_far, after=(direction,))
-    steps = [(0, 0), (0, 1), (0, 3), (1, 0), (1, 1), (1, 3), (0, 2), (1, 2)]
-    shards = jnp.stack([(my_lo + lo) % LO * X + (my_x + x) % X for lo, x in steps])
-    for_other, own_keys = keys_of([other, own], shards, [half, w_up, w_down, w_z, zx_up, zx_down, w_far, zx_far])
+    for_other, own_keys = keys_of(
+        [other, own], shards[4:], [zx_up, zx_down, w_far, zx_far], [other_near, own_near], (direction,)
+    )
+
     mine = exchange(jnp.broadcast_to(direction[None], (chips, ROWS, rank)), same_shard)
     theirs = move(mine, core=1)
     (for_other,) = together(for_other, after=(mine,))

time: 136 us -> 131 us (0.963)
  waiting for transfers between devices: 32.8 us -> 20.7 us
  Pallas kernels: 25.3 us -> 32.8 us
  starting transfers between devices: 36 us -> 32.3 us
  matrix products: 9.7 us -> 12.8 us
  blocking collectives: 7.92 us -> 9.95 us
  other arithmetic: 13.8 us -> 11.8 us
    ppermute x14, waiting for transfers between devices: 29.5 us -> 14.1 us  [move(): lax.ppermute(array, AXES, [(device(*at), device(at[0] + x, at[1] + y, at[...]
    pallas_call x1 -> x2, Pallas kernels: 16 us -> 22.2 us  [keys_of(): pl.pallas_call(body, grid_spec=pltpu.PrefetchScalarGridSpec(num_scalar_pr...]
    ppermute x3, waiting for transfers between devices: 0.01 us -> 2.82 us  [move_apart(): return lax.ppermute(array, AXES, pairs)]
    ppermute x14, starting transfers between devices: 19.6 us -> 17 us  [move(): lax.ppermute(array, AXES, [(device(*at), device(at[0] + x, at[1] + y, at[...]
    dot_general x1, matrix products: 2.67 us -> 4.85 us  [local(): lax.dot_general(other, low_other, contract, preferred_element_type=jnp.fl...]
    dot_general x1, matrix products: 2.46 us -> 4.63 us  [local(): lax.dot_general(own, low, contract, preferred_element_type=jnp.float32)]
    all_to_all x1, blocking collectives: 7.92 us -> 9.95 us  [exchange(): lax.all_to_all(array, AXES, split_axis=0, concat_axis=0, axis_index_group...]
    pallas_call x1, Pallas kernels: 1 us -> 2.37 us  [pack_rows(): pl.pallas_call(body, grid_spec=pltpu.PrefetchScalarGridSpec(num_scalar_pr...]
  transfers between devices with their start and end apart: 20 -> 20, of which waited for: 4 -> 5; matrix products, arithmetic and copies ran while one was open for 21% -> 23% of each run, Pallas kernels for 13% -> 19%
where the time goes in v4:
time: 131 us; the launch traced here: 130 us
  Pallas kernels  32.8 us (25%)
  starting transfers between devices  32.3 us (25%)
  waiting for transfers between devices  20.7 us (16%)
  matrix products  12.8 us (10%)
  other arithmetic  11.8 us (9%)
  blocking collectives  9.95 us (8%)
  local copies, waits for them, and re-layouts  8.75 us (7%)
    pallas_call x2, Pallas kernels, keys_of(): pl.pallas_call(body, grid_spec=pltpu.PrefetchScalarGridSpec(num_scalar_pr...  22.2 us
    ppermute x14, starting transfers between devices, move(): lax.ppermute(array, AXES, [(device(*at), device(at[0] + x, at[1] + y, at[...  17 us
    ppermute x14, waiting for transfers between devices, move(): lax.ppermute(array, AXES, [(device(*at), device(at[0] + x, at[1] + y, at[...  14.1 us
    all_to_all x3, starting transfers between devices, exchange(): lax.all_to_all(array, AXES, split_axis=0, concat_axis=0, axis_index_group...  13.1 us
    all_to_all x1, blocking collectives, exchange(): lax.all_to_all(array, AXES, split_axis=0, concat_axis=0, axis_index_group...  9.95 us
    pallas_call x1, Pallas kernels, pack_columns(): pl.pallas_call(body, grid_spec=pltpu.PrefetchScalarGridSpec(num_scalar_pr...  8.19 us
    dot_general x1, matrix products, local(): lax.dot_general(other, low_other, contract, preferred_element_type=jnp.fl...  4.85 us
    dot_general x1, matrix products, local(): lax.dot_general(own, low, contract, preferred_element_type=jnp.float32)  4.63 us
  transfers between devices with their start and end apart: 20, of which 5 were waited for; matrix products, arithmetic and copies ran while one was open for 23% of the time, Pallas kernels for 19%

profile of v4, /device:TPU:1, one launch (start us, length us, event | category | flops | bytes accessed | tf_op | source)
XLA Modules:
  0.0 130.0 jit_solution(10854641171816682241)
XLA Ops:
  0.7 8.2 %pack_columns.1 = (bf16[512,4096]{1,0:T(8,128)(2,1)}, bf16[512,4096]{1,0:T(8,128)(2,1)}) custom-call(s32[1]{0:T(128)} %bitcast.4.place_ref, bf16[512,8192]{1,0:T(8,128)(2,1)} %x_ref.1), custom_call_target="tpu_custom_call" | custom-call | flops 1 | bytes 1 | tf_op jit(solution)/shard_map/pack_columns/pallas_call | solution.py:41
  8.9 1.4 %collective-permute-start = (bf16[512,4096]{1,0:T(8,128)(2,1)}, bf16[512,4096]{1,0:T(8,128)(2,1)}, u32[]{:S(2)}, u32[]{:S(2)}) collective-permute-start(bf16[512,4096]{1,0:T(8,128)(2,1)} %get-tuple-element.18), channel_id=1, source_target_pairs={{0,8},{1,9},{2,10},{3,11},{8,0},{9,1},{10,2},{11,3},{4,12},{5,13},... | collective-permute-start | bytes 12582920 | tf_op jit(solution)/shard_map/ppermute | solution.py:166
  10.2 2.4 %pack_rows.1 = bf16[8,64,1024]{2,1,0:T(8,128)(2,1)} custom-call(s32[1]{0:T(128)} %bitcast.4.place_ref, bf16[8,2,64,1024]{3,2,1,0:T(8,128)(2,1)} %bitcast.74, bf16[512,4096]{1,0:T(8,128)(2,1)} %get-tuple-element.19.after_ref.refs_1_), custom_call_target="tpu_custom_call" | custom-call | flops 1 | bytes 1 | tf_op jit(solution)/shard_map/pack_rows/pallas_call | solution.py:64
  12.6 2.6 %collective-permute-start.5 = (bf16[512,1024]{1,0:T(8,128)(2,1)}, bf16[512,1024]{1,0:T(8,128)(2,1)}, u32[]{:S(2)}, u32[]{:S(2)}) collective-permute-start(bf16[512,1024]{1,0:T(8,128)(2,1)} %bitcast.77), channel_id=1, source_target_pairs={{0,3},{1,0},{2,1},{3,2},{8,11},{9,8},{10,9},{11,10},{4,7},{5,4},{6... | collective-permute-start | bytes 3145736 | tf_op jit(solution)/shard_map/ppermute | solution.py:166
  15.2 1.6 %collective-permute-start.7 = (bf16[512,1024]{1,0:T(8,128)(2,1)}, bf16[512,1024]{1,0:T(8,128)(2,1)}, u32[]{:S(2)}, u32[]{:S(2)}) collective-permute-start(bf16[512,1024]{1,0:T(8,128)(2,1)} %bitcast.79), channel_id=1, source_target_pairs={{0,20},{1,21},{2,22},{3,23},{8,12},{9,13},{10,14},{11,15},{4,0},{5... | collective-permute-start | bytes 3145736 | tf_op jit(solution)/shard_map/ppermute | solution.py:176
  17.6 2.8 %collective-permute-start.1 = (bf16[512,512]{1,0:T(8,128)(2,1)S(1)}, bf16[512,512]{1,0:T(8,128)(2,1)S(1)}, u32[]{:S(2)}, u32[]{:S(2)}) collective-permute-start(bf16[512,512]{1,0:T(8,128)(2,1)S(1)} %convolution_convert_fusion), channel_id=1, source_target_pairs={{0,8},{1,9},{2,10},{3,11},{8,0},{9,1},{10,2},{11,3},{4,12},{5,13},... | collective-permute-start | bytes 1572872 | tf_op jit(solution)/shard_map/ppermute | solution.py:166
  21.0 4.6 %fusion.11 = f32[4096,512]{1,0:T(8,128)S(1)} fusion(bf16[512,4096]{1,0:T(8,128)(2,1)} %get-tuple-element.19.after_ref.refs_1_, bf16[512,512]{1,0:T(8,128)(2,1)S(1)} %convolution_convert_fusion), kind=kOutput, calls=%fused_computation.35 | convolution fusion | flops 2147483648 | bytes 13107200 | tf_op jit(solution)/shard_map/dot_general | solution.py:215
  25.7 4.9 %add_convert_fusion = bf16[4096,512]{1,0:T(8,128)(2,1)S(1)} fusion(f32[4096,512]{1,0:T(8,128)S(1)} %fusion.11, bf16[512,4096]{1,0:T(8,128)(2,1)} %collective-permute-done.refs_0_, bf16[512,512]{1,0:T(8,128)(2,1)S(1)} %collective-permute-done.1), kind=kOutput, calls=%fused_computation | convolution fusion | flops 2151677952 | bytes 17301504 | tf_op jit(solution)/shard_map/dot_general | solution.py:216
  30.6 2.3 %fusion.10 = (bf16[4096,256]{1,0:T(8,128)(2,1)}, bf16[4096,256]{1,0:T(8,128)(2,1)}) fusion(bf16[4096,512]{1,0:T(8,128)(2,1)S(1)} %add_convert_fusion), kind=kLoop, calls=%fused_computation.34 | loop fusion | bytes 8388608 | tf_op jit(solution)/shard_map/slice | solution.py:237
  32.8 4.2 %all-to-all-start = ((bf16[4,1024,256]{2,1,0:T(8,128)(2,1)}), bf16[4,1024,256]{2,1,0:T(8,128)(2,1)S(1)}, u32[]{:S(2)}, u32[]{:S(2)}) async-start(bf16[4,1024,256]{2,1,0:T(8,128)(2,1)} %bitcast.70), calls=%async_computation | async-start | bytes 4194304 | tf_op jit(solution)/shard_map/all_to_all | solution.py:180
  37.0 2.9 %constant_dynamic-slice_fusion.3 = (bf16[4,1,4,1,64,256]{5,4,3,2,1,0:T(8,128)(2,1)}, bf16[4,1,4,1,64,256]{5,4,3,2,1,0:T(8,128)(2,1)}, bf16[4,1,4,1,64,256]{5,4,3,2,1,0:T(8,128)(2,1)}, bf16[4,1,4,1,64,256]{5,4,3,2,1,0:T(8,128)(2,1)}) fusion(bf16[4,2,4,2,64,256]{5,4,3,2,1,0:T(8,128)(2,1)} %bitcast.69, s32[]{:T(128)S(6)} %select_n.211, s32[]{:T(128)S(6)} %select_n.214, ...), kind=kLoop, calls=%fused_computation.31 | loop fusion | bytes 4194336 | tf_op jit(solution)/shard_map/dynamic_slice | solution.py:228
  40.0 0.9 collective-permute-start.4
  42.4 2.7 %collective-permute-start.9 = (bf16[512,1024]{1,0:T(8,128)(2,1)}, bf16[512,1024]{1,0:T(8,128)(2,1)}, u32[]{:S(2)}, u32[]{:S(2)}) collective-permute-start(bf16[512,1024]{1,0:T(8,128)(2,1)} %get-tuple-element.22), channel_id=1, source_target_pairs={{0,3},{1,0},{2,1},{3,2},{8,11},{9,8},{10,9},{11,10},{4,7},{5,4},{6... | collective-permute-start | bytes 3145736 | tf_op jit(solution)/shard_map/ppermute | solution.py:166
  45.0 2.3 %broadcast_select_fusion.refs_1_ = bf16[512,1024]{1,0:T(8,128)(2,1)} fusion(bf16[512,1024]{1,0:T(8,128)(2,1)} %get-tuple-element.20, bf16[512,1024]{1,0:T(8,128)(2,1)} %get-tuple-element.21, pred[]{:T(512)S(6)} %eq.41), kind=kLoop, calls=%fused_computation.10 | loop fusion | flops 524288 | bytes 3145729 | tf_op jit(solution)/shard_map/jit(_where)/select_n | solution.py:248
  47.4 10.1 %keys_of.2 = (f32[512,1024]{1,0:T(8,128)}, f32[512,1024]{1,0:T(8,128)}) custom-call(s32[4]{0:T(128)} %pad_add_fusion.1.shard_ref, bf16[512,4096]{1,0:T(8,128)(2,1)} %collective-permute-done.refs_0_, bf16[512,4096]{1,0:T(8,128)(2,1)} %get-tuple-element.19.after_ref.refs_1_, bf16[4,128,1024]{2,1,0:T(8,128)(2,1)} %bitcast.80, ...), custom_call_target="tpu_custom_call" | custom-call | flops 4294967296 | bytes 8388608 | tf_op jit(solution)/shard_map/keys_of/pallas_call | solution.py:117
  57.5 6.1 %collective-permute-done.3 = bf16[16,64,256]{2,1,0:T(8,128)(2,1)} collective-permute-done((bf16[16,64,256]{2,1,0:T(8,128)(2,1)}, bf16[16,64,256]{2,1,0:T(8,128)(2,1)}, u32[]{:S(2)}, u32[]{:S(2)}) %collective-permute-start.3) | collective-permute-done | bytes 524320 | tf_op jit(solution)/shard_map/ppermute | solution.py:166
  63.6 3.3 %collective-permute-done.2 = bf16[16,64,256]{2,1,0:T(8,128)(2,1)} collective-permute-done((bf16[16,64,256]{2,1,0:T(8,128)(2,1)}, bf16[16,64,256]{2,1,0:T(8,128)(2,1)}, u32[]{:S(2)}, u32[]{:S(2)}) %collective-permute-start.2) | collective-permute-done | bytes 524320 | tf_op jit(solution)/shard_map/ppermute | solution.py:166
  66.9 2.5 %fusion.2.refs_0_ = bf16[16,64,256]{2,1,0:T(8,128)(2,1)} fusion(bf16[16,64,256]{2,1,0:T(8,128)(2,1)} %collective-permute-done.4, bf16[16,64,256]{2,1,0:T(8,128)(2,1)} %collective-permute-done.3, bf16[16,64,256]{2,1,0:T(8,128)(2,1)} %collective-permute-done.2, bf16[4,1,4,1,64,256]{5,4,3,2,1,0:T(8,128)(2,1)S(1)} %copy-done.3), kind=kLoop, calls=%fused_computation.8 | loop fusion | flops 2097152 | bytes 2621440 | tf_op jit(solution)/shard_map/convert_element_type | solution.py:235
  69.9 4.2 %all-to-all-start.1 = ((bf16[4,256,256]{2,1,0:T(8,128)(2,1)}), bf16[4,256,256]{2,1,0:T(8,128)(2,1)}, u32[]{:S(2)}, u32[]{:S(2)}) async-start(bf16[4,256,256]{2,1,0:T(8,128)(2,1)} %bitcast.71), calls=%async_computation.1 | async-start | bytes 1048576 | tf_op jit(solution)/shard_map/all_to_all | solution.py:180
  77.4 3.7 %all-to-all-done.1 = bf16[4,256,256]{2,1,0:T(8,128)(2,1)} async-done(((bf16[4,256,256]{2,1,0:T(8,128)(2,1)}), bf16[4,256,256]{2,1,0:T(8,128)(2,1)}, u32[]{:S(2)}, u32[]{:S(2)}) %all-to-all-start.1) | async-done | bytes 524320 | tf_op jit(solution)/shard_map/all_to_all | solution.py:180
  81.1 1.2 add_convert_fusion.3
  82.3 2.8 %collective-permute-done.8.refs_0_ = bf16[512,1024]{1,0:T(8,128)(2,1)} collective-permute-done((bf16[512,1024]{1,0:T(8,128)(2,1)}, bf16[512,1024]{1,0:T(8,128)(2,1)}, u32[]{:S(2)}, u32[]{:S(2)}) %collective-permute-start.8) | collective-permute-done | bytes 1048608 | tf_op jit(solution)/shard_map/ppermute | solution.py:176
  85.3 1.0 fusion.5
  86.3 9.9 %all_to_all.20 = bf16[4,64,512]{2,1,0:T(8,128)(2,1)S(1)} all-to-all(bf16[4,64,512]{2,1,0:T(8,128)(2,1)S(1)} %pad_maximum_fusion.1), channel_id=1, replica_groups={{0,1,2,3},{8,9,10,11},{4,5,6,7},{12,13,14,15},{16,17,18,19},{24,25,26,2..., dimensions={0} | all-to-all | bytes 524288 | tf_op jit(solution)/shard_map/all_to_all | solution.py:180
  97.9 4.7 %all-to-all-start.3 = ((bf16[8,64,512]{2,1,0:T(8,128)(2,1)}), bf16[8,64,512]{2,1,0:T(8,128)(2,1)S(1)}, u32[]{:S(2)}, u32[]{:S(2)}) async-start(bf16[8,64,512]{2,1,0:T(8,128)(2,1)} %broadcast_in_dim.2), calls=%async_computation.3 | async-start | bytes 1048576 | tf_op jit(solution)/shard_map/all_to_all | solution.py:180
  103.2 1.0 copy-done.6
  104.2 12.1 %keys_of.3 = (f32[512,1024]{1,0:T(8,128)}, f32[512,1024]{1,0:T(8,128)}) custom-call(s32[4]{0:T(128)} %pad_add_fusion.shard_ref, bf16[512,4096]{1,0:T(8,128)(2,1)} %collective-permute-done.refs_0_, bf16[512,4096]{1,0:T(8,128)(2,1)} %get-tuple-element.19.after_ref.refs_1_, bf16[4,128,1024]{2,1,0:T(8,128)(2,1)} %bitcast.25.refs_2_, ...), custom_call_target="tpu_custom_call" | custom-call | flops 1 | bytes 1 | tf_op jit(solution)/shard_map/keys_of/pallas_call | solution.py:117
  117.1 2.9 %collective-permute-start.15 = (f32[512,1024]{1,0:T(8,128)}, f32[512,1024]{1,0:T(8,128)S(1)}, u32[]{:S(2)}, u32[]{:S(2)}) collective-permute-start(f32[512,1024]{1,0:T(8,128)} %together.7), channel_id=1, source_target_pairs={{0,8},{1,9},{2,10},{3,11},{8,0},{9,1},{10,2},{11,3},{4,12},{5,13},... | collective-permute-start | bytes 6291464 | tf_op jit(solution)/shard_map/ppermute | solution.py:166
  120.0 4.7 %collective-permute-done.16 = bf16[8,64,512]{2,1,0:T(8,128)(2,1)S(1)} collective-permute-done((bf16[8,64,512]{2,1,0:T(8,128)(2,1)}, bf16[8,64,512]{2,1,0:T(8,128)(2,1)S(1)}, u32[]{:S(2)}, u32[]{:S(2)}) %collective-permute-start.16) | collective-permute-done | bytes 524320 | tf_op jit(solution)/shard_map/ppermute | solution.py:166
  124.7 1.1 select_bitcast_fusion.1
  126.0 2.6 %subtract_convert_fusion = bf16[1024,1024]{1,0:T(8,128)(2,1)} fusion(bf16[1024,1024]{1,0:T(8,128)(2,1)S(1)} %copy-done.5, bf16[1024,512]{1,0:T(8,128)(2,1)S(1)} %bitcast.76, bf16[1024,512]{1,0:T(8,128)(2,1)S(1)} %copy-done), kind=kOutput, calls=%fused_computation.1 | convolution fusion | flops 1077936128 | bytes 6291456 | tf_op jit(solution)/shard_map/dot_general | solution.py:274
  128.7 1.3 add_convert_fusion.1
  (66 shorter events, 10.0 us)
Async XLA Ops:
  0.6 16.2 %copy-start = (bf16[1024,512]{1,0:T(8,128)(2,1)S(1)}, bf16[1024,512]{1,0:T(8,128)(2,1)}, u32[]{:S(2)}) copy-start(bf16[1024,512]{1,0:T(8,128)(2,1)} %param.9) | copy-start | bytes 3145732
  8.9 8.0 %copy-start.13 = (bf16[512,1024]{1,0:T(8,128)(2,1)S(1)}, bf16[512,1024]{1,0:T(8,128)(2,1)}, u32[]{:S(2)}) copy-start(bf16[512,1024]{1,0:T(8,128)(2,1)} %param.7) | copy-start | bytes 3145732
  8.9 16.8 %collective-permute-start = (bf16[512,4096]{1,0:T(8,128)(2,1)}, bf16[512,4096]{1,0:T(8,128)(2,1)}, u32[]{:S(2)}, u32[]{:S(2)}) collective-permute-start(bf16[512,4096]{1,0:T(8,128)(2,1)} %get-tuple-element.18), channel_id=1, source_target_pairs={{0,8},{1,9},{2,10},{3,11},{8,0},{9,1},{10,2},{11,3},{4,12},{5,13},... | collective-permute-start | bytes 12582920 | tf_op jit(solution)/shard_map/ppermute | solution.py:166
  12.6 29.0 %collective-permute-start.5 = (bf16[512,1024]{1,0:T(8,128)(2,1)}, bf16[512,1024]{1,0:T(8,128)(2,1)}, u32[]{:S(2)}, u32[]{:S(2)}) collective-permute-start(bf16[512,1024]{1,0:T(8,128)(2,1)} %bitcast.77), channel_id=1, source_target_pairs={{0,3},{1,0},{2,1},{3,2},{8,11},{9,8},{10,9},{11,10},{4,7},{5,4},{6... | collective-permute-start | bytes 3145736 | tf_op jit(solution)/shard_map/ppermute | solution.py:166
  15.2 27.2 %collective-permute-start.6 = (bf16[512,1024]{1,0:T(8,128)(2,1)}, bf16[512,1024]{1,0:T(8,128)(2,1)}, u32[]{:S(2)}, u32[]{:S(2)}) collective-permute-start(bf16[512,1024]{1,0:T(8,128)(2,1)} %bitcast.78), channel_id=1, source_target_pairs={{0,1},{1,2},{2,3},{3,0},{8,9},{9,10},{10,11},{11,8},{4,5},{5,6},{6... | collective-permute-start | bytes 3145736 | tf_op jit(solution)/shard_map/ppermute | solution.py:166
  15.2 27.2 %collective-permute-start.7 = (bf16[512,1024]{1,0:T(8,128)(2,1)}, bf16[512,1024]{1,0:T(8,128)(2,1)}, u32[]{:S(2)}, u32[]{:S(2)}) collective-permute-start(bf16[512,1024]{1,0:T(8,128)(2,1)} %bitcast.79), channel_id=1, source_target_pairs={{0,20},{1,21},{2,22},{3,23},{8,12},{9,13},{10,14},{11,15},{4,0},{5... | collective-permute-start | bytes 3145736 | tf_op jit(solution)/shard_map/ppermute | solution.py:176
  17.6 8.1 %collective-permute-start.1 = (bf16[512,512]{1,0:T(8,128)(2,1)S(1)}, bf16[512,512]{1,0:T(8,128)(2,1)S(1)}, u32[]{:S(2)}, u32[]{:S(2)}) collective-permute-start(bf16[512,512]{1,0:T(8,128)(2,1)S(1)} %convolution_convert_fusion), channel_id=1, source_target_pairs={{0,8},{1,9},{2,10},{3,11},{8,0},{9,1},{10,2},{11,3},{4,12},{5,13},... | collective-permute-start | bytes 1572872 | tf_op jit(solution)/shard_map/ppermute | solution.py:166
  32.8 37.0 %all-to-all-start = ((bf16[4,1024,256]{2,1,0:T(8,128)(2,1)}), bf16[4,1024,256]{2,1,0:T(8,128)(2,1)S(1)}, u32[]{:S(2)}, u32[]{:S(2)}) async-start(bf16[4,1024,256]{2,1,0:T(8,128)(2,1)} %bitcast.70), calls=%async_computation | async-start | bytes 4194304 | tf_op jit(solution)/shard_map/all_to_all | solution.py:180
  40.0 17.5 %collective-permute-start.4 = (bf16[16,64,256]{2,1,0:T(8,128)(2,1)}, bf16[16,64,256]{2,1,0:T(8,128)(2,1)}, u32[]{:S(2)}, u32[]{:S(2)}) collective-permute-start(bf16[16,64,256]{2,1,0:T(8,128)(2,1)} %bitcast.9.refs_5_), channel_id=1, source_target_pairs={{0,16},{1,17},{2,18},{3,19},{8,24},{9,25},{10,26},{11,27},{4,20},{... | collective-permute-start | bytes 1572872 | tf_op jit(solution)/shard_map/ppermute | solution.py:166
  40.9 22.7 %collective-permute-start.3 = (bf16[16,64,256]{2,1,0:T(8,128)(2,1)}, bf16[16,64,256]{2,1,0:T(8,128)(2,1)}, u32[]{:S(2)}, u32[]{:S(2)}) collective-permute-start(bf16[16,64,256]{2,1,0:T(8,128)(2,1)} %bitcast.8.refs_4_), channel_id=1, source_target_pairs={{0,20},{1,21},{2,22},{3,23},{8,28},{9,29},{10,30},{11,31},{4,0},{5... | collective-permute-start | bytes 1572872 | tf_op jit(solution)/shard_map/ppermute | solution.py:166
  41.6 25.2 %collective-permute-start.2 = (bf16[16,64,256]{2,1,0:T(8,128)(2,1)}, bf16[16,64,256]{2,1,0:T(8,128)(2,1)}, u32[]{:S(2)}, u32[]{:S(2)}) collective-permute-start(bf16[16,64,256]{2,1,0:T(8,128)(2,1)} %bitcast.7.refs_3_), channel_id=1, source_target_pairs={{0,4},{1,5},{2,6},{3,7},{8,12},{9,13},{10,14},{11,15},{4,16},{5,17... | collective-permute-start | bytes 1572872 | tf_op jit(solution)/shard_map/ppermute | solution.py:166
  42.4 34.3 %collective-permute-start.9 = (bf16[512,1024]{1,0:T(8,128)(2,1)}, bf16[512,1024]{1,0:T(8,128)(2,1)}, u32[]{:S(2)}, u32[]{:S(2)}) collective-permute-start(bf16[512,1024]{1,0:T(8,128)(2,1)} %get-tuple-element.22), channel_id=1, source_target_pairs={{0,3},{1,0},{2,1},{3,2},{8,11},{9,8},{10,9},{11,10},{4,7},{5,4},{6... | collective-permute-start | bytes 3145736 | tf_op jit(solution)/shard_map/ppermute | solution.py:166
  45.0 37.3 %collective-permute-start.10 = (bf16[512,1024]{1,0:T(8,128)(2,1)}, bf16[512,1024]{1,0:T(8,128)(2,1)}, u32[]{:S(2)}, u32[]{:S(2)}) collective-permute-start(bf16[512,1024]{1,0:T(8,128)(2,1)} %get-tuple-element.22), channel_id=1, source_target_pairs={{0,1},{1,2},{2,3},{3,0},{8,9},{9,10},{10,11},{11,8},{4,5},{5,6},{6... | collective-permute-start | bytes 3145736 | tf_op jit(solution)/shard_map/ppermute | solution.py:166
  47.4 19.5 %copy-start.3 = (bf16[4,1,4,1,64,256]{5,4,3,2,1,0:T(8,128)(2,1)S(1)}, bf16[4,1,4,1,64,256]{5,4,3,2,1,0:T(8,128)(2,1)}, u32[]{:S(2)}) copy-start(bf16[4,1,4,1,64,256]{5,4,3,2,1,0:T(8,128)(2,1)} %get-tuple-element.37) | copy-start | bytes 1572868
  69.4 15.8 %collective-permute-start.8 = (bf16[512,1024]{1,0:T(8,128)(2,1)}, bf16[512,1024]{1,0:T(8,128)(2,1)}, u32[]{:S(2)}, u32[]{:S(2)}) collective-permute-start(bf16[512,1024]{1,0:T(8,128)(2,1)} %get-tuple-element.24), channel_id=1, source_target_pairs={{0,3},{1,0},{2,1},{3,2},{8,9},{9,10},{10,11},{11,8},{4,7},{5,4},{6... | collective-permute-start | bytes 3145736 | tf_op jit(solution)/shard_map/ppermute | solution.py:176
  69.9 11.3 %all-to-all-start.1 = ((bf16[4,256,256]{2,1,0:T(8,128)(2,1)}), bf16[4,256,256]{2,1,0:T(8,128)(2,1)}, u32[]{:S(2)}, u32[]{:S(2)}) async-start(bf16[4,256,256]{2,1,0:T(8,128)(2,1)} %bitcast.71), calls=%async_computation.1 | async-start | bytes 1048576 | tf_op jit(solution)/shard_map/all_to_all | solution.py:180
  74.1 22.1 %copy-start.11 = (f32[64,512]{1,0:T(8,128)S(1)}, f32[64,512]{1,0:T(8,128)}, u32[]{:S(2)}) copy-start(f32[64,512]{1,0:T(8,128)} %param.10) | copy-start | bytes 393220
  74.1 22.1 %copy-start.12 = (f32[64,512]{1,0:T(8,128)S(1)}, f32[64,512]{1,0:T(8,128)}, u32[]{:S(2)}) copy-start(f32[64,512]{1,0:T(8,128)} %param.11) | copy-start | bytes 393220
  75.2 9.9 %copy-start.8 = (bf16[4,64,256]{2,1,0:T(8,128)(2,1)}, bf16[4,64,256]{2,1,0:T(8,128)(2,1)S(1)}, u32[]{:S(2)}) copy-start(bf16[4,64,256]{2,1,0:T(8,128)(2,1)S(1)} %get-tuple-element.45.refs_3_) | copy-start | bytes 393220
  75.2 9.9 %copy-start.9 = (bf16[4,64,256]{2,1,0:T(8,128)(2,1)}, bf16[4,64,256]{2,1,0:T(8,128)(2,1)S(1)}, u32[]{:S(2)}) copy-start(bf16[4,64,256]{2,1,0:T(8,128)(2,1)S(1)} %get-tuple-element.44.refs_4_) | copy-start | bytes 393220
  75.2 9.9 %copy-start.10 = (bf16[4,64,256]{2,1,0:T(8,128)(2,1)}, bf16[4,64,256]{2,1,0:T(8,128)(2,1)S(1)}, u32[]{:S(2)}) copy-start(bf16[4,64,256]{2,1,0:T(8,128)(2,1)S(1)} %get-tuple-element.43.refs_5_) | copy-start | bytes 393220
  75.2 10.0 %collective-permute-start.14 = (bf16[4,64,256]{2,1,0:T(8,128)(2,1)S(1)}, bf16[4,64,256]{2,1,0:T(8,128)(2,1)S(1)}, u32[]{:S(2)}, u32[]{:S(2)}) collective-permute-start(bf16[4,64,256]{2,1,0:T(8,128)(2,1)S(1)} %get-tuple-element.43.refs_5_), channel_id=1, source_target_pairs={{0,16},{1,17},{2,18},{3,19},{8,24},{9,25},{10,26},{11,27},{4,20},{... | collective-permute-start | bytes 393224 | tf_op jit(solution)/shard_map/ppermute | solution.py:166
  75.9 9.3 %collective-permute-start.13 = (bf16[4,64,256]{2,1,0:T(8,128)(2,1)S(1)}, bf16[4,64,256]{2,1,0:T(8,128)(2,1)S(1)}, u32[]{:S(2)}, u32[]{:S(2)}) collective-permute-start(bf16[4,64,256]{2,1,0:T(8,128)(2,1)S(1)} %get-tuple-element.44.refs_4_), channel_id=1, source_target_pairs={{0,20},{1,21},{2,22},{3,23},{8,28},{9,29},{10,30},{11,31},{4,0},{5... | collective-permute-start | bytes 393224 | tf_op jit(solution)/shard_map/ppermute | solution.py:166
  76.7 8.6 %collective-permute-start.12 = (bf16[4,64,256]{2,1,0:T(8,128)(2,1)S(1)}, bf16[4,64,256]{2,1,0:T(8,128)(2,1)S(1)}, u32[]{:S(2)}, u32[]{:S(2)}) collective-permute-start(bf16[4,64,256]{2,1,0:T(8,128)(2,1)S(1)} %get-tuple-element.45.refs_3_), channel_id=1, source_target_pairs={{0,4},{1,5},{2,6},{3,7},{8,12},{9,13},{10,14},{11,15},{4,16},{5,17... | collective-permute-start | bytes 393224 | tf_op jit(solution)/shard_map/ppermute | solution.py:166
  85.1 18.0 %collective-permute-start.11 = (bf16[512,1024]{1,0:T(8,128)(2,1)}, bf16[512,1024]{1,0:T(8,128)(2,1)S(1)}, u32[]{:S(2)}, u32[]{:S(2)}) collective-permute-start(bf16[512,1024]{1,0:T(8,128)(2,1)} %get-tuple-element.27), channel_id=1, source_target_pairs={{0,20},{1,21},{2,22},{3,23},{8,12},{9,13},{10,14},{11,15},{4,0},{5... | collective-permute-start | bytes 3145736 | tf_op jit(solution)/shard_map/ppermute | solution.py:176
  97.0 6.1 %copy-start.7 = (bf16[64,512]{1,0:T(8,128)(2,1)}, bf16[64,512]{1,0:T(8,128)(2,1)S(1)}, u32[]{:S(2)}) copy-start(bf16[64,512]{1,0:T(8,128)(2,1)S(1)} %get-tuple-element.32.refs_8_) | copy-start | bytes 196612
  97.9 18.4 %all-to-all-start.3 = ((bf16[8,64,512]{2,1,0:T(8,128)(2,1)}), bf16[8,64,512]{2,1,0:T(8,128)(2,1)S(1)}, u32[]{:S(2)}, u32[]{:S(2)}) async-start(bf16[8,64,512]{2,1,0:T(8,128)(2,1)} %broadcast_in_dim.2), calls=%async_computation.3 | async-start | bytes 1048576 | tf_op jit(solution)/shard_map/all_to_all | solution.py:180
  103.2 1.0 copy-start.6
  117.1 8.9 %copy-start.5 = (bf16[1024,1024]{1,0:T(8,128)(2,1)S(1)}, bf16[1024,1024]{1,0:T(8,128)(2,1)}, u32[]{:S(2)}) copy-start(bf16[1024,1024]{1,0:T(8,128)(2,1)} %param.8) | copy-start | bytes 6291460
  117.1 11.6 %collective-permute-start.15 = (f32[512,1024]{1,0:T(8,128)}, f32[512,1024]{1,0:T(8,128)S(1)}, u32[]{:S(2)}, u32[]{:S(2)}) collective-permute-start(f32[512,1024]{1,0:T(8,128)} %together.7), channel_id=1, source_target_pairs={{0,8},{1,9},{2,10},{3,11},{8,0},{9,1},{10,2},{11,3},{4,12},{5,13},... | collective-permute-start | bytes 6291464 | tf_op jit(solution)/shard_map/ppermute | solution.py:166
  120.0 4.7 %collective-permute-start.16 = (bf16[8,64,512]{2,1,0:T(8,128)(2,1)}, bf16[8,64,512]{2,1,0:T(8,128)(2,1)S(1)}, u32[]{:S(2)}, u32[]{:S(2)}) collective-permute-start(bf16[8,64,512]{2,1,0:T(8,128)(2,1)} %copy-done.1), channel_id=1, source_target_pairs={{0,8},{1,9},{2,10},{3,11},{8,0},{9,1},{10,2},{11,3},{4,12},{5,13},... | collective-permute-start | bytes 1572872 | tf_op jit(solution)/shard_map/ppermute | solution.py:166
  126.0 2.7 %copy-start.4 = (f32[512,1024]{1,0:T(8,128)S(1)}, f32[512,1024]{1,0:T(8,128)}, u32[]{:S(2)}) copy-start(f32[512,1024]{1,0:T(8,128)} %get-tuple-element.30) | copy-start | bytes 6291460
  (2 other events, 1.6 us)

commit v5 on v4

--- a/solution.py
+++ b/solution.py
@@ -79,7 +79,7 @@
     )(place, weight, after)
 
 
-def keys_of(packed, shards, pieces, addends=(), after=()):
+def keys_of(packed, shard, steps, pieces, addends=(), after=()):
     rows, features = pieces[0].shape
     count, many = len(pieces), len(packed)
     part = rows // 4
@@ -92,13 +92,15 @@
     def body(shard_ref, *refs):
         ins, plus, outs = refs[: many + count], refs[many + count :], refs[inputs : inputs + many]
         rows_ref, packed_ref, sems = refs[-3:]
+        at_lo, at_x = shard_ref[0] // X, shard_ref[0] % X
+        shards = [(at_lo + lo) % LO * X + (at_x + x) % X for lo, x in steps]
         copies = [pltpu.make_async_copy(ins[many + k], rows_ref.at[:, k], sems.at[many, k]) for k in range(count)]
         loads = []
         for i in range(many):
             loads.append([])
             for y in range(4):
                 for k in range(count):
-                    at = pl.multiple_of((y * every_shard + shard_ref[k]) * part, part)
+                    at = pl.multiple_of((y * every_shard + shards[k]) * part, part)
                     to = packed_ref.at[i, :, pl.ds((y * count + k) * part, part)]
                     loads[i].append(pltpu.make_async_copy(ins[i].at[:, pl.ds(at, part)], to, sems.at[i, y * count + k]))
         for copy in copies + sum(loads, []):
@@ -137,7 +139,7 @@
             transcendentals=0,
         ),
         name="keys_of",
-    )(shards, *packed, *[piece.reshape(4, part, features) for piece in pieces], *addends, *after)
+    )(shard, *packed, *[piece.reshape(4, part, features) for piece in pieces], *addends, *after)
 
 
 def together(*arrays, after=()):
@@ -183,7 +185,7 @@
 def local(tokens, cotangent, weight, basis, exp_avg, exp_avg_sq):
     core = lax.axis_index("dp") % 2
     shard = lax.axis_index("fsdp")
-    my_x, my_lo = shard % X, shard // X
+    my_lo = shard // X
     my_z = lax.axis_index("dp") // 2 % 2 * 2 + my_lo
     features = weight.shape[1]
     chips = lax.axis_size("dp") // CORE
@@ -243,8 +245,8 @@
     zx_up = move(w_z, x=-1)
     zx_down = move(w_z, x=1)
     steps = [(0, 0), (0, 1), (0, 3), (1, 0), (1, 1), (1, 3), (0, 2), (1, 2)]
-    shards = jnp.stack([(my_lo + lo) % LO * X + (my_x + x) % X for lo, x in steps])
-    other_near, own_near = keys_of([other, own], shards[:4], [half, w_up, w_down, w_z])
+    at = shard.reshape(1)
+    other_near, own_near = keys_of([other, own], at, steps[:4], [half, w_up, w_down, w_z])
     second, w_far = together(second, jnp.where(core == 0, w_up, w_down), after=(own_near,))
     w_far = move_apart(w_far, x=-1)
     second = sum_all(exchange(second.reshape(4, X * ROWS, rank // 2), along_y)).astype(jnp.bfloat16)
@@ -262,7 +264,7 @@
     direction = new_avg / first_fix / (jnp.sqrt(new_sq / second_fix) + 1e-08)
     direction = direction.astype(jnp.bfloat16)
     for_other, own_keys = keys_of(
-        [other, own], shards[4:], [zx_up, zx_down, w_far, zx_far], [other_near, own_near], (direction,)
+        [other, own], at, steps[4:], [zx_up, zx_down, w_far, zx_far], [other_near, own_near], (direction,)
     )
 
     mine = exchange(jnp.broadcast_to(direction[None], (chips, ROWS, rank)), same_shard)

time: 131 us -> 129 us (0.985)
  Pallas kernels: 32.8 us -> 31.4 us
    pallas_call x2, Pallas kernels: 22.2 us -> 20.8 us  [keys_of(): pl.pallas_call(body, grid_spec=pltpu.PrefetchScalarGridSpec(num_scalar_pr...]
    another operation x4 -> x2, other arithmetic: 2.69 us -> 1.42 us
  transfers between devices with their start and end apart: 20 -> 20, of which waited for: 5 -> 5; matrix products, arithmetic and copies ran while one was open for 23% -> 22% of each run, Pallas kernels for 19% -> 18%
where the time goes in v5:
time: 129 us; the launch traced here: 128 us
  starting transfers between devices  32 us (25%)
  Pallas kernels  31.4 us (24%)
  waiting for transfers between devices  21.6 us (17%)
  matrix products  12.8 us (10%)
  other arithmetic  10.6 us (8%)
  blocking collectives  9.94 us (8%)
  local copies, waits for them, and re-layouts  8.73 us (7%)
    pallas_call x2, Pallas kernels, keys_of(): pl.pallas_call(body, grid_spec=pltpu.PrefetchScalarGridSpec(num_scalar_pr...  20.8 us
    ppermute x14, starting transfers between devices, move(): lax.ppermute(array, AXES, [(device(*at), device(at[0] + x, at[1] + y, at[...  16.8 us
    ppermute x14, waiting for transfers between devices, move(): lax.ppermute(array, AXES, [(device(*at), device(at[0] + x, at[1] + y, at[...  15 us
    all_to_all x3, starting transfers between devices, exchange(): lax.all_to_all(array, AXES, split_axis=0, concat_axis=0, axis_index_group...  13 us
    all_to_all x1, blocking collectives, exchange(): lax.all_to_all(array, AXES, split_axis=0, concat_axis=0, axis_index_group...  9.94 us
    pallas_call x1, Pallas kernels, pack_columns(): pl.pallas_call(body, grid_spec=pltpu.PrefetchScalarGridSpec(num_scalar_pr...  8.19 us
    dot_general x1, matrix products, local(): lax.dot_general(other, low_other, contract, preferred_element_type=jnp.fl...  4.86 us
    dot_general x1, matrix products, local(): lax.dot_general(own, low, contract, preferred_element_type=jnp.float32)  4.63 us
  transfers between devices with their start and end apart: 20, of which 5 were waited for; matrix products, arithmetic and copies ran while one was open for 22% of the time, Pallas kernels for 18%

profile of v5, /device:TPU:1, one launch (start us, length us, event | category | flops | bytes accessed | tf_op | source)
XLA Modules:
  0.0 127.9 jit_solution(1029893066657752073)
XLA Ops:
  0.7 8.2 %pack_columns.1 = (bf16[512,4096]{1,0:T(8,128)(2,1)}, bf16[512,4096]{1,0:T(8,128)(2,1)}) custom-call(s32[1]{0:T(128)} %bitcast.1.place_ref, bf16[512,8192]{1,0:T(8,128)(2,1)} %x_ref.1), custom_call_target="tpu_custom_call" | custom-call | flops 1 | bytes 1 | tf_op jit(solution)/shard_map/pack_columns/pallas_call | solution.py:41
  8.9 1.4 %collective-permute-start = (bf16[512,4096]{1,0:T(8,128)(2,1)}, bf16[512,4096]{1,0:T(8,128)(2,1)}, u32[]{:S(2)}, u32[]{:S(2)}) collective-permute-start(bf16[512,4096]{1,0:T(8,128)(2,1)} %get-tuple-element.18), channel_id=1, source_target_pairs={{0,8},{1,9},{2,10},{3,11},{8,0},{9,1},{10,2},{11,3},{4,12},{5,13},... | collective-permute-start | bytes 12582920 | tf_op jit(solution)/shard_map/ppermute | solution.py:168
  10.2 2.4 %pack_rows.1 = bf16[8,64,1024]{2,1,0:T(8,128)(2,1)} custom-call(s32[1]{0:T(128)} %bitcast.1.place_ref, bf16[8,2,64,1024]{3,2,1,0:T(8,128)(2,1)} %bitcast.67, bf16[512,4096]{1,0:T(8,128)(2,1)} %get-tuple-element.19.after_ref.refs_1_), custom_call_target="tpu_custom_call" | custom-call | flops 1 | bytes 1 | tf_op jit(solution)/shard_map/pack_rows/pallas_call | solution.py:64
  12.6 2.6 %collective-permute-start.5 = (bf16[512,1024]{1,0:T(8,128)(2,1)}, bf16[512,1024]{1,0:T(8,128)(2,1)}, u32[]{:S(2)}, u32[]{:S(2)}) collective-permute-start(bf16[512,1024]{1,0:T(8,128)(2,1)} %bitcast.70), channel_id=1, source_target_pairs={{0,3},{1,0},{2,1},{3,2},{8,11},{9,8},{10,9},{11,10},{4,7},{5,4},{6... | collective-permute-start | bytes 3145736 | tf_op jit(solution)/shard_map/ppermute | solution.py:168
  15.2 1.6 %collective-permute-start.7 = (bf16[512,1024]{1,0:T(8,128)(2,1)}, bf16[512,1024]{1,0:T(8,128)(2,1)}, u32[]{:S(2)}, u32[]{:S(2)}) collective-permute-start(bf16[512,1024]{1,0:T(8,128)(2,1)} %bitcast.72), channel_id=1, source_target_pairs={{0,20},{1,21},{2,22},{3,23},{8,12},{9,13},{10,14},{11,15},{4,0},{5... | collective-permute-start | bytes 3145736 | tf_op jit(solution)/shard_map/ppermute | solution.py:178
  17.6 2.8 %collective-permute-start.1 = (bf16[512,512]{1,0:T(8,128)(2,1)S(1)}, bf16[512,512]{1,0:T(8,128)(2,1)S(1)}, u32[]{:S(2)}, u32[]{:S(2)}) collective-permute-start(bf16[512,512]{1,0:T(8,128)(2,1)S(1)} %convolution_convert_fusion), channel_id=1, source_target_pairs={{0,8},{1,9},{2,10},{3,11},{8,0},{9,1},{10,2},{11,3},{4,12},{5,13},... | collective-permute-start | bytes 1572872 | tf_op jit(solution)/shard_map/ppermute | solution.py:168
  20.4 4.6 %fusion.11 = f32[4096,512]{1,0:T(8,128)S(1)} fusion(bf16[512,4096]{1,0:T(8,128)(2,1)} %get-tuple-element.19.after_ref.refs_1_, bf16[512,512]{1,0:T(8,128)(2,1)S(1)} %convolution_convert_fusion), kind=kOutput, calls=%fused_computation.33 | convolution fusion | flops 2147483648 | bytes 13107200 | tf_op jit(solution)/shard_map/dot_general | solution.py:217
  25.0 4.9 %add_convert_fusion = bf16[4096,512]{1,0:T(8,128)(2,1)S(1)} fusion(f32[4096,512]{1,0:T(8,128)S(1)} %fusion.11, bf16[512,4096]{1,0:T(8,128)(2,1)} %collective-permute-done.refs_0_, bf16[512,512]{1,0:T(8,128)(2,1)S(1)} %collective-permute-done.1), kind=kOutput, calls=%fused_computation | convolution fusion | flops 2151677952 | bytes 17301504 | tf_op jit(solution)/shard_map/dot_general | solution.py:218
  29.9 2.3 %fusion.10 = (bf16[4096,256]{1,0:T(8,128)(2,1)}, bf16[4096,256]{1,0:T(8,128)(2,1)}) fusion(bf16[4096,512]{1,0:T(8,128)(2,1)S(1)} %add_convert_fusion), kind=kLoop, calls=%fused_computation.32 | loop fusion | bytes 8388608 | tf_op jit(solution)/shard_map/slice | solution.py:239
  32.2 4.2 %all-to-all-start = ((bf16[4,1024,256]{2,1,0:T(8,128)(2,1)}), bf16[4,1024,256]{2,1,0:T(8,128)(2,1)S(1)}, u32[]{:S(2)}, u32[]{:S(2)}) async-start(bf16[4,1024,256]{2,1,0:T(8,128)(2,1)} %bitcast.63), calls=%async_computation | async-start | bytes 4194304 | tf_op jit(solution)/shard_map/all_to_all | solution.py:182
  36.4 2.9 %constant_dynamic-slice_fusion.3 = (bf16[4,1,4,1,64,256]{5,4,3,2,1,0:T(8,128)(2,1)}, bf16[4,1,4,1,64,256]{5,4,3,2,1,0:T(8,128)(2,1)}, bf16[4,1,4,1,64,256]{5,4,3,2,1,0:T(8,128)(2,1)}, bf16[4,1,4,1,64,256]{5,4,3,2,1,0:T(8,128)(2,1)}) fusion(bf16[4,2,4,2,64,256]{5,4,3,2,1,0:T(8,128)(2,1)} %bitcast.62, s32[]{:T(128)S(6)} %select_n.157, s32[]{:T(128)S(6)} %select_n.160, ...), kind=kLoop, calls=%fused_computation.31 | loop fusion | bytes 4194336 | tf_op jit(solution)/shard_map/dynamic_slice | solution.py:230
  41.6 2.7 %collective-permute-start.9 = (bf16[512,1024]{1,0:T(8,128)(2,1)}, bf16[512,1024]{1,0:T(8,128)(2,1)}, u32[]{:S(2)}, u32[]{:S(2)}) collective-permute-start(bf16[512,1024]{1,0:T(8,128)(2,1)} %get-tuple-element.22), channel_id=1, source_target_pairs={{0,3},{1,0},{2,1},{3,2},{8,11},{9,8},{10,9},{11,10},{4,7},{5,4},{6... | collective-permute-start | bytes 3145736 | tf_op jit(solution)/shard_map/ppermute | solution.py:168
  44.3 2.3 %broadcast_select_fusion.refs_1_ = bf16[512,1024]{1,0:T(8,128)(2,1)} fusion(bf16[512,1024]{1,0:T(8,128)(2,1)} %get-tuple-element.20, bf16[512,1024]{1,0:T(8,128)(2,1)} %get-tuple-element.21, pred[]{:T(512)S(6)} %eq.24), kind=kLoop, calls=%fused_computation.10 | loop fusion | flops 524288 | bytes 3145729 | tf_op jit(solution)/shard_map/jit(_where)/select_n | solution.py:250
  46.6 9.4 %keys_of.2 = (f32[512,1024]{1,0:T(8,128)}, f32[512,1024]{1,0:T(8,128)}) custom-call(s32[1]{0:T(128)} %bitcast.shard_ref, bf16[512,4096]{1,0:T(8,128)(2,1)} %collective-permute-done.refs_0_, bf16[512,4096]{1,0:T(8,128)(2,1)} %get-tuple-element.19.after_ref.refs_1_, bf16[4,128,1024]{2,1,0:T(8,128)(2,1)} %bitcast.73, bf16[4,128,1024]{2,1,0:T(8,128)(2,1)} %bitcast.10.refs_3_, ...), custom_call_target="tpu_custom_call" | custom-call | flops 4294967296 | bytes 8388608 | tf_op jit(solution)/shard_map/keys_of/pallas_call | solution.py:119
  56.0 7.1 %collective-permute-done.3 = bf16[16,64,256]{2,1,0:T(8,128)(2,1)} collective-permute-done((bf16[16,64,256]{2,1,0:T(8,128)(2,1)}, bf16[16,64,256]{2,1,0:T(8,128)(2,1)}, u32[]{:S(2)}, u32[]{:S(2)}) %collective-permute-start.3) | collective-permute-done | bytes 524320 | tf_op jit(solution)/shard_map/ppermute | solution.py:168
  63.1 3.1 %collective-permute-done.2 = bf16[16,64,256]{2,1,0:T(8,128)(2,1)} collective-permute-done((bf16[16,64,256]{2,1,0:T(8,128)(2,1)}, bf16[16,64,256]{2,1,0:T(8,128)(2,1)}, u32[]{:S(2)}, u32[]{:S(2)}) %collective-permute-start.2) | collective-permute-done | bytes 524320 | tf_op jit(solution)/shard_map/ppermute | solution.py:168
  66.2 2.5 %fusion.2.refs_0_ = bf16[16,64,256]{2,1,0:T(8,128)(2,1)} fusion(bf16[16,64,256]{2,1,0:T(8,128)(2,1)} %collective-permute-done.4, bf16[16,64,256]{2,1,0:T(8,128)(2,1)} %collective-permute-done.3, bf16[16,64,256]{2,1,0:T(8,128)(2,1)} %collective-permute-done.2, bf16[4,1,4,1,64,256]{5,4,3,2,1,0:T(8,128)(2,1)S(1)} %copy-done.3), kind=kLoop, calls=%fused_computation.8 | loop fusion | flops 2097152 | bytes 2621440 | tf_op jit(solution)/shard_map/convert_element_type | solution.py:237
  69.2 4.2 %all-to-all-start.1 = ((bf16[4,256,256]{2,1,0:T(8,128)(2,1)}), bf16[4,256,256]{2,1,0:T(8,128)(2,1)}, u32[]{:S(2)}, u32[]{:S(2)}) async-start(bf16[4,256,256]{2,1,0:T(8,128)(2,1)} %bitcast.64), calls=%async_computation.1 | async-start | bytes 1048576 | tf_op jit(solution)/shard_map/all_to_all | solution.py:182
  76.7 3.8 %all-to-all-done.1 = bf16[4,256,256]{2,1,0:T(8,128)(2,1)} async-done(((bf16[4,256,256]{2,1,0:T(8,128)(2,1)}), bf16[4,256,256]{2,1,0:T(8,128)(2,1)}, u32[]{:S(2)}, u32[]{:S(2)}) %all-to-all-start.1) | async-done | bytes 524320 | tf_op jit(solution)/shard_map/all_to_all | solution.py:182
  80.5 1.2 add_convert_fusion.3
  81.7 2.8 %collective-permute-done.8.refs_0_ = bf16[512,1024]{1,0:T(8,128)(2,1)} collective-permute-done((bf16[512,1024]{1,0:T(8,128)(2,1)}, bf16[512,1024]{1,0:T(8,128)(2,1)}, u32[]{:S(2)}, u32[]{:S(2)}) %collective-permute-start.8) | collective-permute-done | bytes 1048608 | tf_op jit(solution)/shard_map/ppermute | solution.py:178
  84.6 1.0 fusion.5
  85.6 9.9 %all_to_all.20 = bf16[4,64,512]{2,1,0:T(8,128)(2,1)S(1)} all-to-all(bf16[4,64,512]{2,1,0:T(8,128)(2,1)S(1)} %pad_maximum_fusion.1), channel_id=1, replica_groups={{0,1,2,3},{8,9,10,11},{4,5,6,7},{12,13,14,15},{16,17,18,19},{24,25,26,2..., dimensions={0} | all-to-all | bytes 524288 | tf_op jit(solution)/shard_map/all_to_all | solution.py:182
  96.4 0.8 broadcast_in_dim.2
  97.2 4.6 %all-to-all-start.3 = ((bf16[8,64,512]{2,1,0:T(8,128)(2,1)}), bf16[8,64,512]{2,1,0:T(8,128)(2,1)S(1)}, u32[]{:S(2)}, u32[]{:S(2)}) async-start(bf16[8,64,512]{2,1,0:T(8,128)(2,1)} %broadcast_in_dim.2), calls=%async_computation.3 | async-start | bytes 1048576 | tf_op jit(solution)/shard_map/all_to_all | solution.py:182
  101.8 1.0 copy-done.6
  102.8 11.4 %keys_of.3 = (f32[512,1024]{1,0:T(8,128)}, f32[512,1024]{1,0:T(8,128)}) custom-call(s32[1]{0:T(128)} %bitcast.shard_ref, bf16[512,4096]{1,0:T(8,128)(2,1)} %collective-permute-done.refs_0_, bf16[512,4096]{1,0:T(8,128)(2,1)} %get-tuple-element.19.after_ref.refs_1_, bf16[4,128,1024]{2,1,0:T(8,128)(2,1)} %bitcast.18.refs_2_, ...), custom_call_target="tpu_custom_call" | custom-call | flops 1 | bytes 1 | tf_op jit(solution)/shard_map/keys_of/pallas_call | solution.py:119
  115.0 2.9 %collective-permute-start.15 = (f32[512,1024]{1,0:T(8,128)}, f32[512,1024]{1,0:T(8,128)S(1)}, u32[]{:S(2)}, u32[]{:S(2)}) collective-permute-start(f32[512,1024]{1,0:T(8,128)} %together.7), channel_id=1, source_target_pairs={{0,8},{1,9},{2,10},{3,11},{8,0},{9,1},{10,2},{11,3},{4,12},{5,13},... | collective-permute-start | bytes 6291464 | tf_op jit(solution)/shard_map/ppermute | solution.py:168
  117.9 4.7 %collective-permute-done.16 = bf16[8,64,512]{2,1,0:T(8,128)(2,1)S(1)} collective-permute-done((bf16[8,64,512]{2,1,0:T(8,128)(2,1)}, bf16[8,64,512]{2,1,0:T(8,128)(2,1)S(1)}, u32[]{:S(2)}, u32[]{:S(2)}) %collective-permute-start.16) | collective-permute-done | bytes 524320 | tf_op jit(solution)/shard_map/ppermute | solution.py:168
  122.7 1.1 select_bitcast_fusion.1
  124.0 2.6 %subtract_convert_fusion = bf16[1024,1024]{1,0:T(8,128)(2,1)} fusion(bf16[1024,1024]{1,0:T(8,128)(2,1)S(1)} %copy-done.5, bf16[1024,512]{1,0:T(8,128)(2,1)S(1)} %bitcast.69, bf16[1024,512]{1,0:T(8,128)(2,1)S(1)} %copy-done), kind=kOutput, calls=%fused_computation.1 | convolution fusion | flops 1077936128 | bytes 6291456 | tf_op jit(solution)/shard_map/dot_general | solution.py:276
  126.6 1.3 %add_convert_fusion.1 = bf16[512,1024]{1,0:T(8,128)(2,1)} fusion(f32[512,1024]{1,0:T(8,128)S(1)} %copy-done.4, f32[512,1024]{1,0:T(8,128)S(1)} %collective-permute-done.15), kind=kLoop, calls=%fused_computation.2 | loop fusion | flops 1048576 | bytes 5242880 | tf_op jit(solution)/shard_map/convert_element_type | solution.py:273
  (64 shorter events, 8.6 us)
Async XLA Ops:
  0.6 16.2 %copy-start = (bf16[1024,512]{1,0:T(8,128)(2,1)S(1)}, bf16[1024,512]{1,0:T(8,128)(2,1)}, u32[]{:S(2)}) copy-start(bf16[1024,512]{1,0:T(8,128)(2,1)} %param.9) | copy-start | bytes 3145732
  8.9 8.0 %copy-start.13 = (bf16[512,1024]{1,0:T(8,128)(2,1)S(1)}, bf16[512,1024]{1,0:T(8,128)(2,1)}, u32[]{:S(2)}) copy-start(bf16[512,1024]{1,0:T(8,128)(2,1)} %param.7) | copy-start | bytes 3145732
  8.9 16.2 %collective-permute-start = (bf16[512,4096]{1,0:T(8,128)(2,1)}, bf16[512,4096]{1,0:T(8,128)(2,1)}, u32[]{:S(2)}, u32[]{:S(2)}) collective-permute-start(bf16[512,4096]{1,0:T(8,128)(2,1)} %get-tuple-element.18), channel_id=1, source_target_pairs={{0,8},{1,9},{2,10},{3,11},{8,0},{9,1},{10,2},{11,3},{4,12},{5,13},... | collective-permute-start | bytes 12582920 | tf_op jit(solution)/shard_map/ppermute | solution.py:168
  12.6 28.3 %collective-permute-start.5 = (bf16[512,1024]{1,0:T(8,128)(2,1)}, bf16[512,1024]{1,0:T(8,128)(2,1)}, u32[]{:S(2)}, u32[]{:S(2)}) collective-permute-start(bf16[512,1024]{1,0:T(8,128)(2,1)} %bitcast.70), channel_id=1, source_target_pairs={{0,3},{1,0},{2,1},{3,2},{8,11},{9,8},{10,9},{11,10},{4,7},{5,4},{6... | collective-permute-start | bytes 3145736 | tf_op jit(solution)/shard_map/ppermute | solution.py:168
  15.2 26.4 %collective-permute-start.6 = (bf16[512,1024]{1,0:T(8,128)(2,1)}, bf16[512,1024]{1,0:T(8,128)(2,1)}, u32[]{:S(2)}, u32[]{:S(2)}) collective-permute-start(bf16[512,1024]{1,0:T(8,128)(2,1)} %bitcast.71), channel_id=1, source_target_pairs={{0,1},{1,2},{2,3},{3,0},{8,9},{9,10},{10,11},{11,8},{4,5},{5,6},{6... | collective-permute-start | bytes 3145736 | tf_op jit(solution)/shard_map/ppermute | solution.py:168
  15.2 26.4 %collective-permute-start.7 = (bf16[512,1024]{1,0:T(8,128)(2,1)}, bf16[512,1024]{1,0:T(8,128)(2,1)}, u32[]{:S(2)}, u32[]{:S(2)}) collective-permute-start(bf16[512,1024]{1,0:T(8,128)(2,1)} %bitcast.72), channel_id=1, source_target_pairs={{0,20},{1,21},{2,22},{3,23},{8,12},{9,13},{10,14},{11,15},{4,0},{5... | collective-permute-start | bytes 3145736 | tf_op jit(solution)/shard_map/ppermute | solution.py:178
  17.6 7.5 %collective-permute-start.1 = (bf16[512,512]{1,0:T(8,128)(2,1)S(1)}, bf16[512,512]{1,0:T(8,128)(2,1)S(1)}, u32[]{:S(2)}, u32[]{:S(2)}) collective-permute-start(bf16[512,512]{1,0:T(8,128)(2,1)S(1)} %convolution_convert_fusion), channel_id=1, source_target_pairs={{0,8},{1,9},{2,10},{3,11},{8,0},{9,1},{10,2},{11,3},{4,12},{5,13},... | collective-permute-start | bytes 1572872 | tf_op jit(solution)/shard_map/ppermute | solution.py:168
  32.2 37.0 %all-to-all-start = ((bf16[4,1024,256]{2,1,0:T(8,128)(2,1)}), bf16[4,1024,256]{2,1,0:T(8,128)(2,1)S(1)}, u32[]{:S(2)}, u32[]{:S(2)}) async-start(bf16[4,1024,256]{2,1,0:T(8,128)(2,1)} %bitcast.63), calls=%async_computation | async-start | bytes 4194304 | tf_op jit(solution)/shard_map/all_to_all | solution.py:182
  39.3 16.7 %collective-permute-start.4 = (bf16[16,64,256]{2,1,0:T(8,128)(2,1)}, bf16[16,64,256]{2,1,0:T(8,128)(2,1)}, u32[]{:S(2)}, u32[]{:S(2)}) collective-permute-start(bf16[16,64,256]{2,1,0:T(8,128)(2,1)} %bitcast.6.refs_5_), channel_id=1, source_target_pairs={{0,16},{1,17},{2,18},{3,19},{8,24},{9,25},{10,26},{11,27},{4,20},{... | collective-permute-start | bytes 1572872 | tf_op jit(solution)/shard_map/ppermute | solution.py:168
  40.1 22.9 %collective-permute-start.3 = (bf16[16,64,256]{2,1,0:T(8,128)(2,1)}, bf16[16,64,256]{2,1,0:T(8,128)(2,1)}, u32[]{:S(2)}, u32[]{:S(2)}) collective-permute-start(bf16[16,64,256]{2,1,0:T(8,128)(2,1)} %bitcast.5.refs_4_), channel_id=1, source_target_pairs={{0,20},{1,21},{2,22},{3,23},{8,28},{9,29},{10,30},{11,31},{4,0},{5... | collective-permute-start | bytes 1572872 | tf_op jit(solution)/shard_map/ppermute | solution.py:168
  40.9 25.3 %collective-permute-start.2 = (bf16[16,64,256]{2,1,0:T(8,128)(2,1)}, bf16[16,64,256]{2,1,0:T(8,128)(2,1)}, u32[]{:S(2)}, u32[]{:S(2)}) collective-permute-start(bf16[16,64,256]{2,1,0:T(8,128)(2,1)} %bitcast.4.refs_3_), channel_id=1, source_target_pairs={{0,4},{1,5},{2,6},{3,7},{8,12},{9,13},{10,14},{11,15},{4,16},{5,17... | collective-permute-start | bytes 1572872 | tf_op jit(solution)/shard_map/ppermute | solution.py:168
  41.6 34.3 %collective-permute-start.9 = (bf16[512,1024]{1,0:T(8,128)(2,1)}, bf16[512,1024]{1,0:T(8,128)(2,1)}, u32[]{:S(2)}, u32[]{:S(2)}) collective-permute-start(bf16[512,1024]{1,0:T(8,128)(2,1)} %get-tuple-element.22), channel_id=1, source_target_pairs={{0,3},{1,0},{2,1},{3,2},{8,11},{9,8},{10,9},{11,10},{4,7},{5,4},{6... | collective-permute-start | bytes 3145736 | tf_op jit(solution)/shard_map/ppermute | solution.py:168
  44.3 37.4 %collective-permute-start.10 = (bf16[512,1024]{1,0:T(8,128)(2,1)}, bf16[512,1024]{1,0:T(8,128)(2,1)}, u32[]{:S(2)}, u32[]{:S(2)}) collective-permute-start(bf16[512,1024]{1,0:T(8,128)(2,1)} %get-tuple-element.22), channel_id=1, source_target_pairs={{0,1},{1,2},{2,3},{3,0},{8,9},{9,10},{10,11},{11,8},{4,5},{5,6},{6... | collective-permute-start | bytes 3145736 | tf_op jit(solution)/shard_map/ppermute | solution.py:168
  46.6 19.6 %copy-start.3 = (bf16[4,1,4,1,64,256]{5,4,3,2,1,0:T(8,128)(2,1)S(1)}, bf16[4,1,4,1,64,256]{5,4,3,2,1,0:T(8,128)(2,1)}, u32[]{:S(2)}) copy-start(bf16[4,1,4,1,64,256]{5,4,3,2,1,0:T(8,128)(2,1)} %get-tuple-element.37) | copy-start | bytes 1572868
  68.7 15.8 %collective-permute-start.8 = (bf16[512,1024]{1,0:T(8,128)(2,1)}, bf16[512,1024]{1,0:T(8,128)(2,1)}, u32[]{:S(2)}, u32[]{:S(2)}) collective-permute-start(bf16[512,1024]{1,0:T(8,128)(2,1)} %get-tuple-element.24), channel_id=1, source_target_pairs={{0,3},{1,0},{2,1},{3,2},{8,9},{9,10},{10,11},{11,8},{4,7},{5,4},{6... | collective-permute-start | bytes 3145736 | tf_op jit(solution)/shard_map/ppermute | solution.py:178
  69.2 11.3 %all-to-all-start.1 = ((bf16[4,256,256]{2,1,0:T(8,128)(2,1)}), bf16[4,256,256]{2,1,0:T(8,128)(2,1)}, u32[]{:S(2)}, u32[]{:S(2)}) async-start(bf16[4,256,256]{2,1,0:T(8,128)(2,1)} %bitcast.64), calls=%async_computation.1 | async-start | bytes 1048576 | tf_op jit(solution)/shard_map/all_to_all | solution.py:182
  73.4 22.1 %copy-start.11 = (f32[64,512]{1,0:T(8,128)S(1)}, f32[64,512]{1,0:T(8,128)}, u32[]{:S(2)}) copy-start(f32[64,512]{1,0:T(8,128)} %param.10) | copy-start | bytes 393220
  73.4 22.1 %copy-start.12 = (f32[64,512]{1,0:T(8,128)S(1)}, f32[64,512]{1,0:T(8,128)}, u32[]{:S(2)}) copy-start(f32[64,512]{1,0:T(8,128)} %param.11) | copy-start | bytes 393220
  74.5 9.9 %copy-start.8 = (bf16[4,64,256]{2,1,0:T(8,128)(2,1)}, bf16[4,64,256]{2,1,0:T(8,128)(2,1)S(1)}, u32[]{:S(2)}) copy-start(bf16[4,64,256]{2,1,0:T(8,128)(2,1)S(1)} %get-tuple-element.45.refs_3_) | copy-start | bytes 393220
  74.5 9.9 %copy-start.9 = (bf16[4,64,256]{2,1,0:T(8,128)(2,1)}, bf16[4,64,256]{2,1,0:T(8,128)(2,1)S(1)}, u32[]{:S(2)}) copy-start(bf16[4,64,256]{2,1,0:T(8,128)(2,1)S(1)} %get-tuple-element.44.refs_4_) | copy-start | bytes 393220
  74.6 9.9 %copy-start.10 = (bf16[4,64,256]{2,1,0:T(8,128)(2,1)}, bf16[4,64,256]{2,1,0:T(8,128)(2,1)S(1)}, u32[]{:S(2)}) copy-start(bf16[4,64,256]{2,1,0:T(8,128)(2,1)S(1)} %get-tuple-element.43.refs_5_) | copy-start | bytes 393220
  74.6 10.0 %collective-permute-start.14 = (bf16[4,64,256]{2,1,0:T(8,128)(2,1)S(1)}, bf16[4,64,256]{2,1,0:T(8,128)(2,1)S(1)}, u32[]{:S(2)}, u32[]{:S(2)}) collective-permute-start(bf16[4,64,256]{2,1,0:T(8,128)(2,1)S(1)} %get-tuple-element.43.refs_5_), channel_id=1, source_target_pairs={{0,16},{1,17},{2,18},{3,19},{8,24},{9,25},{10,26},{11,27},{4,20},{... | collective-permute-start | bytes 393224 | tf_op jit(solution)/shard_map/ppermute | solution.py:168
  75.2 9.4 %collective-permute-start.13 = (bf16[4,64,256]{2,1,0:T(8,128)(2,1)S(1)}, bf16[4,64,256]{2,1,0:T(8,128)(2,1)S(1)}, u32[]{:S(2)}, u32[]{:S(2)}) collective-permute-start(bf16[4,64,256]{2,1,0:T(8,128)(2,1)S(1)} %get-tuple-element.44.refs_4_), channel_id=1, source_target_pairs={{0,20},{1,21},{2,22},{3,23},{8,28},{9,29},{10,30},{11,31},{4,0},{5... | collective-permute-start | bytes 393224 | tf_op jit(solution)/shard_map/ppermute | solution.py:168
  75.9 8.7 %collective-permute-start.12 = (bf16[4,64,256]{2,1,0:T(8,128)(2,1)S(1)}, bf16[4,64,256]{2,1,0:T(8,128)(2,1)S(1)}, u32[]{:S(2)}, u32[]{:S(2)}) collective-permute-start(bf16[4,64,256]{2,1,0:T(8,128)(2,1)S(1)} %get-tuple-element.45.refs_3_), channel_id=1, source_target_pairs={{0,4},{1,5},{2,6},{3,7},{8,12},{9,13},{10,14},{11,15},{4,16},{5,17... | collective-permute-start | bytes 393224 | tf_op jit(solution)/shard_map/ppermute | solution.py:168
  84.5 17.3 %collective-permute-start.11 = (bf16[512,1024]{1,0:T(8,128)(2,1)}, bf16[512,1024]{1,0:T(8,128)(2,1)S(1)}, u32[]{:S(2)}, u32[]{:S(2)}) collective-permute-start(bf16[512,1024]{1,0:T(8,128)(2,1)} %get-tuple-element.27), channel_id=1, source_target_pairs={{0,20},{1,21},{2,22},{3,23},{8,12},{9,13},{10,14},{11,15},{4,0},{5... | collective-permute-start | bytes 3145736 | tf_op jit(solution)/shard_map/ppermute | solution.py:178
  96.4 5.4 %copy-start.7 = (bf16[64,512]{1,0:T(8,128)(2,1)}, bf16[64,512]{1,0:T(8,128)(2,1)S(1)}, u32[]{:S(2)}) copy-start(bf16[64,512]{1,0:T(8,128)(2,1)S(1)} %get-tuple-element.32.refs_8_) | copy-start | bytes 196612
  97.2 17.0 %all-to-all-start.3 = ((bf16[8,64,512]{2,1,0:T(8,128)(2,1)}), bf16[8,64,512]{2,1,0:T(8,128)(2,1)S(1)}, u32[]{:S(2)}, u32[]{:S(2)}) async-start(bf16[8,64,512]{2,1,0:T(8,128)(2,1)} %broadcast_in_dim.2), calls=%async_computation.3 | async-start | bytes 1048576 | tf_op jit(solution)/shard_map/all_to_all | solution.py:182
  101.8 1.0 copy-start.6
  115.0 8.9 %copy-start.5 = (bf16[1024,1024]{1,0:T(8,128)(2,1)S(1)}, bf16[1024,1024]{1,0:T(8,128)(2,1)}, u32[]{:S(2)}) copy-start(bf16[1024,1024]{1,0:T(8,128)(2,1)} %param.8) | copy-start | bytes 6291460
  115.0 11.6 %collective-permute-start.15 = (f32[512,1024]{1,0:T(8,128)}, f32[512,1024]{1,0:T(8,128)S(1)}, u32[]{:S(2)}, u32[]{:S(2)}) collective-permute-start(f32[512,1024]{1,0:T(8,128)} %together.7), channel_id=1, source_target_pairs={{0,8},{1,9},{2,10},{3,11},{8,0},{9,1},{10,2},{11,3},{4,12},{5,13},... | collective-permute-start | bytes 6291464 | tf_op jit(solution)/shard_map/ppermute | solution.py:168
  117.9 4.7 %collective-permute-start.16 = (bf16[8,64,512]{2,1,0:T(8,128)(2,1)}, bf16[8,64,512]{2,1,0:T(8,128)(2,1)S(1)}, u32[]{:S(2)}, u32[]{:S(2)}) collective-permute-start(bf16[8,64,512]{2,1,0:T(8,128)(2,1)} %copy-done.1), channel_id=1, source_target_pairs={{0,8},{1,9},{2,10},{3,11},{8,0},{9,1},{10,2},{11,3},{4,12},{5,13},... | collective-permute-start | bytes 1572872 | tf_op jit(solution)/shard_map/ppermute | solution.py:168
  124.0 2.7 %copy-start.4 = (f32[512,1024]{1,0:T(8,128)S(1)}, f32[512,1024]{1,0:T(8,128)}, u32[]{:S(2)}) copy-start(f32[512,1024]{1,0:T(8,128)} %get-tuple-element.30) | copy-start | bytes 6291460
  (2 other events, 1.6 us)

commit v6 on v5

--- a/solution.py
+++ b/solution.py
@@ -238,9 +238,9 @@
 
     first = partial[:, : rank // 2].reshape(4, -1, rank // 2)
     first = sum_all(exchange(first, along_y)).astype(jnp.bfloat16)
-    second = partial[:, rank // 2 :].reshape(4, LO, X, 2, ROWS, rank // 2)
-    others = [(step, take(second, step)) for step in (1, 3, 2)]
-    second = sum_z(take(second, 0), others)
+    second = partial.reshape(4, LO, X, 2, ROWS, rank)
+    others = [(step, take(second, step)[:, :, rank // 2 :]) for step in (1, 3, 2)]
+    second = sum_z(take(second, 0)[:, :, rank // 2 :], others)
     w_up, w_down, w_z = together(w_up, w_down, w_z, after=[part for _, part in others])
     zx_up = move(w_z, x=-1)
     zx_down = move(w_z, x=1)

time: 129 us -> 132 us (1.023)
  local copies, waits for them, and re-layouts: 8.73 us -> 13.2 us
  waiting for transfers between devices: 21.6 us -> 20.1 us
    slice x0 -> x3, local copies, waits for them, and re-layouts: none -> 2.56 us  [local(): take(second, step)[:, :, rank // 2:]]
    unnamed x28, local copies, waits for them, and re-layouts: 2.58 us -> 4.62 us
    ppermute x14, waiting for transfers between devices: 15 us -> 13.4 us  [move(): lax.ppermute(array, AXES, [(device(*at), device(at[0] + x, at[1] + y, at[...]
  transfers between devices with their start and end apart: 20 -> 20, of which waited for: 5 -> 5; matrix products, arithmetic and copies ran while one was open for 22% -> 24% of each run, Pallas kernels for 18% -> 18%
where the time goes in v6:
time: 132 us; the launch traced here: 131 us
  starting transfers between devices  31.9 us (24%)
  Pallas kernels  31.4 us (24%)
  waiting for transfers between devices  20.1 us (15%)
  local copies, waits for them, and re-layouts  13.2 us (10%)
  matrix products  12.8 us (10%)
  other arithmetic  10.7 us (8%)
  blocking collectives  9.96 us (8%)
    pallas_call x2, Pallas kernels, keys_of(): pl.pallas_call(body, grid_spec=pltpu.PrefetchScalarGridSpec(num_scalar_pr...  20.8 us
    ppermute x14, starting transfers between devices, move(): lax.ppermute(array, AXES, [(device(*at), device(at[0] + x, at[1] + y, at[...  16.8 us
    ppermute x14, waiting for transfers between devices, move(): lax.ppermute(array, AXES, [(device(*at), device(at[0] + x, at[1] + y, at[...  13.4 us
    all_to_all x3, starting transfers between devices, exchange(): lax.all_to_all(array, AXES, split_axis=0, concat_axis=0, axis_index_group...  13 us
    all_to_all x1, blocking collectives, exchange(): lax.all_to_all(array, AXES, split_axis=0, concat_axis=0, axis_index_group...  9.96 us
    pallas_call x1, Pallas kernels, pack_columns(): pl.pallas_call(body, grid_spec=pltpu.PrefetchScalarGridSpec(num_scalar_pr...  8.2 us
    dot_general x1, matrix products, local(): lax.dot_general(other, low_other, contract, preferred_element_type=jnp.fl...  4.85 us
    dot_general x1, matrix products, local(): lax.dot_general(own, low, contract, preferred_element_type=jnp.float32)  4.63 us
  transfers between devices with their start and end apart: 20, of which 5 were waited for; matrix products, arithmetic and copies ran while one was open for 24% of the time, Pallas kernels for 18%

profile of v6, /device:TPU:1, one launch (start us, length us, event | category | flops | bytes accessed | tf_op | source)
XLA Modules:
  0.0 131.0 jit_solution(5669267604118033437)
XLA Ops:
  0.7 8.2 %pack_columns.1 = (bf16[512,4096]{1,0:T(8,128)(2,1)}, bf16[512,4096]{1,0:T(8,128)(2,1)}) custom-call(s32[1]{0:T(128)} %bitcast.1.place_ref, bf16[512,8192]{1,0:T(8,128)(2,1)} %x_ref.1), custom_call_target="tpu_custom_call" | custom-call | flops 1 | bytes 1 | tf_op jit(solution)/shard_map/pack_columns/pallas_call | solution.py:41
  8.9 1.4 %collective-permute-start = (bf16[512,4096]{1,0:T(8,128)(2,1)}, bf16[512,4096]{1,0:T(8,128)(2,1)}, u32[]{:S(2)}, u32[]{:S(2)}) collective-permute-start(bf16[512,4096]{1,0:T(8,128)(2,1)} %get-tuple-element.18), channel_id=1, source_target_pairs={{0,8},{1,9},{2,10},{3,11},{8,0},{9,1},{10,2},{11,3},{4,12},{5,13},... | collective-permute-start | bytes 12582920 | tf_op jit(solution)/shard_map/ppermute | solution.py:168
  10.2 2.4 %pack_rows.1 = bf16[8,64,1024]{2,1,0:T(8,128)(2,1)} custom-call(s32[1]{0:T(128)} %bitcast.1.place_ref, bf16[8,2,64,1024]{3,2,1,0:T(8,128)(2,1)} %bitcast.69, bf16[512,4096]{1,0:T(8,128)(2,1)} %get-tuple-element.19.after_ref.refs_1_), custom_call_target="tpu_custom_call" | custom-call | flops 1 | bytes 1 | tf_op jit(solution)/shard_map/pack_rows/pallas_call | solution.py:64
  12.7 2.6 %collective-permute-start.5 = (bf16[512,1024]{1,0:T(8,128)(2,1)}, bf16[512,1024]{1,0:T(8,128)(2,1)}, u32[]{:S(2)}, u32[]{:S(2)}) collective-permute-start(bf16[512,1024]{1,0:T(8,128)(2,1)} %bitcast.72), channel_id=1, source_target_pairs={{0,3},{1,0},{2,1},{3,2},{8,11},{9,8},{10,9},{11,10},{4,7},{5,4},{6... | collective-permute-start | bytes 3145736 | tf_op jit(solution)/shard_map/ppermute | solution.py:168
  15.2 1.6 %collective-permute-start.7 = (bf16[512,1024]{1,0:T(8,128)(2,1)}, bf16[512,1024]{1,0:T(8,128)(2,1)}, u32[]{:S(2)}, u32[]{:S(2)}) collective-permute-start(bf16[512,1024]{1,0:T(8,128)(2,1)} %bitcast.74), channel_id=1, source_target_pairs={{0,20},{1,21},{2,22},{3,23},{8,12},{9,13},{10,14},{11,15},{4,0},{5... | collective-permute-start | bytes 3145736 | tf_op jit(solution)/shard_map/ppermute | solution.py:178
  17.6 2.8 %collective-permute-start.1 = (bf16[512,512]{1,0:T(8,128)(2,1)S(1)}, bf16[512,512]{1,0:T(8,128)(2,1)S(1)}, u32[]{:S(2)}, u32[]{:S(2)}) collective-permute-start(bf16[512,512]{1,0:T(8,128)(2,1)S(1)} %convolution_convert_fusion), channel_id=1, source_target_pairs={{0,8},{1,9},{2,10},{3,11},{8,0},{9,1},{10,2},{11,3},{4,12},{5,13},... | collective-permute-start | bytes 1572872 | tf_op jit(solution)/shard_map/ppermute | solution.py:168
  20.4 4.6 %fusion.7 = f32[4096,512]{1,0:T(8,128)S(1)} fusion(bf16[512,4096]{1,0:T(8,128)(2,1)} %get-tuple-element.19.after_ref.refs_1_, bf16[512,512]{1,0:T(8,128)(2,1)S(1)} %convolution_convert_fusion), kind=kOutput, calls=%fused_computation.29 | convolution fusion | flops 2147483648 | bytes 13107200 | tf_op jit(solution)/shard_map/dot_general | solution.py:217
  25.1 4.9 %add_convert_fusion = bf16[4096,512]{1,0:T(8,128)(2,1)S(1)} fusion(f32[4096,512]{1,0:T(8,128)S(1)} %fusion.7, bf16[512,4096]{1,0:T(8,128)(2,1)} %collective-permute-done.refs_0_, bf16[512,512]{1,0:T(8,128)(2,1)S(1)} %collective-permute-done.1), kind=kOutput, calls=%fused_computation | convolution fusion | flops 2151677952 | bytes 17301504 | tf_op jit(solution)/shard_map/dot_general | solution.py:218
  30.0 2.0 %copy-done.1 = bf16[4096,512]{1,0:T(8,128)(2,1)} copy-done((bf16[4096,512]{1,0:T(8,128)(2,1)}, bf16[4096,512]{1,0:T(8,128)(2,1)S(1)}, u32[]{:S(2)}) %copy-start.1) | copy-done | bytes 4194328
  32.0 1.4 %slice.72 = bf16[4096,256]{1,0:T(8,128)(2,1)} slice(bf16[4096,512]{1,0:T(8,128)(2,1)S(1)} %add_convert_fusion), slice={[0:4096], [0:256]} | slice | bytes 4194304 | tf_op jit(solution)/shard_map/slice | solution.py:239
  33.4 4.2 %all-to-all-start = ((bf16[4,1024,256]{2,1,0:T(8,128)(2,1)}), bf16[4,1024,256]{2,1,0:T(8,128)(2,1)S(1)}, u32[]{:S(2)}, u32[]{:S(2)}) async-start(bf16[4,1024,256]{2,1,0:T(8,128)(2,1)} %bitcast.61), calls=%async_computation | async-start | bytes 4194304 | tf_op jit(solution)/shard_map/all_to_all | solution.py:182
  37.6 3.6 %constant_dynamic-slice_fusion.3 = (bf16[4,1,4,1,64,512]{5,4,3,2,1,0:T(8,128)(2,1)}, bf16[4,1,4,1,64,512]{5,4,3,2,1,0:T(8,128)(2,1)S(1)}, bf16[4,1,4,1,64,512]{5...) fusion(bf16[4,2,4,2,64,512]{5,4,3,2,1,0:T(8,128)(2,1)} %bitcast.60, s32[]{:T(128)S(6)} %select_n.157, ...), kind=kLoop, calls=%fused_computation.28 | loop fusion | bytes 8388640 | tf_op jit(solution)/shard_map/dynamic_slice | solution.py:230
  46.1 2.7 %collective-permute-start.9 = (bf16[512,1024]{1,0:T(8,128)(2,1)}, bf16[512,1024]{1,0:T(8,128)(2,1)}, u32[]{:S(2)}, u32[]{:S(2)}) collective-permute-start(bf16[512,1024]{1,0:T(8,128)(2,1)} %get-tuple-element.22), channel_id=1, source_target_pairs={{0,3},{1,0},{2,1},{3,2},{8,11},{9,8},{10,9},{11,10},{4,7},{5,4},{6... | collective-permute-start | bytes 3145736 | tf_op jit(solution)/shard_map/ppermute | solution.py:168
  48.8 2.3 %broadcast_select_fusion.refs_1_ = bf16[512,1024]{1,0:T(8,128)(2,1)} fusion(bf16[512,1024]{1,0:T(8,128)(2,1)} %get-tuple-element.20, bf16[512,1024]{1,0:T(8,128)(2,1)} %get-tuple-element.21, pred[]{:T(512)S(6)} %eq.24), kind=kLoop, calls=%fused_computation.7 | loop fusion | flops 524288 | bytes 3145729 | tf_op jit(solution)/shard_map/jit(_where)/select_n | solution.py:250
  51.1 9.2 %keys_of.2 = (f32[512,1024]{1,0:T(8,128)}, f32[512,1024]{1,0:T(8,128)}) custom-call(s32[1]{0:T(128)} %bitcast.shard_ref, bf16[512,4096]{1,0:T(8,128)(2,1)} %collective-permute-done.refs_0_, bf16[512,4096]{1,0:T(8,128)(2,1)} %get-tuple-element.19.after_ref.refs_1_, bf16[4,128,1024]{2,1,0:T(8,128)(2,1)} %bitcast.75, bf16[4,128,1024]{2,1,0:T(8,128)(2,1)} %bitcast.10.refs_3_, ...), custom_call_target="tpu_custom_call" | custom-call | flops 4294967296 | bytes 8388608 | tf_op jit(solution)/shard_map/keys_of/pallas_call | solution.py:119
  60.4 5.5 %collective-permute-done.3 = bf16[16,64,256]{2,1,0:T(8,128)(2,1)} collective-permute-done((bf16[16,64,256]{2,1,0:T(8,128)(2,1)}, bf16[16,64,256]{2,1,0:T(8,128)(2,1)}, u32[]{:S(2)}, u32[]{:S(2)}) %collective-permute-start.3) | collective-permute-done | bytes 524320 | tf_op jit(solution)/shard_map/ppermute | solution.py:168
  65.9 3.2 %collective-permute-done.2 = bf16[16,64,256]{2,1,0:T(8,128)(2,1)} collective-permute-done((bf16[16,64,256]{2,1,0:T(8,128)(2,1)}, bf16[16,64,256]{2,1,0:T(8,128)(2,1)}, u32[]{:S(2)}, u32[]{:S(2)}) %collective-permute-start.2) | collective-permute-done | bytes 524320 | tf_op jit(solution)/shard_map/ppermute | solution.py:168
  69.0 2.7 %add_convert_fusion.3.refs_0_ = bf16[16,64,256]{2,1,0:T(8,128)(2,1)} fusion(bf16[16,64,256]{2,1,0:T(8,128)(2,1)} %collective-permute-done.4, bf16[16,64,256]{2,1,0:T(8,128)(2,1)} %collective-permute-done.3, bf16[16,64,256]{2,1,0:T(8,128)(2,1)} %collective-permute-done.2, bf16[16,64,512]{2,1,0:T(8,128)(2,1)} %bitcast.63), kind=kLoop, calls=%fused_computation.6 | loop fusion | flops 2097152 | bytes 2621440 | tf_op jit(solution)/shard_map/convert_element_type | solution.py:237
  72.2 4.2 %all-to-all-start.1 = ((bf16[4,256,256]{2,1,0:T(8,128)(2,1)}), bf16[4,256,256]{2,1,0:T(8,128)(2,1)}, u32[]{:S(2)}, u32[]{:S(2)}) async-start(bf16[4,256,256]{2,1,0:T(8,128)(2,1)} %bitcast.62), calls=%async_computation.1 | async-start | bytes 1048576 | tf_op jit(solution)/shard_map/all_to_all | solution.py:182
  79.6 3.8 %all-to-all-done.1 = bf16[4,256,256]{2,1,0:T(8,128)(2,1)} async-done(((bf16[4,256,256]{2,1,0:T(8,128)(2,1)}), bf16[4,256,256]{2,1,0:T(8,128)(2,1)}, u32[]{:S(2)}, u32[]{:S(2)}) %all-to-all-start.1) | async-done | bytes 524320 | tf_op jit(solution)/shard_map/all_to_all | solution.py:182
  83.4 1.2 add_convert_fusion.4
  84.6 2.8 %collective-permute-done.8.refs_0_ = bf16[512,1024]{1,0:T(8,128)(2,1)} collective-permute-done((bf16[512,1024]{1,0:T(8,128)(2,1)}, bf16[512,1024]{1,0:T(8,128)(2,1)}, u32[]{:S(2)}, u32[]{:S(2)}) %collective-permute-start.8) | collective-permute-done | bytes 1048608 | tf_op jit(solution)/shard_map/ppermute | solution.py:178
  87.6 1.0 fusion.2
  88.6 10.0 %all_to_all.20 = bf16[4,64,512]{2,1,0:T(8,128)(2,1)S(1)} all-to-all(bf16[4,64,512]{2,1,0:T(8,128)(2,1)S(1)} %pad_maximum_fusion.1), channel_id=1, replica_groups={{0,1,2,3},{8,9,10,11},{4,5,6,7},{12,13,14,15},{16,17,18,19},{24,25,26,2..., dimensions={0} | all-to-all | bytes 524288 | tf_op jit(solution)/shard_map/all_to_all | solution.py:182
  100.2 4.6 %all-to-all-start.3 = ((bf16[8,64,512]{2,1,0:T(8,128)(2,1)}), bf16[8,64,512]{2,1,0:T(8,128)(2,1)S(1)}, u32[]{:S(2)}, u32[]{:S(2)}) async-start(bf16[8,64,512]{2,1,0:T(8,128)(2,1)} %broadcast_in_dim.2), calls=%async_computation.3 | async-start | bytes 1048576 | tf_op jit(solution)/shard_map/all_to_all | solution.py:182
  104.8 1.0 copy-done.6
  105.7 11.5 %keys_of.3 = (f32[512,1024]{1,0:T(8,128)}, f32[512,1024]{1,0:T(8,128)}) custom-call(s32[1]{0:T(128)} %bitcast.shard_ref, bf16[512,4096]{1,0:T(8,128)(2,1)} %collective-permute-done.refs_0_, bf16[512,4096]{1,0:T(8,128)(2,1)} %get-tuple-element.19.after_ref.refs_1_, bf16[4,128,1024]{2,1,0:T(8,128)(2,1)} %bitcast.18.refs_2_, ...), custom_call_target="tpu_custom_call" | custom-call | flops 1 | bytes 1 | tf_op jit(solution)/shard_map/keys_of/pallas_call | solution.py:119
  118.1 2.9 %collective-permute-start.15 = (f32[512,1024]{1,0:T(8,128)}, f32[512,1024]{1,0:T(8,128)S(1)}, u32[]{:S(2)}, u32[]{:S(2)}) collective-permute-start(f32[512,1024]{1,0:T(8,128)} %together.7), channel_id=1, source_target_pairs={{0,8},{1,9},{2,10},{3,11},{8,0},{9,1},{10,2},{11,3},{4,12},{5,13},... | collective-permute-start | bytes 6291464 | tf_op jit(solution)/shard_map/ppermute | solution.py:168
  121.0 4.7 %collective-permute-done.16 = bf16[8,64,512]{2,1,0:T(8,128)(2,1)S(1)} collective-permute-done((bf16[8,64,512]{2,1,0:T(8,128)(2,1)}, bf16[8,64,512]{2,1,0:T(8,128)(2,1)S(1)}, u32[]{:S(2)}, u32[]{:S(2)}) %collective-permute-start.16) | collective-permute-done | bytes 524320 | tf_op jit(solution)/shard_map/ppermute | solution.py:168
  125.7 1.1 select_bitcast_fusion.1
  127.1 2.6 %subtract_convert_fusion = bf16[1024,1024]{1,0:T(8,128)(2,1)} fusion(bf16[1024,1024]{1,0:T(8,128)(2,1)S(1)} %copy-done.5, bf16[1024,512]{1,0:T(8,128)(2,1)S(1)} %bitcast.71, bf16[1024,512]{1,0:T(8,128)(2,1)S(1)} %copy-done), kind=kOutput, calls=%fused_computation.1 | convolution fusion | flops 1077936128 | bytes 6291456 | tf_op jit(solution)/shard_map/dot_general | solution.py:276
  129.7 1.3 add_convert_fusion.1
  (67 shorter events, 12.0 us)
Async XLA Ops:
  0.6 16.3 %copy-start = (bf16[1024,512]{1,0:T(8,128)(2,1)S(1)}, bf16[1024,512]{1,0:T(8,128)(2,1)}, u32[]{:S(2)}) copy-start(bf16[1024,512]{1,0:T(8,128)(2,1)} %param.9) | copy-start | bytes 3145732
  8.9 8.0 %copy-start.13 = (bf16[512,1024]{1,0:T(8,128)(2,1)S(1)}, bf16[512,1024]{1,0:T(8,128)(2,1)}, u32[]{:S(2)}) copy-start(bf16[512,1024]{1,0:T(8,128)(2,1)} %param.7) | copy-start | bytes 3145732
  8.9 16.2 %collective-permute-start = (bf16[512,4096]{1,0:T(8,128)(2,1)}, bf16[512,4096]{1,0:T(8,128)(2,1)}, u32[]{:S(2)}, u32[]{:S(2)}) collective-permute-start(bf16[512,4096]{1,0:T(8,128)(2,1)} %get-tuple-element.18), channel_id=1, source_target_pairs={{0,8},{1,9},{2,10},{3,11},{8,0},{9,1},{10,2},{11,3},{4,12},{5,13},... | collective-permute-start | bytes 12582920 | tf_op jit(solution)/shard_map/ppermute | solution.py:168
  12.7 32.7 %collective-permute-start.5 = (bf16[512,1024]{1,0:T(8,128)(2,1)}, bf16[512,1024]{1,0:T(8,128)(2,1)}, u32[]{:S(2)}, u32[]{:S(2)}) collective-permute-start(bf16[512,1024]{1,0:T(8,128)(2,1)} %bitcast.72), channel_id=1, source_target_pairs={{0,3},{1,0},{2,1},{3,2},{8,11},{9,8},{10,9},{11,10},{4,7},{5,4},{6... | collective-permute-start | bytes 3145736 | tf_op jit(solution)/shard_map/ppermute | solution.py:168
  15.2 30.9 %collective-permute-start.6 = (bf16[512,1024]{1,0:T(8,128)(2,1)}, bf16[512,1024]{1,0:T(8,128)(2,1)}, u32[]{:S(2)}, u32[]{:S(2)}) collective-permute-start(bf16[512,1024]{1,0:T(8,128)(2,1)} %bitcast.73), channel_id=1, source_target_pairs={{0,1},{1,2},{2,3},{3,0},{8,9},{9,10},{10,11},{11,8},{4,5},{5,6},{6... | collective-permute-start | bytes 3145736 | tf_op jit(solution)/shard_map/ppermute | solution.py:168
  15.2 30.9 %collective-permute-start.7 = (bf16[512,1024]{1,0:T(8,128)(2,1)}, bf16[512,1024]{1,0:T(8,128)(2,1)}, u32[]{:S(2)}, u32[]{:S(2)}) collective-permute-start(bf16[512,1024]{1,0:T(8,128)(2,1)} %bitcast.74), channel_id=1, source_target_pairs={{0,20},{1,21},{2,22},{3,23},{8,12},{9,13},{10,14},{11,15},{4,0},{5... | collective-permute-start | bytes 3145736 | tf_op jit(solution)/shard_map/ppermute | solution.py:178
  17.6 7.5 %collective-permute-start.1 = (bf16[512,512]{1,0:T(8,128)(2,1)S(1)}, bf16[512,512]{1,0:T(8,128)(2,1)S(1)}, u32[]{:S(2)}, u32[]{:S(2)}) collective-permute-start(bf16[512,512]{1,0:T(8,128)(2,1)S(1)} %convolution_convert_fusion), channel_id=1, source_target_pairs={{0,8},{1,9},{2,10},{3,11},{8,0},{9,1},{10,2},{11,3},{4,12},{5,13},... | collective-permute-start | bytes 1572872 | tf_op jit(solution)/shard_map/ppermute | solution.py:168
  30.0 2.0 %copy-start.1 = (bf16[4096,512]{1,0:T(8,128)(2,1)}, bf16[4096,512]{1,0:T(8,128)(2,1)S(1)}, u32[]{:S(2)}) copy-start(bf16[4096,512]{1,0:T(8,128)(2,1)S(1)} %add_convert_fusion) | copy-start | bytes 12582916
  33.4 38.7 %all-to-all-start = ((bf16[4,1024,256]{2,1,0:T(8,128)(2,1)}), bf16[4,1024,256]{2,1,0:T(8,128)(2,1)S(1)}, u32[]{:S(2)}, u32[]{:S(2)}) async-start(bf16[4,1024,256]{2,1,0:T(8,128)(2,1)} %bitcast.61), calls=%async_computation | async-start | bytes 4194304 | tf_op jit(solution)/shard_map/all_to_all | solution.py:182
  42.1 18.2 %collective-permute-start.4 = (bf16[16,64,256]{2,1,0:T(8,128)(2,1)}, bf16[16,64,256]{2,1,0:T(8,128)(2,1)}, u32[]{:S(2)}, u32[]{:S(2)}) collective-permute-start(bf16[16,64,256]{2,1,0:T(8,128)(2,1)} %slice.71.refs_5_), channel_id=1, source_target_pairs={{0,16},{1,17},{2,18},{3,19},{8,24},{9,25},{10,26},{11,27},{4,20},{... | collective-permute-start | bytes 1572872 | tf_op jit(solution)/shard_map/ppermute | solution.py:168
  43.8 22.1 %collective-permute-start.3 = (bf16[16,64,256]{2,1,0:T(8,128)(2,1)}, bf16[16,64,256]{2,1,0:T(8,128)(2,1)}, u32[]{:S(2)}, u32[]{:S(2)}) collective-permute-start(bf16[16,64,256]{2,1,0:T(8,128)(2,1)} %slice.70.refs_4_), channel_id=1, source_target_pairs={{0,20},{1,21},{2,22},{3,23},{8,28},{9,29},{10,30},{11,31},{4,0},{5... | collective-permute-start | bytes 1572872 | tf_op jit(solution)/shard_map/ppermute | solution.py:168
  45.4 23.6 %collective-permute-start.2 = (bf16[16,64,256]{2,1,0:T(8,128)(2,1)}, bf16[16,64,256]{2,1,0:T(8,128)(2,1)}, u32[]{:S(2)}, u32[]{:S(2)}) collective-permute-start(bf16[16,64,256]{2,1,0:T(8,128)(2,1)} %slice.69.refs_3_), channel_id=1, source_target_pairs={{0,4},{1,5},{2,6},{3,7},{8,12},{9,13},{10,14},{11,15},{4,16},{5,17... | collective-permute-start | bytes 1572872 | tf_op jit(solution)/shard_map/ppermute | solution.py:168
  46.1 32.8 %collective-permute-start.9 = (bf16[512,1024]{1,0:T(8,128)(2,1)}, bf16[512,1024]{1,0:T(8,128)(2,1)}, u32[]{:S(2)}, u32[]{:S(2)}) collective-permute-start(bf16[512,1024]{1,0:T(8,128)(2,1)} %get-tuple-element.22), channel_id=1, source_target_pairs={{0,3},{1,0},{2,1},{3,2},{8,11},{9,8},{10,9},{11,10},{4,7},{5,4},{6... | collective-permute-start | bytes 3145736 | tf_op jit(solution)/shard_map/ppermute | solution.py:168
  48.8 35.8 %collective-permute-start.10 = (bf16[512,1024]{1,0:T(8,128)(2,1)}, bf16[512,1024]{1,0:T(8,128)(2,1)}, u32[]{:S(2)}, u32[]{:S(2)}) collective-permute-start(bf16[512,1024]{1,0:T(8,128)(2,1)} %get-tuple-element.22), channel_id=1, source_target_pairs={{0,1},{1,2},{2,3},{3,0},{8,9},{9,10},{10,11},{11,8},{4,5},{5,6},{6... | collective-permute-start | bytes 3145736 | tf_op jit(solution)/shard_map/ppermute | solution.py:168
  71.7 15.8 %collective-permute-start.8 = (bf16[512,1024]{1,0:T(8,128)(2,1)}, bf16[512,1024]{1,0:T(8,128)(2,1)}, u32[]{:S(2)}, u32[]{:S(2)}) collective-permute-start(bf16[512,1024]{1,0:T(8,128)(2,1)} %get-tuple-element.24), channel_id=1, source_target_pairs={{0,3},{1,0},{2,1},{3,2},{8,9},{9,10},{10,11},{11,8},{4,7},{5,4},{6... | collective-permute-start | bytes 3145736 | tf_op jit(solution)/shard_map/ppermute | solution.py:178
  72.2 11.3 %all-to-all-start.1 = ((bf16[4,256,256]{2,1,0:T(8,128)(2,1)}), bf16[4,256,256]{2,1,0:T(8,128)(2,1)}, u32[]{:S(2)}, u32[]{:S(2)}) async-start(bf16[4,256,256]{2,1,0:T(8,128)(2,1)} %bitcast.62), calls=%async_computation.1 | async-start | bytes 1048576 | tf_op jit(solution)/shard_map/all_to_all | solution.py:182
  76.4 22.1 %copy-start.11 = (f32[64,512]{1,0:T(8,128)S(1)}, f32[64,512]{1,0:T(8,128)}, u32[]{:S(2)}) copy-start(f32[64,512]{1,0:T(8,128)} %param.10) | copy-start | bytes 393220
  76.4 22.1 %copy-start.12 = (f32[64,512]{1,0:T(8,128)S(1)}, f32[64,512]{1,0:T(8,128)}, u32[]{:S(2)}) copy-start(f32[64,512]{1,0:T(8,128)} %param.11) | copy-start | bytes 393220
  77.5 9.9 %copy-start.8 = (bf16[4,64,256]{2,1,0:T(8,128)(2,1)}, bf16[4,64,256]{2,1,0:T(8,128)(2,1)S(1)}, u32[]{:S(2)}) copy-start(bf16[4,64,256]{2,1,0:T(8,128)(2,1)S(1)} %get-tuple-element.43.refs_3_) | copy-start | bytes 393220
  77.5 9.9 %copy-start.9 = (bf16[4,64,256]{2,1,0:T(8,128)(2,1)}, bf16[4,64,256]{2,1,0:T(8,128)(2,1)S(1)}, u32[]{:S(2)}) copy-start(bf16[4,64,256]{2,1,0:T(8,128)(2,1)S(1)} %get-tuple-element.42.refs_4_) | copy-start | bytes 393220
  77.5 9.9 %copy-start.10 = (bf16[4,64,256]{2,1,0:T(8,128)(2,1)}, bf16[4,64,256]{2,1,0:T(8,128)(2,1)S(1)}, u32[]{:S(2)}) copy-start(bf16[4,64,256]{2,1,0:T(8,128)(2,1)S(1)} %get-tuple-element.41.refs_5_) | copy-start | bytes 393220
  77.5 10.0 %collective-permute-start.14 = (bf16[4,64,256]{2,1,0:T(8,128)(2,1)S(1)}, bf16[4,64,256]{2,1,0:T(8,128)(2,1)S(1)}, u32[]{:S(2)}, u32[]{:S(2)}) collective-permute-start(bf16[4,64,256]{2,1,0:T(8,128)(2,1)S(1)} %get-tuple-element.41.refs_5_), channel_id=1, source_target_pairs={{0,16},{1,17},{2,18},{3,19},{8,24},{9,25},{10,26},{11,27},{4,20},{... | collective-permute-start | bytes 393224 | tf_op jit(solution)/shard_map/ppermute | solution.py:168
  78.2 9.4 %collective-permute-start.13 = (bf16[4,64,256]{2,1,0:T(8,128)(2,1)S(1)}, bf16[4,64,256]{2,1,0:T(8,128)(2,1)S(1)}, u32[]{:S(2)}, u32[]{:S(2)}) collective-permute-start(bf16[4,64,256]{2,1,0:T(8,128)(2,1)S(1)} %get-tuple-element.42.refs_4_), channel_id=1, source_target_pairs={{0,20},{1,21},{2,22},{3,23},{8,28},{9,29},{10,30},{11,31},{4,0},{5... | collective-permute-start | bytes 393224 | tf_op jit(solution)/shard_map/ppermute | solution.py:168
  78.9 8.7 %collective-permute-start.12 = (bf16[4,64,256]{2,1,0:T(8,128)(2,1)S(1)}, bf16[4,64,256]{2,1,0:T(8,128)(2,1)S(1)}, u32[]{:S(2)}, u32[]{:S(2)}) collective-permute-start(bf16[4,64,256]{2,1,0:T(8,128)(2,1)S(1)} %get-tuple-element.43.refs_3_), channel_id=1, source_target_pairs={{0,4},{1,5},{2,6},{3,7},{8,12},{9,13},{10,14},{11,15},{4,16},{5,17... | collective-permute-start | bytes 393224 | tf_op jit(solution)/shard_map/ppermute | solution.py:168
  87.5 17.3 %collective-permute-start.11 = (bf16[512,1024]{1,0:T(8,128)(2,1)}, bf16[512,1024]{1,0:T(8,128)(2,1)S(1)}, u32[]{:S(2)}, u32[]{:S(2)}) collective-permute-start(bf16[512,1024]{1,0:T(8,128)(2,1)} %get-tuple-element.27), channel_id=1, source_target_pairs={{0,20},{1,21},{2,22},{3,23},{8,12},{9,13},{10,14},{11,15},{4,0},{5... | collective-permute-start | bytes 3145736 | tf_op jit(solution)/shard_map/ppermute | solution.py:178
  99.4 5.4 %copy-start.7 = (bf16[64,512]{1,0:T(8,128)(2,1)}, bf16[64,512]{1,0:T(8,128)(2,1)S(1)}, u32[]{:S(2)}) copy-start(bf16[64,512]{1,0:T(8,128)(2,1)S(1)} %get-tuple-element.32.refs_8_) | copy-start | bytes 196612
  100.2 17.1 %all-to-all-start.3 = ((bf16[8,64,512]{2,1,0:T(8,128)(2,1)}), bf16[8,64,512]{2,1,0:T(8,128)(2,1)S(1)}, u32[]{:S(2)}, u32[]{:S(2)}) async-start(bf16[8,64,512]{2,1,0:T(8,128)(2,1)} %broadcast_in_dim.2), calls=%async_computation.3 | async-start | bytes 1048576 | tf_op jit(solution)/shard_map/all_to_all | solution.py:182
  104.8 1.0 copy-start.6
  118.1 8.9 %copy-start.5 = (bf16[1024,1024]{1,0:T(8,128)(2,1)S(1)}, bf16[1024,1024]{1,0:T(8,128)(2,1)}, u32[]{:S(2)}) copy-start(bf16[1024,1024]{1,0:T(8,128)(2,1)} %param.8) | copy-start | bytes 6291460
  118.1 11.6 %collective-permute-start.15 = (f32[512,1024]{1,0:T(8,128)}, f32[512,1024]{1,0:T(8,128)S(1)}, u32[]{:S(2)}, u32[]{:S(2)}) collective-permute-start(f32[512,1024]{1,0:T(8,128)} %together.7), channel_id=1, source_target_pairs={{0,8},{1,9},{2,10},{3,11},{8,0},{9,1},{10,2},{11,3},{4,12},{5,13},... | collective-permute-start | bytes 6291464 | tf_op jit(solution)/shard_map/ppermute | solution.py:168
  121.0 4.7 %collective-permute-start.16 = (bf16[8,64,512]{2,1,0:T(8,128)(2,1)}, bf16[8,64,512]{2,1,0:T(8,128)(2,1)S(1)}, u32[]{:S(2)}, u32[]{:S(2)}) collective-permute-start(bf16[8,64,512]{2,1,0:T(8,128)(2,1)} %copy-done.2), channel_id=1, source_target_pairs={{0,8},{1,9},{2,10},{3,11},{8,0},{9,1},{10,2},{11,3},{4,12},{5,13},... | collective-permute-start | bytes 1572872 | tf_op jit(solution)/shard_map/ppermute | solution.py:168
  127.0 2.7 %copy-start.4 = (f32[512,1024]{1,0:T(8,128)S(1)}, f32[512,1024]{1,0:T(8,128)}, u32[]{:S(2)}) copy-start(f32[512,1024]{1,0:T(8,128)} %get-tuple-element.30) | copy-start | bytes 6291460
  (2 other events, 1.6 us)
